TPU v7x, 32 devices: a whole 2x2x4 slice. The times are simulated.
32 devices in a mesh: dp: 8 (over z, x), fsdp: 4 (over y, core).
Axes of the slice: x: 2, y: 2, z: 4, core: 2. Of those that a mesh axis runs over, the one named last changes fastest.
Arguments:
- block_in: bfloat16 [32, 768, 1152], P(('dp', 'fsdp')), may hold values from -6 to 6
- condition: bfloat16 [32, 3, 1152], P(('dp', 'fsdp')), may hold values from -6 to 6
- lengths: int32 [32, 3], P(('dp', 'fsdp')), may hold values from 1 to 512, 768 in all within a row
- head_mask: int32 [32, 3, 16], P(('dp', 'fsdp')), may hold values 0 or 1
- group_mask: int32 [32, 3, 16], P(('dp', 'fsdp')), may hold values 0 or 1
- buffer_slot: int32 [32, 768], P(('dp', 'fsdp')), may hold values from -1 to 511, as said below
- ada_weight: bfloat16 [1152, 6912], P('dp', 'fsdp'), may hold values from -0.1875 to 0.1875
- ada_bias: bfloat16 [6912], P('fsdp'), may hold values from -1.796875 to 1.796875
- qkv_weight: bfloat16 [1152, 3456], P('dp', 'fsdp'), may hold values from -0.1875 to 0.1875
- query_bias: bfloat16 [1152], P('fsdp'), may hold values from -1.796875 to 1.796875
- value_bias: bfloat16 [1152], P('fsdp'), may hold values from -1.796875 to 1.796875
- out_weight: bfloat16 [1152, 1152], P('dp', 'fsdp'), may hold values from -0.5 to 0.5
- out_bias: bfloat16 [1152], P('fsdp'), may hold values from -1.796875 to 1.796875
- up_weight: bfloat16 [1152, 4608], P('dp', 'fsdp'), may hold values from -0.1875 to 0.1875
- up_bias: bfloat16 [4608], P('fsdp'), may hold values from -3 to 3
- down_weight: bfloat16 [4608, 1152], P('dp', 'fsdp'), may hold values from -0.125 to 0.125
- down_bias: bfloat16 [1152], P('fsdp'), may hold values from -1.796875 to 1.796875
- cotangent: bfloat16 [32, 768, 1152], P(('dp', 'fsdp')), may hold values from -6 to 6
Outputs:
- block_out: bfloat16 [32, 768, 1152], P(('dp', 'fsdp'))
- grad_block_in: float32 [32, 768, 1152], P(('dp', 'fsdp'))
- grad_ada_weight: float32 [1152, 6912], P('dp', 'fsdp')
- grad_ada_bias: float32 [6912], P('fsdp')
- grad_qkv_weight: float32 [1152, 3456], P('dp', 'fsdp')
- grad_query_bias: float32 [1152], P('fsdp')
- grad_value_bias: float32 [1152], P('fsdp')
- grad_out_weight: float32 [1152, 1152], P('dp', 'fsdp')
- grad_out_bias: float32 [1152], P('fsdp')
- grad_up_weight: float32 [1152, 4608], P('dp', 'fsdp')
- grad_up_bias: float32 [4608], P('fsdp')
- grad_down_weight: float32 [4608, 1152], P('dp', 'fsdp')
- grad_down_bias: float32 [1152], P('fsdp')
Inputs may be any that keep to these rules, and one draw needn't show every extreme that they name: The 3 crop lengths of a row add up to 768. `buffer_slot`: -1 where the router skips the token; else the token's place in its row's feed-forward buffer of 512 places: place // 64 is the dp index whose device runs its feed-forward, place % 64 its position among the at most 64 tokens that the row sends there. Places of a row are distinct. In every draw one dp index, and the last one, receive 64 tokens from every row.
All inputs are finite; a program needn't handle non-finite values. No bound on the sum of `head_mask` or of `group_mask` on one device may be relied on, other than what follows from the above.
Results may differ from a plain program's by a relative error of at most 0.014.
The roundings to bfloat16 on the way count: a program that leaves them out, or rounds other values in their place, can miss the bound.
Values may be sent and summed in bfloat16 or wider, within the bound.
A program may use at most 320 MiB of HBM per device.

v0:
```python
import jax
import jax.numpy as jnp
from jax import lax
from jax.sharding import PartitionSpec as P

D = 1152
HEADS = 16
HEAD_DIM = 72
FF = 4608
GROUPS = 16
TOK_DEV = 768


highest = lax.Precision.HIGHEST
epsilon = 1e-06


def layer_norm(values):
    center = values - jnp.mean(values, axis=-1, keepdims=True)
    variance = jnp.mean(center * center, axis=-1, keepdims=True)
    inverse = lax.rsqrt(variance + epsilon)
    return (center * inverse, inverse)


def norm_back(grad_normed, normed, inverse):
    first_mean = jnp.mean(grad_normed, axis=-1, keepdims=True)
    second_mean = jnp.mean(grad_normed * normed, axis=-1, keepdims=True)
    return inverse * (grad_normed - first_mean - normed * second_mean)


def attention_scores(query_part, key_part, allowed, factor):
    raw_scores = (
        jnp.einsum("qhd,khd->hqk", query_part, key_part, preferred_element_type=jnp.float32)
        * factor
    )
    return jnp.where(allowed[None], raw_scores, -1e30)


def gelu_tanh(values):
    return jax.nn.gelu(values, approximate=True)


def shards(
    block_in,
    condition,
    lengths,
    head_mask,
    group_mask,
    buffer_slot,
    ada_weight,
    ada_bias,
    qkv_weight,
    query_bias,
    value_bias,
    out_weight,
    out_bias,
    up_weight,
    up_bias,
    down_weight,
    down_bias,
    cotangent,
):
    gathered = (
        lax.all_gather(ada_weight, "fsdp", axis=1, tiled=True),
        lax.all_gather(qkv_weight, "fsdp", axis=1, tiled=True),
        lax.all_gather(out_weight, "fsdp", axis=1, tiled=True),
        lax.all_gather(up_weight, "fsdp", axis=1, tiled=True),
        lax.all_gather(down_weight, "fsdp", axis=1, tiled=True),
        lax.all_gather(ada_bias, "fsdp", axis=0, tiled=True),
        lax.all_gather(query_bias, "fsdp", axis=0, tiled=True),
        lax.all_gather(value_bias, "fsdp", axis=0, tiled=True),
        lax.all_gather(out_bias, "fsdp", axis=0, tiled=True),
        lax.all_gather(up_bias, "fsdp", axis=0, tiled=True),
        lax.all_gather(down_bias, "fsdp", axis=0, tiled=True),
    )
    full_ada, full_qkv, full_out, full_up, full_down = (
        lax.all_gather(gathered[0], "dp", axis=0, tiled=True),
        lax.all_gather(gathered[1], "dp", axis=0, tiled=True),
        lax.all_gather(gathered[2], "dp", axis=0, tiled=True),
        lax.all_gather(gathered[3], "dp", axis=0, tiled=True),
        lax.all_gather(gathered[4], "dp", axis=0, tiled=True),
    )
    bias_ada, bias_query, bias_value, bias_out, bias_up, bias_down = [
        vector.astype(jnp.float32) for vector in gathered[5:]
    ]
    inputs = block_in[0].astype(jnp.float32)
    crop_length = lengths[0]
    finish = jnp.cumsum(crop_length)
    opening = finish - crop_length
    position = jnp.arange(TOK_DEV, dtype=jnp.int32)
    member = (
        (position[:, None] >= opening[None, :]) & (position[:, None] < finish[None, :])
    ).astype(jnp.float32)
    segment = jnp.sum((position[:, None] >= finish[None, :]).astype(jnp.int32), axis=1)
    cond_act = jax.nn.silu(condition[0].astype(jnp.float32)).astype(jnp.bfloat16)
    modulation = jnp.dot(cond_act, full_ada, preferred_element_type=jnp.float32) + bias_ada
    pieces = [
        jnp.dot(member, modulation[:, number * D : (number + 1) * D], precision=highest)
        for number in range(6)
    ]
    shift_one, scale_one, gate_one, shift_two, scale_two, gate_two = pieces
    head_keep = jnp.dot(member, head_mask[0].astype(jnp.float32), precision=highest)
    group_keep = jnp.dot(member, group_mask[0].astype(jnp.float32), precision=highest)
    normed_one, inverse_one = layer_norm(inputs)
    first_in = (normed_one * (1.0 + scale_one) + shift_one).astype(jnp.bfloat16)
    qkv_bias = jnp.concatenate([bias_query, jnp.zeros_like(bias_query), bias_value])
    triple = (jnp.dot(first_in, full_qkv, preferred_element_type=jnp.float32) + qkv_bias).astype(
        jnp.bfloat16
    )
    queries = triple[:, :D].reshape(TOK_DEV, HEADS, HEAD_DIM)
    keys_all = triple[:, D : 2 * D].reshape(TOK_DEV, HEADS, HEAD_DIM)
    values_all = triple[:, 2 * D :].reshape(TOK_DEV, HEADS, HEAD_DIM)
    factor = HEAD_DIM ** (-0.5)
    row_block = min(768, TOK_DEV)
    group_size = min(4, HEADS)
    log_totals = {}
    head_parts = []
    for head_start in range(0, HEADS, group_size):
        heads_here = slice(head_start, head_start + group_size)
        row_start = 0
        rows_here = slice(row_start, row_start + row_block)
        allowed = segment[:, None] == segment[None, :]
        scores = attention_scores(
            queries[rows_here, heads_here], keys_all[:, heads_here], allowed, factor
        )
        row_max = jnp.max(scores, axis=-1, keepdims=True)
        log_total = row_max + jnp.log(jnp.sum(jnp.exp(scores - row_max), axis=-1, keepdims=True))
        weights_low = jnp.exp(scores - log_total).astype(jnp.bfloat16)
        row_parts = jnp.einsum(
            "hqk,khd->qhd",
            weights_low,
            values_all[:, heads_here],
            preferred_element_type=jnp.float32,
        )
        log_totals[head_start, row_start] = log_total
        head_parts.append(row_parts)
    attended = jnp.concatenate(head_parts, axis=1)
    mixed = (attended * head_keep[:, :, None]).astype(jnp.bfloat16).reshape(TOK_DEV, D)
    attn_out = jnp.dot(mixed, full_out, preferred_element_type=jnp.float32) + bias_out
    after_attn = inputs + gate_one * attn_out
    normed_two, inverse_two = layer_norm(after_attn)
    second_in = (normed_two * (1.0 + scale_two) + shift_two).astype(jnp.bfloat16)
    keep = (buffer_slot[0] >= 0).astype(jnp.float32)[:, None]
    peers = lax.axis_size("dp")
    capacity = 2 * TOK_DEV // (3 * peers)
    places = peers * capacity
    chooser = (buffer_slot[0][:, None] == jnp.arange(places, dtype=jnp.int32)[None, :]).astype(
        jnp.bfloat16
    )
    outgoing = (
        jnp.einsum("tb,td->bd", chooser, second_in, preferred_element_type=jnp.float32)
        .astype(jnp.bfloat16)
        .reshape(peers, capacity, D)
    )
    outgoing_groups = (
        jnp.einsum(
            "tb,tg->bg",
            chooser,
            group_keep.astype(jnp.bfloat16),
            preferred_element_type=jnp.float32,
        )
        .astype(jnp.bfloat16)
        .reshape(peers, capacity, GROUPS)
    )
    arrived, arrived_groups = (
        lax.all_to_all(outgoing, "dp", split_axis=0, concat_axis=0, tiled=True),
        lax.all_to_all(outgoing_groups, "dp", split_axis=0, concat_axis=0, tiled=True),
    )
    arrived = arrived.reshape(places, D)
    groups_float = arrived_groups.reshape(places, GROUPS).astype(jnp.float32)
    channel_keep = jnp.repeat(groups_float, FF // GROUPS, axis=1)
    hidden = jnp.dot(arrived, full_up, preferred_element_type=jnp.float32) + bias_up
    active = (gelu_tanh(hidden) * channel_keep).astype(jnp.bfloat16)
    branch = (jnp.dot(active, full_down, preferred_element_type=jnp.float32) + bias_down).astype(
        jnp.bfloat16
    )
    returned = lax.all_to_all(
        branch.reshape(peers, capacity, D), "dp", split_axis=0, concat_axis=0, tiled=True
    )
    branch_tok = jnp.einsum(
        "tb,bd->td", chooser, returned.reshape(places, D), preferred_element_type=jnp.float32
    )
    after_mlp = after_attn + gate_two * branch_tok
    block_out = after_mlp.astype(jnp.bfloat16)[None]
    grad_after = cotangent[0].astype(jnp.float32)
    grad_gate_two = grad_after * branch_tok
    grad_branch = (gate_two * keep * grad_after).astype(jnp.bfloat16)
    grad_rows = (
        jnp.einsum("tb,td->bd", chooser, grad_branch, preferred_element_type=jnp.float32)
        .astype(jnp.bfloat16)
        .reshape(peers, capacity, D)
    )
    grad_rows = lax.all_to_all(grad_rows, "dp", split_axis=0, concat_axis=0, tiled=True).reshape(
        places, D
    )
    again = (
        lax.all_gather(qkv_weight, "fsdp", axis=1, tiled=True),
        lax.all_gather(out_weight, "fsdp", axis=1, tiled=True),
        lax.all_gather(up_weight, "fsdp", axis=1, tiled=True),
        lax.all_gather(down_weight, "fsdp", axis=1, tiled=True),
    )
    back_qkv, back_out, back_up, back_down = (
        lax.all_gather(again[0], "dp", axis=0, tiled=True),
        lax.all_gather(again[1], "dp", axis=0, tiled=True),
        lax.all_gather(again[2], "dp", axis=0, tiled=True),
        lax.all_gather(again[3], "dp", axis=0, tiled=True),
    )
    grad_down_bias = jnp.sum(grad_rows.astype(jnp.float32), axis=0)
    grad_down = jnp.einsum("bf,bd->fd", active, grad_rows, preferred_element_type=jnp.float32)
    grad_active = jnp.einsum("bd,fd->bf", grad_rows, back_down, preferred_element_type=jnp.float32)
    gelu_pull = jax.vjp(gelu_tanh, hidden)[1]
    grad_hidden = gelu_pull(grad_active * channel_keep)[0].astype(jnp.bfloat16)
    grad_up_bias = jnp.sum(grad_hidden.astype(jnp.float32), axis=0)
    grad_up = jnp.einsum("bd,bf->df", arrived, grad_hidden, preferred_element_type=jnp.float32)
    grad_arrived = jnp.einsum(
        "bf,df->bd", grad_hidden, back_up, preferred_element_type=jnp.float32
    ).astype(jnp.bfloat16)
    grad_arrived = lax.all_to_all(
        grad_arrived.reshape(peers, capacity, D), "dp", split_axis=0, concat_axis=0, tiled=True
    )
    grad_second = jnp.einsum(
        "tb,bd->td", chooser, grad_arrived.reshape(places, D), preferred_element_type=jnp.float32
    )
    grad_scale_two = grad_second * normed_two
    grad_mid = grad_after + norm_back(grad_second * (1.0 + scale_two), normed_two, inverse_two)
    grad_gate_one = grad_mid * attn_out
    grad_attn = (gate_one * grad_mid).astype(jnp.bfloat16)
    grad_out_bias = jnp.sum(grad_attn.astype(jnp.float32), axis=0)
    grad_out = jnp.einsum("te,tf->ef", mixed, grad_attn, preferred_element_type=jnp.float32)
    grad_mixed = jnp.einsum(
        "tf,ef->te", grad_attn, back_out, preferred_element_type=jnp.float32
    ).astype(jnp.bfloat16)
    grad_attended = (
        grad_mixed.reshape(TOK_DEV, HEADS, HEAD_DIM).astype(jnp.float32) * head_keep[:, :, None]
    ).astype(jnp.bfloat16)
    query_heads = []
    key_heads = []
    value_heads = []
    for head_start in range(0, HEADS, group_size):
        heads_here = slice(head_start, head_start + group_size)
        row_start = 0
        rows_here = slice(row_start, row_start + row_block)
        allowed = segment[:, None] == segment[None, :]
        scores = attention_scores(
            queries[rows_here, heads_here], keys_all[:, heads_here], allowed, factor
        )
        probs = jnp.exp(scores - log_totals[head_start, row_start])
        grad_piece = grad_attended[rows_here, heads_here]
        grad_values = jnp.einsum(
            "hqk,qhd->khd",
            probs.astype(jnp.bfloat16),
            grad_piece,
            preferred_element_type=jnp.float32,
        )
        grad_probs = jnp.einsum(
            "qhd,khd->hqk",
            grad_piece,
            values_all[:, heads_here],
            preferred_element_type=jnp.float32,
        )
        grad_scores = (
            probs * (grad_probs - jnp.sum(probs * grad_probs, axis=-1, keepdims=True))
        ).astype(jnp.bfloat16)
        query_rows = (
            jnp.einsum(
                "hqk,khd->qhd",
                grad_scores,
                keys_all[:, heads_here],
                preferred_element_type=jnp.float32,
            )
            * factor
        )
        grad_keys = (
            jnp.einsum(
                "hqk,qhd->khd",
                grad_scores,
                queries[rows_here, heads_here],
                preferred_element_type=jnp.float32,
            )
            * factor
        )
        query_heads.append(query_rows)
        key_heads.append(grad_keys)
        value_heads.append(grad_values)
    grad_triple = jnp.concatenate(
        [
            jnp.concatenate(query_heads, axis=1).reshape(TOK_DEV, D),
            jnp.concatenate(key_heads, axis=1).reshape(TOK_DEV, D),
            jnp.concatenate(value_heads, axis=1).reshape(TOK_DEV, D),
        ],
        axis=1,
    ).astype(jnp.bfloat16)
    grad_query_bias = jnp.sum(grad_triple[:, :D].astype(jnp.float32), axis=0)
    grad_value_bias = jnp.sum(grad_triple[:, 2 * D :].astype(jnp.float32), axis=0)
    grad_qkv = jnp.einsum("td,te->de", first_in, grad_triple, preferred_element_type=jnp.float32)
    grad_first = jnp.einsum("te,de->td", grad_triple, back_qkv, preferred_element_type=jnp.float32)
    grad_scale_one = grad_first * normed_one
    grad_inputs = grad_mid + norm_back(grad_first * (1.0 + scale_one), normed_one, inverse_one)
    token_grads = [
        grad_first,
        grad_scale_one,
        grad_gate_one,
        grad_second,
        grad_scale_two,
        grad_gate_two,
    ]
    grad_modulation = jnp.concatenate(
        [jnp.einsum("ts,td->sd", member, single, precision=highest) for single in token_grads],
        axis=1,
    )
    grad_ada_bias = jnp.sum(grad_modulation, axis=0)
    grad_ada = jnp.einsum(
        "sd,se->de", cond_act.astype(jnp.float32), grad_modulation, precision=highest
    )
    reduced = (
        lax.psum_scatter(grad_ada, "dp", scatter_dimension=0, tiled=True),
        lax.psum_scatter(grad_qkv, "dp", scatter_dimension=0, tiled=True),
        lax.psum_scatter(grad_out, "dp", scatter_dimension=0, tiled=True),
        lax.psum_scatter(grad_up, "dp", scatter_dimension=0, tiled=True),
        lax.psum_scatter(grad_down, "dp", scatter_dimension=0, tiled=True),
    )
    shares = (
        lax.psum_scatter(reduced[0], "fsdp", scatter_dimension=1, tiled=True),
        lax.psum_scatter(reduced[1], "fsdp", scatter_dimension=1, tiled=True),
        lax.psum_scatter(reduced[2], "fsdp", scatter_dimension=1, tiled=True),
        lax.psum_scatter(reduced[3], "fsdp", scatter_dimension=1, tiled=True),
        lax.psum_scatter(reduced[4], "fsdp", scatter_dimension=1, tiled=True),
        lax.psum_scatter(grad_ada_bias, "fsdp", scatter_dimension=0, tiled=True),
        lax.psum_scatter(grad_query_bias, "fsdp", scatter_dimension=0, tiled=True),
        lax.psum_scatter(grad_value_bias, "fsdp", scatter_dimension=0, tiled=True),
        lax.psum_scatter(grad_out_bias, "fsdp", scatter_dimension=0, tiled=True),
        lax.psum_scatter(grad_up_bias, "fsdp", scatter_dimension=0, tiled=True),
        lax.psum_scatter(grad_down_bias, "fsdp", scatter_dimension=0, tiled=True),
    )
    matrix_shares = shares[:5]
    bias_shares = shares[5:]
    bias_totals = lax.psum(
        (
            bias_shares[0],
            bias_shares[1],
            bias_shares[2],
            bias_shares[3],
            bias_shares[4],
            bias_shares[5],
        ),
        "dp",
    )
    return (
        block_out,
        grad_inputs[None],
        matrix_shares[0],
        bias_totals[0],
        matrix_shares[1],
        bias_totals[1],
        bias_totals[2],
        matrix_shares[2],
        bias_totals[3],
        matrix_shares[3],
        bias_totals[4],
        matrix_shares[4],
        bias_totals[5],
    )


def solution(mesh):
    placed = (
        P(("dp", "fsdp"), None, None),
        P(("dp", "fsdp"), None, None),
        P(("dp", "fsdp"), None),
        P(("dp", "fsdp"), None, None),
        P(("dp", "fsdp"), None, None),
        P(("dp", "fsdp"), None),
        P("dp", "fsdp"),
        P("fsdp"),
        P("dp", "fsdp"),
        P("fsdp"),
        P("fsdp"),
        P("dp", "fsdp"),
        P("fsdp"),
        P("dp", "fsdp"),
        P("fsdp"),
        P("dp", "fsdp"),
        P("fsdp"),
        P(("dp", "fsdp"), None, None),
    )
    return jax.shard_map(
        shards,
        mesh=mesh,
        in_specs=placed,
        out_specs=(
            P(("dp", "fsdp"), None, None),
            P(("dp", "fsdp"), None, None),
            P("dp", "fsdp"),
            P("fsdp"),
            P("dp", "fsdp"),
            P("fsdp"),
            P("fsdp"),
            P("dp", "fsdp"),
            P("fsdp"),
            P("dp", "fsdp"),
            P("fsdp"),
            P("dp", "fsdp"),
            P("fsdp"),
        ),
        check_vma=False,
    )
```

profile of v0, /device:TPU:9, one launch (start us, length us, event | category | flops | bytes accessed | tf_op | source)
XLA Modules:
  0.0 2774.8 jit_solution(10845043566539648752)
XLA Ops:
  9.4 24.1 all-gather.27.cloned.1.call-done
  39.1 13.9 all-gather.1
  75.0 11.6 all-reduce.13
  91.4 203.3 %all-gather.13.cloned.1.call-done = bf16[1152,6912]{1,0:T(8,128)(2,1)} async-done(((bf16[144,6912]{1,0:T(8,128)(2,1)}), bf16[1152,6912]{1,0:T(8,128)(2,1)}) %all-gather.13.cloned.1.call-update) | async-done | bytes 15925264 | tf_op jit(solution)/shard_map/all_gather | solution.py:77
  309.9 105.2 %all-gather.15.cloned.1.call-done = bf16[1152,3456]{1,0:T(8,128)(2,1)} async-done(((bf16[144,3456]{1,0:T(8,128)(2,1)}), bf16[1152,3456]{1,0:T(8,128)(2,1)}) %all-gather.15.cloned.1.call-update) | async-done | bytes 7962640 | tf_op jit(solution)/shard_map/all_gather | solution.py:78
  415.1 11.0 add_convert_fusion
  451.5 14.0 exponential_reduce_fusion.3
  465.6 10.5 exponential_reduce_fusion.2
  565.6 97.7 %all-gather.21.cloned.1.call-done = bf16[1152,4608]{1,0:T(8,128)(2,1)} async-done(((bf16[144,4608]{1,0:T(8,128)(2,1)}), bf16[1152,4608]{1,0:T(8,128)(2,1)}) %all-gather.21.cloned.1.call-update) | async-done | bytes 10616848 | tf_op jit(solution)/shard_map/all_gather | solution.py:80
  663.3 15.6 multiply_convert_fusion.4
  678.9 139.0 %all-gather.25.cloned.1.call-done = bf16[4608,1152]{1,0:T(8,128)(2,1)} async-done(((bf16[576,1152]{1,0:T(8,128)(2,1)}), bf16[4608,1152]{1,0:T(8,128)(2,1)}) %all-gather.25.cloned.1.call-update) | async-done | bytes 10616848 | tf_op jit(solution)/shard_map/all_gather | solution.py:81
  817.9 12.0 fusion.41
  836.6 19.4 convert_reduce_fusion
  856.0 12.0 convolution_convert_fusion.1
  878.1 20.7 all-to-all-done.4
  956.6 29.0 %multiply_reduce_fusion.3 = (f32[4,768]{1,0:T(4,128)S(1)}, f32[4,768]{1,0:T(4,128)S(1)}, f32[4,768]{1,0:T(4,128)S(1)}, f32[4,768]{1,0:T(4,128)S(1)}, f32[4,768,768]{1,2,0:T(8,128)}) fusion(f32[4,768,768]{1,2,0:T(8,128)} %get-tuple-element.141, f32[4,768]{1,0:T(4,128)S(1)} %copy-done.44, pred[768,768]{0,1:T(8,128)(4,1)S(1)} %copy-done.14, ...), kind=kOutput, calls=%fused_computation.18 | convolution fusion | flops 386912256 | bytes 78397440 | tf_op jit(solution)/shard_map/qhd,khd->hqk/dot_general | solution.py:255
  987.0 35.4 %multiply_convert_fusion.3 = (bf16[4,768,768]{1,2,0:T(8,128)(2,1)}, bf16[4,768,768]{1,2,0:T(8,128)(2,1)}, bf16[4,768,768]{1,2,0:T(8,128)(2,1)}, bf16[4,768,768]{1,2,0:T(8,128)(2,1)}) fusion(f32[4,768,768]{1,2,0:T(8,128)} %get-tuple-element.147, f32[4,768,768]{1,2,0:T(8,128)} %get-tuple-element.141, f32[4,768]{1,0:T(4,128)S(1)} %get-tuple-element.95, ...), kind=kLoop, calls=%fused_computation.17 | loop fusion | flops 56623104 | bytes 95059968 | tf_op jit(solution)/shard_map/convert_element_type | solution.py:263
  1041.7 13.1 fusion.52
  1056.9 15.0 fusion.153
  1087.5 17.2 fusion.128
  1104.8 12.7 fusion.161
  1117.6 12.2 fusion.160
  1132.4 202.0 %reduce-scatter.21.cloned.1.call-done = f32[144,3456]{1,0:T(8,128)} async-done(((f32[1152,3456]{1,0:T(8,128)}), f32[144,3456]{1,0:T(8,128)}) %reduce-scatter.21.cloned.1.call-update) | async-done | bytes 1990672 | tf_op jit(solution)/shard_map/reduce_scatter | solution.py:317
  1338.0 512.4 %reduce-scatter.19.cloned.1.call-done = f32[144,6912]{1,0:T(8,128)} async-done(((f32[1152,6912]{1,0:T(8,128)}), f32[144,6912]{1,0:T(8,128)}) %reduce-scatter.19.cloned.1.call-update) | async-done | bytes 3981328 | tf_op jit(solution)/shard_map/reduce_scatter | solution.py:316
  1856.8 344.3 %reduce-scatter.29.cloned.1.call-done = f32[576,1152]{1,0:T(8,128)} async-done(((f32[4608,1152]{1,0:T(8,128)}), f32[576,1152]{1,0:T(8,128)}) %reduce-scatter.29.cloned.1.call-update) | async-done | bytes 2654224 | tf_op jit(solution)/shard_map/reduce_scatter | solution.py:320
  2205.0 346.5 %reduce-scatter.25.cloned.1.call-done = f32[144,4608]{1,0:T(8,128)} async-done(((f32[1152,4608]{1,0:T(8,128)}), f32[144,4608]{1,0:T(8,128)}) %reduce-scatter.25.cloned.1.call-update) | async-done | bytes 2654224 | tf_op jit(solution)/shard_map/reduce_scatter | solution.py:319
  2559.8 12.0 all-reduce.12
  2572.3 27.1 all-reduce.11
  2608.0 15.5 reduce-scatter.33.cloned.1.call-done
  2625.7 64.1 %reduce-scatter.31.cloned.1.call-done = f32[1728,144]{1,0:T(8,128)} async-done(((f32[6912,144]{1,0:T(8,128)}), f32[1728,144]{1,0:T(8,128)}) %reduce-scatter.31.cloned.1.call-update) | async-done | bytes 995344
  2692.8 36.8 %reduce-scatter.37.cloned.1.call-done = f32[288,576]{1,0:T(8,128)} async-done(((f32[1152,576]{1,0:T(8,128)}), f32[288,576]{1,0:T(8,128)}) %reduce-scatter.37.cloned.1.call-update) | async-done | bytes 663568
  2729.6 38.1 %reduce-scatter.27.cloned.1.call-done = f32[144,1152]{1,0:T(8,128)} async-done(((f32[144,4608]{1,0:T(8,128)}), f32[144,1152]{1,0:T(8,128)}) %reduce-scatter.27.cloned.1.call-update) | async-done | bytes 663568 | tf_op jit(solution)/shard_map/reduce_scatter | solution.py:326
  (396 shorter events, 312.0 us)
Async XLA Ops:
  7.2 26.4 all-gather.27.cloned.1.call-start
  7.9 55.6 %all-gather.19.cloned.1.call-start = ((), (), s32[]{:S(2)}) async-start(), calls=%async_computation.18 | async-start | bytes 1658880 | tf_op jit(solution)/shard_map/all_gather | solution.py:67
  8.7 79.7 %all-gather.23.cloned.1.call-start = ((), (), s32[]{:S(2)}) async-start(), calls=%async_computation.20 | async-start | bytes 1843200 | tf_op jit(solution)/shard_map/all_gather | solution.py:68
  9.4 285.3 %all-gather.13.cloned.1.call-start = ((), (), s32[]{:S(2)}) async-start(), calls=%async_computation.15 | async-start | bytes 17915904 | tf_op jit(solution)/shard_map/all_gather | solution.py:77
  39.1 376.1 %all-gather.15.cloned.1.call-start = ((), (), s32[]{:S(2)}) async-start(), calls=%async_computation.16 | async-start | bytes 8957952 | tf_op jit(solution)/shard_map/all_gather | solution.py:78
  55.3 436.4 %all-gather.17.cloned.1.call-start = ((), (), s32[]{:S(2)}) async-start(), calls=%async_computation.17 | async-start | bytes 2985984 | tf_op jit(solution)/shard_map/all_gather | solution.py:79
  63.5 599.9 %all-gather.21.cloned.1.call-start = ((), (), s32[]{:S(2)}) async-start(), calls=%async_computation.19 | async-start | bytes 11943936 | tf_op jit(solution)/shard_map/all_gather | solution.py:80
  64.4 433.1 %copy-start.59 = (s32[3,1]{0,1:T(1,128)}, s32[3,1]{0,1:T(1,128)S(1)}, u32[]{:S(2)}) copy-start(s32[3,1]{0,1:T(1,128)S(1)} %reduce-window.4) | copy-start | bytes 40
  64.5 239.8 %copy-start.62 = (s32[3]{0:T(128)}, s32[3]{0:T(128)S(1)}, u32[]{:S(2)}) copy-start(s32[3]{0:T(128)S(1)} %fusion.125) | copy-start | bytes 40
  66.3 443.0 %all-to-all-start.1 = ((bf16[8,2,512]{2,1,0:T(2,128)(2,1)}), bf16[8,2,512]{2,1,0:T(2,128)(2,1)}, u32[]{:S(2)}, u32[]{:S(2)}) async-start(bf16[8,2,512]{2,1,0:T(2,128)(2,1)} %reshape.297), calls=%async_computation.1 | async-start | bytes 32768 | tf_op jit(solution)/shard_map/all_to_all | solution.py:167
  71.7 746.2 %all-gather.25.cloned.1.call-start = ((), (), s32[]{:S(2)}) async-start(), calls=%async_computation.21 | async-start | bytes 11943936 | tf_op jit(solution)/shard_map/all_gather | solution.py:81
  87.0 207.7 %copy-start.70 = (bf16[1,3,1152]{2,1,0:T(4,128)(2,1)S(1)}, bf16[1,3,1152]{2,1,0:T(4,128)(2,1)}, u32[]{:S(2)}) copy-start(bf16[1,3,1152]{2,1,0:T(4,128)(2,1)} %param.19) | copy-start | bytes 20740
  87.1 217.2 %copy-start.54 = (f32[768]{0:T(1024)}, f32[768]{0:T(1024)S(1)}, u32[]{:S(2)}) copy-start(f32[768]{0:T(1024)S(1)} %broadcast_multiply_fusion.5) | copy-start | bytes 9220
  87.7 216.6 %copy-start.65 = (f32[768]{0:T(1024)}, f32[768]{0:T(1024)S(1)}, u32[]{:S(2)}) copy-start(f32[768]{0:T(1024)S(1)} %add_rsqrt_fusion.1) | copy-start | bytes 9220
  87.9 403.3 %copy-start.50 = (f32[768,16]{0,1:T(8,128)}, f32[768,16]{0,1:T(8,128)S(1)}, u32[]{:S(2)}) copy-start(f32[768,16]{0,1:T(8,128)S(1)} %fusion.122) | copy-start | bytes 147460
  88.4 400.0 %copy-start.13 = (pred[768,768]{0,1:T(8,128)(4,1)}, pred[768,768]{0,1:T(8,128)(4,1)S(1)}, u32[]{:S(2)}) copy-start(pred[768,768]{0,1:T(8,128)(4,1)S(1)} %broadcast_compare_fusion) | copy-start | bytes 1769476
  501.7 402.2 %copy-start.1 = (f32[768,1152]{1,0:T(8,128)}, f32[768,1152]{1,0:T(8,128)S(1)}, u32[]{:S(2)}) copy-start(f32[768,1152]{1,0:T(8,128)S(1)} %get-tuple-element.129) | copy-start | bytes 10616836
  501.7 402.2 %copy-start.51 = (f32[768]{0:T(1024)}, f32[768]{0:T(1024)S(1)}, u32[]{:S(2)}) copy-start(f32[768]{0:T(1024)S(1)} %broadcast_multiply_fusion.4) | copy-start | bytes 9220
  509.2 48.0 %all-to-all-start = ((bf16[8,64,1152]{2,1,0:T(8,128)(2,1)}), bf16[8,64,1152]{2,1,0:T(8,128)(2,1)}, u32[]{:S(2)}, u32[]{:S(2)}) async-start(bf16[8,64,1152]{2,1,0:T(8,128)(2,1)} %bitcast.280), calls=%async_computation | async-start | bytes 2359296 | tf_op jit(solution)/shard_map/all_to_all | solution.py:166
  557.3 272.6 %all-to-all-start.3 = ((bf16[8,64,1152]{2,1,0:T(8,128)(2,1)}), bf16[8,64,1152]{2,1,0:T(8,128)(2,1)}, u32[]{:S(2)}, u32[]{:S(2)}) async-start(bf16[8,64,1152]{2,1,0:T(8,128)(2,1)} %bitcast.262), calls=%async_computation.3 | async-start | bytes 2359296 | tf_op jit(solution)/shard_map/all_to_all | solution.py:193
  829.9 38.1 %all-to-all-start.2 = ((bf16[8,64,1152]{2,1,0:T(8,128)(2,1)}), bf16[8,64,1152]{2,1,0:T(8,128)(2,1)}, u32[]{:S(2)}, u32[]{:S(2)}) async-start(bf16[8,64,1152]{2,1,0:T(8,128)(2,1)} %bitcast.281), calls=%async_computation.2 | async-start | bytes 2359296 | tf_op jit(solution)/shard_map/all_to_all | solution.py:177
  868.0 30.7 %all-to-all-start.4 = ((bf16[8,64,1152]{2,1,0:T(8,128)(2,1)}), bf16[8,64,1152]{2,1,0:T(8,128)(2,1)}, u32[]{:S(2)}, u32[]{:S(2)}) async-start(bf16[8,64,1152]{2,1,0:T(8,128)(2,1)} %bitcast.282), calls=%async_computation.4 | async-start | bytes 2359296 | tf_op jit(solution)/shard_map/all_to_all | solution.py:218
  873.5 256.3 %reduce-scatter.23.cloned.1.call-start = ((), (), s32[]{:S(2)}) async-start(), calls=%async_computation.24 | async-start | bytes 5971968 | tf_op jit(solution)/shard_map/reduce_scatter | solution.py:318
  956.6 377.9 %reduce-scatter.21.cloned.1.call-start = ((), (), s32[]{:S(2)}) async-start(), calls=%async_computation.23 | async-start | bytes 17915904 | tf_op jit(solution)/shard_map/reduce_scatter | solution.py:317
  1054.9 795.6 %reduce-scatter.19.cloned.1.call-start = ((), (), s32[]{:S(2)}) async-start(), calls=%async_computation.22 | async-start | bytes 35831808 | tf_op jit(solution)/shard_map/reduce_scatter | solution.py:316
  1104.8 1096.4 %reduce-scatter.29.cloned.1.call-start = ((), (), s32[]{:S(2)}) async-start(), calls=%async_computation.27 | async-start | bytes 23887872 | tf_op jit(solution)/shard_map/reduce_scatter | solution.py:320
  1117.5 1434.0 %reduce-scatter.25.cloned.1.call-start = ((), (), s32[]{:S(2)}) async-start(), calls=%async_computation.25 | async-start | bytes 23887872 | tf_op jit(solution)/shard_map/reduce_scatter | solution.py:319
  1129.8 1476.4 %reduce-scatter.35.cloned.1.call-start = ((), (), s32[]{:S(2)}) async-start(), calls=%async_computation.31 | async-start | bytes 1474560
  1132.4 1491.1 %reduce-scatter.33.cloned.1.call-start = ((), (), s32[]{:S(2)}) async-start(), calls=%async_computation.30 | async-start | bytes 4423680
  1338.0 1351.8 %reduce-scatter.31.cloned.1.call-start = ((), (), s32[]{:S(2)}) async-start(), calls=%async_computation.29 | async-start | bytes 8847360
  1856.8 872.8 %reduce-scatter.37.cloned.1.call-start = ((), (), s32[]{:S(2)}) async-start(), calls=%async_computation.32 | async-start | bytes 3686400
  2204.7 563.0 %reduce-scatter.27.cloned.1.call-start = ((), (), s32[]{:S(2)}) async-start(), calls=%async_computation.26 | async-start | bytes 3317760 | tf_op jit(solution)/shard_map/reduce_scatter | solution.py:326
  (94 other events, 701.3 us)
Sparse Core Ops, SparseCore 0:
  9.6 23.9 all-gather.26
  35.1 21.5 all-gather.18
  58.3 19.1 all-gather.22
  80.1 214.5 all-gather.12
  297.3 117.7 all-gather.14
  417.7 54.3 all-gather.16
  474.2 189.0 all-gather.20
  665.5 152.3 all-gather.24
  956.7 106.4 reduce-scatter.22
  1067.5 266.9 reduce-scatter.20
  1338.8 511.5 reduce-scatter.18
  1854.7 346.4 reduce-scatter.28
  2205.0 346.4 reduce-scatter.24
  2554.1 26.4 reduce-scatter.34
  2583.0 40.4 reduce-scatter.32
  2626.0 63.7 reduce-scatter.30
  2692.8 36.7 reduce-scatter.36
  2732.7 34.8 reduce-scatter.26
where the time goes:
time: 2780 us; the launch traced here: 2770 us
  waiting for transfers between devices  2160 us (78%)
  matrix products  322 us (12%)
  local copies, waits for them, and re-layouts  93.2 us (3%)
  blocking collectives  77.7 us (3%)
  other arithmetic  73.2 us (3%)
  starting transfers between devices  32.6 us (1%)
    reduce_scatter x1, waiting for transfers between devices, shards(): lax.psum_scatter(grad_ada, 'dp', scatter_dimension=0, tiled=True)  512 us
    reduce_scatter x1, waiting for transfers between devices, shards(): lax.psum_scatter(grad_up, 'dp', scatter_dimension=0, tiled=True)  347 us
    reduce_scatter x1, waiting for transfers between devices, shards(): lax.psum_scatter(grad_down, 'dp', scatter_dimension=0, tiled=True)  344 us
    all_gather x1, waiting for transfers between devices, shards(): lax.all_gather(gathered[0], 'dp', axis=0, tiled=True)  203 us
    reduce_scatter x1, waiting for transfers between devices, shards(): lax.psum_scatter(grad_qkv, 'dp', scatter_dimension=0, tiled=True)  202 us
    all_gather x1, waiting for transfers between devices, shards(): lax.all_gather(gathered[4], 'dp', axis=0, tiled=True)  139 us
    unnamed x22, waiting for transfers between devices  119 us
    all_gather x1, waiting for transfers between devices, shards(): lax.all_gather(gathered[1], 'dp', axis=0, tiled=True)  105 us
  transfers between devices with their start and end apart: 23, of which 15 were waited for; matrix products, arithmetic and copies ran while one was open for 15% of the time, Pallas kernels for 0%

commit v1 on v0

--- a/solution.py
+++ b/solution.py
@@ -60,28 +60,26 @@
     down_bias,
     cotangent,
 ):
-    gathered = (
-        lax.all_gather(ada_weight, "fsdp", axis=1, tiled=True),
-        lax.all_gather(qkv_weight, "fsdp", axis=1, tiled=True),
-        lax.all_gather(out_weight, "fsdp", axis=1, tiled=True),
-        lax.all_gather(up_weight, "fsdp", axis=1, tiled=True),
-        lax.all_gather(down_weight, "fsdp", axis=1, tiled=True),
-        lax.all_gather(ada_bias, "fsdp", axis=0, tiled=True),
-        lax.all_gather(query_bias, "fsdp", axis=0, tiled=True),
-        lax.all_gather(value_bias, "fsdp", axis=0, tiled=True),
-        lax.all_gather(out_bias, "fsdp", axis=0, tiled=True),
-        lax.all_gather(up_bias, "fsdp", axis=0, tiled=True),
-        lax.all_gather(down_bias, "fsdp", axis=0, tiled=True),
-    )
-    full_ada, full_qkv, full_out, full_up, full_down = (
-        lax.all_gather(gathered[0], "dp", axis=0, tiled=True),
-        lax.all_gather(gathered[1], "dp", axis=0, tiled=True),
-        lax.all_gather(gathered[2], "dp", axis=0, tiled=True),
-        lax.all_gather(gathered[3], "dp", axis=0, tiled=True),
-        lax.all_gather(gathered[4], "dp", axis=0, tiled=True),
-    )
-    bias_ada, bias_query, bias_value, bias_out, bias_up, bias_down = [
-        vector.astype(jnp.float32) for vector in gathered[5:]
+    peers = lax.axis_size("dp")
+    mates = lax.axis_size("fsdp")
+
+    def gather_matrix(shard):
+        stacked = lax.all_gather(shard, ("dp", "fsdp"), axis=0, tiled=False)
+        rows, columns = shard.shape
+        stacked = stacked.reshape(peers, mates, rows, columns).transpose(0, 2, 1, 3)
+        return stacked.reshape(peers * rows, mates * columns)
+
+    full_qkv, full_out, full_up, full_down = [
+        gather_matrix(shard) for shard in (qkv_weight, out_weight, up_weight, down_weight)
+    ]
+    vectors = (query_bias, value_bias, out_bias, up_bias, down_bias)
+    packed_bias = lax.all_gather(jnp.concatenate(vectors), "fsdp", axis=0, tiled=False)
+    edges = [0]
+    for vector in vectors:
+        edges.append(edges[-1] + vector.shape[0])
+    bias_query, bias_value, bias_out, bias_up, bias_down = [
+        packed_bias[:, low:high].reshape(-1).astype(jnp.float32)
+        for low, high in zip(edges[:-1], edges[1:])
     ]
     inputs = block_in[0].astype(jnp.float32)
     crop_length = lengths[0]
@@ -93,7 +91,14 @@
     ).astype(jnp.float32)
     segment = jnp.sum((position[:, None] >= finish[None, :]).astype(jnp.int32), axis=1)
     cond_act = jax.nn.silu(condition[0].astype(jnp.float32)).astype(jnp.bfloat16)
-    modulation = jnp.dot(cond_act, full_ada, preferred_element_type=jnp.float32) + bias_ada
+    crops = cond_act.shape[0]
+    cond_all = lax.all_gather(cond_act, ("dp", "fsdp"), axis=0, tiled=True)
+    depth = ada_weight.shape[0]
+    cond_slice = lax.dynamic_slice_in_dim(cond_all, lax.axis_index("dp") * depth, depth, axis=1)
+    partial_mod = jnp.dot(cond_slice, ada_weight, preferred_element_type=jnp.float32)
+    column_mod = lax.psum_scatter(partial_mod, "dp", scatter_dimension=0, tiled=True)
+    column_mod = column_mod + ada_bias.astype(jnp.float32)
+    modulation = lax.all_to_all(column_mod, "fsdp", split_axis=0, concat_axis=1, tiled=True)
     pieces = [
         jnp.dot(member, modulation[:, number * D : (number + 1) * D], precision=highest)
         for number in range(6)
@@ -141,70 +146,37 @@
     normed_two, inverse_two = layer_norm(after_attn)
     second_in = (normed_two * (1.0 + scale_two) + shift_two).astype(jnp.bfloat16)
     keep = (buffer_slot[0] >= 0).astype(jnp.float32)[:, None]
-    peers = lax.axis_size("dp")
-    capacity = 2 * TOK_DEV // (3 * peers)
-    places = peers * capacity
+    places = 2 * TOK_DEV // 3
     chooser = (buffer_slot[0][:, None] == jnp.arange(places, dtype=jnp.int32)[None, :]).astype(
         jnp.bfloat16
     )
-    outgoing = (
-        jnp.einsum("tb,td->bd", chooser, second_in, preferred_element_type=jnp.float32)
-        .astype(jnp.bfloat16)
-        .reshape(peers, capacity, D)
-    )
-    outgoing_groups = (
-        jnp.einsum(
-            "tb,tg->bg",
-            chooser,
-            group_keep.astype(jnp.bfloat16),
-            preferred_element_type=jnp.float32,
-        )
-        .astype(jnp.bfloat16)
-        .reshape(peers, capacity, GROUPS)
-    )
-    arrived, arrived_groups = (
-        lax.all_to_all(outgoing, "dp", split_axis=0, concat_axis=0, tiled=True),
-        lax.all_to_all(outgoing_groups, "dp", split_axis=0, concat_axis=0, tiled=True),
-    )
-    arrived = arrived.reshape(places, D)
-    groups_float = arrived_groups.reshape(places, GROUPS).astype(jnp.float32)
+    arrived = jnp.einsum(
+        "tb,td->bd", chooser, second_in, preferred_element_type=jnp.float32
+    ).astype(jnp.bfloat16)
+    groups_float = jnp.einsum(
+        "tb,tg->bg",
+        chooser,
+        group_keep.astype(jnp.bfloat16),
+        preferred_element_type=jnp.float32,
+    )
     channel_keep = jnp.repeat(groups_float, FF // GROUPS, axis=1)
     hidden = jnp.dot(arrived, full_up, preferred_element_type=jnp.float32) + bias_up
     active = (gelu_tanh(hidden) * channel_keep).astype(jnp.bfloat16)
     branch = (jnp.dot(active, full_down, preferred_element_type=jnp.float32) + bias_down).astype(
         jnp.bfloat16
     )
-    returned = lax.all_to_all(
-        branch.reshape(peers, capacity, D), "dp", split_axis=0, concat_axis=0, tiled=True
-    )
     branch_tok = jnp.einsum(
-        "tb,bd->td", chooser, returned.reshape(places, D), preferred_element_type=jnp.float32
+        "tb,bd->td", chooser, branch, preferred_element_type=jnp.float32
     )
     after_mlp = after_attn + gate_two * branch_tok
     block_out = after_mlp.astype(jnp.bfloat16)[None]
     grad_after = cotangent[0].astype(jnp.float32)
     grad_gate_two = grad_after * branch_tok
     grad_branch = (gate_two * keep * grad_after).astype(jnp.bfloat16)
-    grad_rows = (
-        jnp.einsum("tb,td->bd", chooser, grad_branch, preferred_element_type=jnp.float32)
-        .astype(jnp.bfloat16)
-        .reshape(peers, capacity, D)
-    )
-    grad_rows = lax.all_to_all(grad_rows, "dp", split_axis=0, concat_axis=0, tiled=True).reshape(
-        places, D
-    )
-    again = (
-        lax.all_gather(qkv_weight, "fsdp", axis=1, tiled=True),
-        lax.all_gather(out_weight, "fsdp", axis=1, tiled=True),
-        lax.all_gather(up_weight, "fsdp", axis=1, tiled=True),
-        lax.all_gather(down_weight, "fsdp", axis=1, tiled=True),
-    )
-    back_qkv, back_out, back_up, back_down = (
-        lax.all_gather(again[0], "dp", axis=0, tiled=True),
-        lax.all_gather(again[1], "dp", axis=0, tiled=True),
-        lax.all_gather(again[2], "dp", axis=0, tiled=True),
-        lax.all_gather(again[3], "dp", axis=0, tiled=True),
-    )
+    grad_rows = jnp.einsum(
+        "tb,td->bd", chooser, grad_branch, preferred_element_type=jnp.float32
+    ).astype(jnp.bfloat16)
+    back_qkv, back_out, back_up, back_down = full_qkv, full_out, full_up, full_down
     grad_down_bias = jnp.sum(grad_rows.astype(jnp.float32), axis=0)
     grad_down = jnp.einsum("bf,bd->fd", active, grad_rows, preferred_element_type=jnp.float32)
     grad_active = jnp.einsum("bd,fd->bf", grad_rows, back_down, preferred_element_type=jnp.float32)
@@ -215,11 +187,8 @@
     grad_arrived = jnp.einsum(
         "bf,df->bd", grad_hidden, back_up, preferred_element_type=jnp.float32
     ).astype(jnp.bfloat16)
-    grad_arrived = lax.all_to_all(
-        grad_arrived.reshape(peers, capacity, D), "dp", split_axis=0, concat_axis=0, tiled=True
-    )
     grad_second = jnp.einsum(
-        "tb,bd->td", chooser, grad_arrived.reshape(places, D), preferred_element_type=jnp.float32
+        "tb,bd->td", chooser, grad_arrived, preferred_element_type=jnp.float32
     )
     grad_scale_two = grad_second * normed_two
     grad_mid = grad_after + norm_back(grad_second * (1.0 + scale_two), normed_two, inverse_two)
@@ -308,57 +277,42 @@
         [jnp.einsum("ts,td->sd", member, single, precision=highest) for single in token_grads],
         axis=1,
     )
-    grad_ada_bias = jnp.sum(grad_modulation, axis=0)
+    mod_columns = lax.all_to_all(
+        grad_modulation, "fsdp", split_axis=1, concat_axis=0, tiled=True
+    )
+    mod_all = lax.all_gather(mod_columns, "dp", axis=0, tiled=True)
+    grad_ada_bias = jnp.sum(mod_all, axis=0)
     grad_ada = jnp.einsum(
-        "sd,se->de", cond_act.astype(jnp.float32), grad_modulation, precision=highest
-    )
-    reduced = (
-        lax.psum_scatter(grad_ada, "dp", scatter_dimension=0, tiled=True),
-        lax.psum_scatter(grad_qkv, "dp", scatter_dimension=0, tiled=True),
-        lax.psum_scatter(grad_out, "dp", scatter_dimension=0, tiled=True),
-        lax.psum_scatter(grad_up, "dp", scatter_dimension=0, tiled=True),
-        lax.psum_scatter(grad_down, "dp", scatter_dimension=0, tiled=True),
-    )
-    shares = (
-        lax.psum_scatter(reduced[0], "fsdp", scatter_dimension=1, tiled=True),
-        lax.psum_scatter(reduced[1], "fsdp", scatter_dimension=1, tiled=True),
-        lax.psum_scatter(reduced[2], "fsdp", scatter_dimension=1, tiled=True),
-        lax.psum_scatter(reduced[3], "fsdp", scatter_dimension=1, tiled=True),
-        lax.psum_scatter(reduced[4], "fsdp", scatter_dimension=1, tiled=True),
-        lax.psum_scatter(grad_ada_bias, "fsdp", scatter_dimension=0, tiled=True),
-        lax.psum_scatter(grad_query_bias, "fsdp", scatter_dimension=0, tiled=True),
-        lax.psum_scatter(grad_value_bias, "fsdp", scatter_dimension=0, tiled=True),
-        lax.psum_scatter(grad_out_bias, "fsdp", scatter_dimension=0, tiled=True),
-        lax.psum_scatter(grad_up_bias, "fsdp", scatter_dimension=0, tiled=True),
-        lax.psum_scatter(grad_down_bias, "fsdp", scatter_dimension=0, tiled=True),
-    )
-    matrix_shares = shares[:5]
-    bias_shares = shares[5:]
-    bias_totals = lax.psum(
-        (
-            bias_shares[0],
-            bias_shares[1],
-            bias_shares[2],
-            bias_shares[3],
-            bias_shares[4],
-            bias_shares[5],
-        ),
-        "dp",
-    )
+        "sd,se->de", cond_slice.astype(jnp.float32), mod_all, precision=highest
+    )
+
+    def scatter_matrix(full):
+        rows, columns = full.shape[0] // peers, full.shape[1] // mates
+        blocks = full.astype(jnp.bfloat16).reshape(peers, rows, mates, columns)
+        blocks = blocks.transpose(0, 2, 1, 3).reshape(peers * mates * rows, columns)
+        share = lax.psum_scatter(blocks, ("dp", "fsdp"), scatter_dimension=0, tiled=True)
+        return share.astype(jnp.float32)
+
+    shares = [scatter_matrix(full) for full in (grad_qkv, grad_out, grad_up, grad_down)]
+    bias_grads = (grad_query_bias, grad_value_bias, grad_out_bias, grad_up_bias, grad_down_bias)
+    packed = jnp.concatenate([vector.reshape(mates, -1) for vector in bias_grads], axis=1)
+    packed = lax.psum_scatter(packed, "fsdp", scatter_dimension=0, tiled=True)
+    packed = lax.psum(packed[0], "dp")
+    totals = [packed[low:high] for low, high in zip(edges[:-1], edges[1:])]
     return (
         block_out,
         grad_inputs[None],
-        matrix_shares[0],
-        bias_totals[0],
-        matrix_shares[1],
-        bias_totals[1],
-        bias_totals[2],
-        matrix_shares[2],
-        bias_totals[3],
-        matrix_shares[3],
-        bias_totals[4],
-        matrix_shares[4],
-        bias_totals[5],
+        grad_ada,
+        grad_ada_bias,
+        shares[0],
+        totals[0],
+        totals[1],
+        shares[1],
+        totals[2],
+        shares[2],
+        totals[3],
+        shares[3],
+        totals[4],
     )
 
 

time: 2780 us -> 1170 us (0.42)
  waiting for transfers between devices: 2160 us -> 346 us
  local copies, waits for them, and re-layouts: 93.2 us -> 267 us
  blocking collectives: 77.7 us -> 141 us
    reduce_scatter x6 -> x3, waiting for transfers between devices: 1440 us -> 146 us  [scatter_matrix(): lax.psum_scatter(blocks, ('dp', 'fsdp'), scatter_dimension=0, tiled=True)]
    all_gather x8 -> x4, waiting for transfers between devices: 569 us -> 65 us  [gather_matrix(): stacked = lax.all_gather(shard, ('dp', 'fsdp'), axis=0, tiled=False)]
    reshape x2 -> x16, local copies, waits for them, and re-layouts: 0.11 us -> 148 us  [the longest x4 60 us: scatter_matrix(): blocks = full.astype(jnp.bfloat16).reshape(peers, rows, mates, columns)]
    all_gather x3, blocking collectives: 27 us -> 69 us  [the longest x1 36.9 us: shards(): cond_all = lax.all_gather(cond_act, ('dp', 'fsdp'), axis=0, tiled=True)]
    dot_general x6 -> x4, matrix products: 58.5 us -> 35.8 us  [the longest x1 18.3 us: shards(): jnp.einsum('tb,bd->td', chooser, grad_arrived, preferred_element_type=jnp...]
    unnamed x22 -> x11, waiting for transfers between devices: 119 us -> 132 us
  transfers between devices with their start and end apart: 23 -> 12, of which waited for: 15 -> 5; matrix products, arithmetic and copies ran while one was open for 15% -> 35% of each run, Pallas kernels for 0% -> 0%
where the time goes in v1:
time: 1170 us; the launch traced here: 1160 us
  waiting for transfers between devices  346 us (30%)
  matrix products  301 us (26%)
  local copies, waits for them, and re-layouts  267 us (23%)
  blocking collectives  141 us (12%)
  other arithmetic  76.8 us (7%)
  between operations  16.6 us (1%)
  starting transfers between devices  11.8 us (1%)
    reduce_scatter x3, waiting for transfers between devices, scatter_matrix(): lax.psum_scatter(blocks, ('dp', 'fsdp'), scatter_dimension=0, tiled=True)  146 us
    unnamed x11, waiting for transfers between devices  132 us
    all_gather x4, waiting for transfers between devices, gather_matrix(): stacked = lax.all_gather(shard, ('dp', 'fsdp'), axis=0, tiled=False)  65 us
    reshape x4, local copies, waits for them, and re-layouts, scatter_matrix(): blocks = full.astype(jnp.bfloat16).reshape(peers, rows, mates, columns)  60 us
    reshape x4, local copies, waits for them, and re-layouts, gather_matrix(): stacked = stacked.reshape(peers, mates, rows, columns).transpose(0, 2, 1, 3)  47.7 us
    unnamed x2, blocking collectives  46 us
    dot_general x4, matrix products, shards(): jnp.einsum('qhd,khd->hqk', grad_piece, values_all[:, heads_here], preferr...  43.5 us
    unnamed x216, local copies, waits for them, and re-layouts  43.1 us
  transfers between devices with their start and end apart: 12, of which 5 were waited for; matrix products, arithmetic and copies ran while one was open for 35% of the time, Pallas kernels for 0%

profile of v1, /device:TPU:9, one launch (start us, length us, event | category | flops | bytes accessed | tf_op | source)
XLA Modules:
  0.0 1160.2 jit_solution(4579493214141441658)
XLA Ops:
  10.8 36.9 %all-gather.5 = bf16[32,3,1152]{2,1,0:T(4,128)(2,1)S(1)} all-gather(bf16[1,3,1152]{2,1,0:T(4,128)(2,1)S(1)} %fusion.123), channel_id=1, replica_groups=mesh['dp'=8,'fsdp'=4] {'dp','fsdp'}, dimensions={0}, use_global_device_ids=true | all-gather | bytes 228096 | tf_op jit(solution)/shard_map/all_gather | solution.py:95
  48.2 34.4 %fusion = f32[16,1728]{1,0:T(8,128)S(1)} fusion(f32[96,1728]{1,0:T(8,128)S(1)} %fusion.109), kind=kCustom, calls=%all-reduce-scatter | all-reduce-scatter fusion | flops 221185 | bytes 774656
  148.4 14.8 %all-gather.14.cloned.1.call-done = bf16[4608,864]{1,0:T(8,128)(2,1)} async-done(((bf16[144,864]{1,0:T(8,128)(2,1)}), bf16[4608,864]{1,0:T(8,128)(2,1)}) %all-gather.14.cloned.1.call-update) | async-done | bytes 7962640 | tf_op jit(solution)/shard_map/all_gather | solution.py:67
  171.5 14.6 %reshape.304 = bf16[1152,3456]{1,0:T(8,128)(2,1)} reshape(bf16[8,144,4,864]{3,2,1,0:T(4,128)(2,1)} %bitcast.238) | data formatting | bytes 15925248 | tf_op jit(solution)/shard_map/reshape | solution.py:70
  186.1 11.0 add_convert_fusion
  225.3 13.9 %exponential_reduce_fusion.3 = (f32[4,768]{1,0:T(4,128)S(1)}, f32[4,768]{1,0:T(4,128)S(1)}, f32[4,768]{1,0:T(4,128)S(1)}, f32[4,768]{1,0:T(4,128)S(1)}, f32[4,768,768]{1,2,0:T(8,128)}) fusion(f32[4,768,768]{1,2,0:T(8,128)} %get-tuple-element.52, f32[4,768]{1,0:T(4,128)S(1)} %get-tuple-element.51, pred[768,768]{0,1:T(8,128)(4,1)S(1)} %broadcast_compare_fusion, ...), kind=kOutput, calls=%fused_computation.34 | convolution fusion | flops 370397184 | bytes 40611840 | tf_op jit(solution)/shard_map/qhd,khd->hqk/dot_general | solution.py:33
  239.2 10.8 exponential_reduce_fusion.2
  295.4 50.2 %all-gather.20.cloned.1.call-done = bf16[32,576,288]{1,2,0:T(8,128)(2,1)} async-done(((bf16[1,576,288]{1,2,0:T(8,128)(2,1)}), bf16[32,576,288]{1,2,0:T(8,128)(2,1)}) %all-gather.20.cloned.1.call-update) | async-done | bytes 10616848 | tf_op jit(solution)/shard_map/all_gather | solution.py:67
  345.5 25.7 %copy.232 = bf16[8,4,576,288]{2,0,3,1:T(8,128)(2,1)} copy(bf16[8,4,576,288]{2,3,1,0:T(8,128)(2,1)} %bitcast.252) | data formatting | bytes 21233664 | tf_op jit(solution)/shard_map/reshape | solution.py:69
  371.2 18.9 %reshape.314 = bf16[4608,1152]{0,1:T(8,128)(2,1)} reshape(bf16[8,576,4,288]{1,0,3,2:T(8,128)(2,1)} %bitcast.227) | data formatting | bytes 21233664 | tf_op jit(solution)/shard_map/reshape | solution.py:70
  390.1 15.5 %multiply_convert_fusion.4 = (bf16[512,4608]{1,0:T(8,128)(2,1)}, f32[512,4608]{1,0:T(8,128)}) fusion(f32[512,4608]{1,0:T(8,128)} %copy.174, f32[4608]{0:T(1024)S(1)} %reshape.335, bf16[512,1152]{1,0:T(8,128)(2,1)} %convolution_convert_fusion.7, bf16[1152,4608]{1,0:T(8,128)(2,1)} %bitcast.254), kind=kOutput, calls=%fused_computation.23 | convolution fusion | flops 5461770240 | bytes 35407872 | tf_op jit(solution)/shard_map/dot_general | solution.py:163
  405.6 16.9 %convert_reduce_fusion = (f32[4608]{0:T(1024)}, bf16[512,4608]{1,0:T(8,128)(2,1)}) fusion(f32[512,4608]{1,0:T(8,128)} %get-tuple-element.57, f32[4608]{0:T(1024)S(1)} %reshape.335, f32[512,4608]{1,0:T(8,128)} %copy.174, bf16[512,1152]{1,0:T(8,128)(2,1)S(1)} %copy-done.78, bf16[4608,1152]{0,1:T(8,128)(2,1)S(1)} %copy-done.17), kind=kOutput, calls=%fused_computation.14 | convolution fusion | flops 5492436480 | bytes 35426304 | tf_op jit(solution)/shard_map/bd,fd->bf/dot_general | solution.py:182
  422.6 18.3 %fusion.157 = (f32[768]{0:T(1024)S(1)}, f32[768]{0:T(1024)S(1)}, f32[768,1152]{1,0:T(8,128)}, f32[768,1152]{1,0:T(8,128)}) fusion(f32[768]{0:T(1024)S(1)} %add_rsqrt_fusion, f32[768,1152]{1,0:T(8,128)} %copy-done.3, f32[768]{0:T(1024)S(1)} %broadcast_multiply_fusion.4, f32[768,1152]{1,0:T(8,128)} %convolution_add_fusion.1, ...), kind=kOutput, calls=%fused_computation.238 | convolution fusion | flops 6348077056 | bytes 29506560 | tf_op jit(solution)/shard_map/tb,bd->td/dot_general | solution.py:190
  440.9 14.7 %fusion.64 = f32[768,1152]{1,0:T(8,128)} fusion(bf16[512,4608]{1,0:T(8,128)(2,1)} %get-tuple-element.56, bf16[4608,1152]{0,1:T(8,128)(2,1)} %reshape.314, f32[1152]{0:T(1024)S(1)} %copy-done.65, s32[768]{0:T(1024)S(1)} %reduce.2), kind=kOutput, calls=%fused_computation.120 | convolution fusion | flops 6343360512 | bytes 18882048 | tf_op jit(solution)/shard_map/tb,bd->td/dot_general | solution.py:168
  455.6 10.6 convert_reduce_fusion.2
  513.1 28.5 %multiply_reduce_fusion.3 = (f32[4,768]{1,0:T(4,128)S(1)}, f32[4,768]{1,0:T(4,128)S(1)}, f32[4,768]{1,0:T(4,128)S(1)}, f32[4,768]{1,0:T(4,128)S(1)}, f32[4,768,768]{1,2,0:T(8,128)}) fusion(f32[4,768,768]{1,2,0:T(8,128)} %get-tuple-element.52, f32[4,768]{1,0:T(4,128)S(1)} %copy-done.45, pred[768,768]{0,1:T(8,128)(4,1)S(1)} %broadcast_compare_fusion, ...), kind=kOutput, calls=%fused_computation.22 | convolution fusion | flops 386912256 | bytes 78397440 | tf_op jit(solution)/shard_map/qhd,khd->hqk/dot_general | solution.py:224
  541.7 33.6 %multiply_convert_fusion.3 = (bf16[4,768,768]{1,2,0:T(8,128)(2,1)}, bf16[4,768,768]{1,2,0:T(8,128)(2,1)}, bf16[4,768,768]{1,2,0:T(8,128)(2,1)}, bf16[4,768,768]{1,2,0:T(8,128)(2,1)}) fusion(f32[4,768,768]{1,2,0:T(8,128)} %get-tuple-element.58, f32[4,768,768]{1,2,0:T(8,128)} %get-tuple-element.52, f32[4,768]{1,0:T(4,128)S(1)} %get-tuple-element.17, ...), kind=kLoop, calls=%fused_computation.21 | loop fusion | flops 56623104 | bytes 95059968 | tf_op jit(solution)/shard_map/convert_element_type | solution.py:232
  614.7 12.3 %convolution_convert_fusion.2 = bf16[1152,3456]{1,0:T(8,128)(2,1)} fusion(bf16[768,1152]{1,0:T(8,128)(2,1)S(1)} %copy-done.33, bf16[768,1152]{0,1:T(8,128)(2,1)S(1)} %bitcast.265, bf16[768,1152]{0,1:T(8,128)(2,1)S(1)} %bitcast.286, bf16[768,1152]{0,1:T(8,128)(2,1)S(1)} %bitcast.267), kind=kOutput, calls=%fused_computation.2 | convolution fusion | flops 6135201792 | bytes 15040512 | tf_op jit(solution)/shard_map/td,te->de/dot_general | solution.py:264
  627.0 17.5 %reshape.318 = bf16[8,144,4,864]{3,2,1,0:T(4,128)(2,1)} reshape(bf16[1152,3456]{1,0:T(8,128)(2,1)} %convolution_convert_fusion.2) | data formatting | bytes 15925248 | tf_op jit(solution)/shard_map/reshape | solution.py:291
  653.9 12.2 %convolution_convert_fusion = bf16[4608,1152]{1,0:T(8,128)(2,1)} fusion(bf16[512,4608]{1,0:T(8,128)(2,1)} %get-tuple-element.56, bf16[512,1152]{1,0:T(8,128)(2,1)S(1)} %copy-done.79), kind=kOutput, calls=%fused_computation | convolution fusion | flops 5441126400 | bytes 16515072 | tf_op jit(solution)/shard_map/bf,bd->fd/dot_general | solution.py:181
  666.1 14.3 %copy.194 = bf16[4608,1152]{0,1:T(8,128)(2,1)} copy(bf16[4608,1152]{1,0:T(8,128)(2,1)} %convolution_convert_fusion) | data formatting | bytes 21233664 | tf_op jit(solution)/shard_map/convert_element_type | solution.py:291
  680.4 19.8 %reshape.329 = bf16[8,576,4,288]{1,0,3,2:T(8,128)(2,1)} reshape(bf16[4608,1152]{0,1:T(8,128)(2,1)} %copy.194) | data formatting | bytes 21233664 | tf_op jit(solution)/shard_map/reshape | solution.py:291
  700.2 18.7 %copy.214 = bf16[8,4,576,288]{3,2,1,0:T(8,128)(2,1)} copy(bf16[8,4,576,288]{2,0,3,1:T(8,128)(2,1)} %bitcast.228) | data formatting | bytes 21233664
  720.2 10.7 convolution_convert_fusion.1
  730.9 15.0 %reshape.327 = bf16[8,144,4,1152]{3,2,1,0:T(4,128)(2,1)} reshape(bf16[1152,4608]{1,0:T(8,128)(2,1)} %convolution_convert_fusion.1) | data formatting | bytes 21233664 | tf_op jit(solution)/shard_map/reshape | solution.py:291
  745.9 10.7 copy.193
  761.9 14.7 %fusion.156 = (f32[768]{0:T(1024)S(1)}, f32[768]{0:T(1024)S(1)}, f32[768,1152]{1,0:T(8,128)}, f32[768,1152]{1,0:T(8,128)}) fusion(f32[768]{0:T(1024)S(1)} %copy-done.59, f32[768]{0:T(1024)S(1)} %copy-done.51, bf16[1,768,1152]{2,1,0:T(8,128)(2,1)S(1)} %copy-done.6, f32[768,1152]{1,0:T(8,128)} %copy-done.12, bf16[1152,3456]{1,0:T(8,128)(2,1)} %reshape.304, ...), kind=kOutput, calls=%fused_computation.237 | convolution fusion | flops 6137411584 | bytes 25669632 | tf_op jit(solution)/shard_map/te,de->td/dot_general | solution.py:265
  796.5 11.6 all-reduce.1
  808.8 25.9 %psum.7 = f32[2304]{0:T(1024)S(1)} all-reduce(f32[2304]{0:T(1024)S(1)} %dynamic-slice_reduce_fusion), channel_id=1, replica_groups=mesh['dp'=8,'fsdp'=4] {'dp'}, use_global_device_ids=true, to_apply=%region_31.32 | all-reduce | flops 2304 | bytes 18432 | tf_op jit(solution)/shard_map/psum | solution.py:300
  840.9 26.1 %all-gather.8 = f32[8,12,1728]{2,1,0:T(8,128)S(1)} all-gather(f32[1,12,1728]{2,1,0:T(8,128)S(1)} %reshape.354), channel_id=1, replica_groups=mesh['dp'=8,'fsdp'=4] {'dp'}, dimensions={0}, use_global_device_ids=true | all-gather | bytes 746496 | tf_op jit(solution)/shard_map/all_gather | solution.py:283
  873.7 129.8 %reduce-scatter.15.cloned.1.call-done = bf16[576,288]{1,0:T(8,128)(2,1)} async-done(((bf16[18432,288]{1,0:T(8,128)(2,1)}), bf16[576,288]{1,0:T(8,128)(2,1)}) %reduce-scatter.15.cloned.1.call-update) | async-done | bytes 331792
  1005.7 145.6 %reduce-scatter.13.cloned.1.call-done = bf16[144,1152]{1,0:T(8,128)(2,1)} async-done(((bf16[4608,1152]{1,0:T(8,128)(2,1)}), bf16[144,1152]{1,0:T(8,128)(2,1)}) %reduce-scatter.13.cloned.1.call-update) | async-done | bytes 331792 | tf_op jit(solution)/shard_map/reduce_scatter | solution.py:293
  (371 shorter events, 289.5 us)
Async XLA Ops:
  7.2 40.7 %copy-start = (bf16[144,1728]{1,0:T(8,128)(2,1)S(1)}, bf16[144,1728]{1,0:T(8,128)(2,1)}, u32[]{:S(2)}) copy-start(bf16[144,1728]{1,0:T(8,128)(2,1)} %param.24) | copy-start | bytes 1492996
  7.2 79.3 %copy-start.76 = (s32[1,3]{1,0:T(1,128)S(1)}, s32[1,3]{1,0:T(1,128)}, u32[]{:S(2)}) copy-start(s32[1,3]{1,0:T(1,128)} %param.20) | copy-start | bytes 40
  7.2 79.5 %copy-start.69 = (s32[1,3,16]{2,0,1:T(1,128)S(1)}, s32[1,3,16]{2,0,1:T(1,128)}, u32[]{:S(2)}) copy-start(s32[1,3,16]{2,0,1:T(1,128)} %param.21) | copy-start | bytes 580
  7.2 79.5 %copy-start.70 = (s32[1,3,16]{2,0,1:T(1,128)S(1)}, s32[1,3,16]{2,0,1:T(1,128)}, u32[]{:S(2)}) copy-start(s32[1,3,16]{2,0,1:T(1,128)} %param.22) | copy-start | bytes 580
  7.2 79.5 %copy-start.68 = (s32[1,768]{1,0:T(1,128)S(1)}, s32[1,768]{1,0:T(1,128)}, u32[]{:S(2)}) copy-start(s32[1,768]{1,0:T(1,128)} %param.23) | copy-start | bytes 9220
  7.2 79.5 %copy-start.74 = (bf16[288]{0:T(512)(128)(2,1)S(1)}, bf16[288]{0:T(512)(128)(2,1)}, u32[]{:S(2)}) copy-start(bf16[288]{0:T(512)(128)(2,1)} %param.34) | copy-start | bytes 1732
  7.2 79.5 %copy-start.66 = (bf16[1152]{0:T(1024)(128)(2,1)S(1)}, bf16[1152]{0:T(1024)(128)(2,1)}, u32[]{:S(2)}) copy-start(bf16[1152]{0:T(1024)(128)(2,1)} %param.32) | copy-start | bytes 6916
  7.3 79.5 %copy-start.73 = (bf16[288]{0:T(512)(128)(2,1)S(1)}, bf16[288]{0:T(512)(128)(2,1)}, u32[]{:S(2)}) copy-start(bf16[288]{0:T(512)(128)(2,1)} %param.30) | copy-start | bytes 1732
  7.3 79.5 %copy-start.72 = (bf16[288]{0:T(512)(128)(2,1)S(1)}, bf16[288]{0:T(512)(128)(2,1)}, u32[]{:S(2)}) copy-start(bf16[288]{0:T(512)(128)(2,1)} %param.28) | copy-start | bytes 1732
  7.3 79.5 %copy-start.71 = (bf16[288]{0:T(512)(128)(2,1)S(1)}, bf16[288]{0:T(512)(128)(2,1)}, u32[]{:S(2)}) copy-start(bf16[288]{0:T(512)(128)(2,1)} %param.27) | copy-start | bytes 1732
  7.3 85.7 %copy-start.5 = (bf16[1,768,1152]{2,1,0:T(8,128)(2,1)S(1)}, bf16[1,768,1152]{2,1,0:T(8,128)(2,1)}, u32[]{:S(2)}) copy-start(bf16[1,768,1152]{2,1,0:T(8,128)(2,1)} %param.18) | copy-start | bytes 5308420
  7.3 129.2 %all-gather.16.cloned.1.call-start = ((), (), s32[]{:S(2)}) async-start(), calls=%async_computation.10 | async-start | bytes 3649536 | tf_op jit(solution)/shard_map/all_gather | solution.py:67
  8.0 155.2 %all-gather.14.cloned.1.call-start = ((), (), s32[]{:S(2)}) async-start(), calls=%async_computation.9 | async-start | bytes 8515584 | tf_op jit(solution)/shard_map/all_gather | solution.py:67
  8.8 273.4 %all-gather.18.cloned.1.call-start = ((), (), s32[]{:S(2)}) async-start(), calls=%async_computation.11 | async-start | bytes 10948608 | tf_op jit(solution)/shard_map/all_gather | solution.py:67
  9.5 336.0 %all-gather.20.cloned.1.call-start = ((), (), s32[]{:S(2)}) async-start(), calls=%async_computation.12 | async-start | bytes 12165120 | tf_op jit(solution)/shard_map/all_gather | solution.py:67
  47.9 47.5 %copy-start.35 = (bf16[96,1152]{1,0:T(8,128)(2,1)}, bf16[96,1152]{1,0:T(8,128)(2,1)S(1)}, u32[]{:S(2)}) copy-start(bf16[96,1152]{1,0:T(8,128)(2,1)S(1)} %reshape.349) | copy-start | bytes 663556
  47.9 47.6 %copy-start.67 = (bf16[1728]{0:T(1024)(128)(2,1)S(1)}, bf16[1728]{0:T(1024)(128)(2,1)}, u32[]{:S(2)}) copy-start(bf16[1728]{0:T(1024)(128)(2,1)} %param.25) | copy-start | bytes 10372
  82.6 29.4 %collective-permute-start = (f32[16,1728]{1,0:T(8,128)S(1)}, f32[16,1728]{1,0:T(8,128)S(1)}, u32[]{:S(2)}, u32[]{:S(2)}) collective-permute-start(f32[16,1728]{1,0:T(8,128)S(1)} %fusion), channel_id=1, source_target_pairs={{0,4},{4,8},{8,12},{12,16},{16,20},{20,24},{24,28},{1,5},{5,9},{9,... | collective-permute-start | bytes 331784
  84.6 27.5 %collective-permute-start.1 = (f32[12,1728]{1,0:T(8,128)S(1)}, f32[12,1728]{1,0:T(8,128)S(1)}, u32[]{:S(2)}, u32[]{:S(2)}) collective-permute-start(f32[12,1728]{1,0:T(8,128)S(1)} %slice.189), channel_id=1, source_target_pairs={{0,8},{4,12},{8,16},{12,20},{16,24},{20,28},{1,9},{5,13},{9,17},{1... | collective-permute-start | bytes 248840
  86.7 187.6 %copy-start.54 = (s32[3,1]{0,1:T(1,128)}, s32[3,1]{0,1:T(1,128)S(1)}, u32[]{:S(2)}) copy-start(s32[3,1]{0,1:T(1,128)S(1)} %reduce-window.4) | copy-start | bytes 40
  93.3 180.9 %copy-start.56 = (s32[3]{0:T(128)}, s32[3]{0:T(128)S(1)}, u32[]{:S(2)}) copy-start(s32[3]{0:T(128)S(1)} %fusion.129) | copy-start | bytes 40
  93.4 34.6 %copy-start.50 = (f32[768]{0:T(1024)}, f32[768]{0:T(1024)S(1)}, u32[]{:S(2)}) copy-start(f32[768]{0:T(1024)S(1)} %broadcast_multiply_fusion.5) | copy-start | bytes 9220
  113.1 7.3 all-to-all-start
  116.6 753.7 %reduce-scatter.11.cloned.1.call-start = ((), (), s32[]{:S(2)}) async-start(), calls=%async_computation.7 | async-start | bytes 3649536 | tf_op jit(solution)/shard_map/reduce_scatter | solution.py:293
  213.9 36.2 %copy-start.2 = (f32[4,768,768]{1,2,0:T(8,128)}, f32[4,768,768]{1,2,0:T(8,128)S(1)}, u32[]{:S(2)}) copy-start(f32[4,768,768]{1,2,0:T(8,128)S(1)} %fusion.99) | copy-start | bytes 28311556
  273.8 181.8 %copy-start.52 = (f32[768]{0:T(1024)}, f32[768]{0:T(1024)S(1)}, u32[]{:S(2)}) copy-start(f32[768]{0:T(1024)S(1)} %broadcast_multiply_fusion.4) | copy-start | bytes 9220
  277.0 178.5 %copy-start.60 = (f32[768]{0:T(1024)}, f32[768]{0:T(1024)S(1)}, u32[]{:S(2)}) copy-start(f32[768]{0:T(1024)S(1)} %add_rsqrt_fusion) | copy-start | bytes 9220
  599.0 272.9 %reduce-scatter.9.cloned.1.call-start = ((), (), s32[]{:S(2)}) async-start(), calls=%async_computation.6 | async-start | bytes 8515584 | tf_op jit(solution)/shard_map/reduce_scatter | solution.py:293
  652.6 350.9 %reduce-scatter.15.cloned.1.call-start = ((), (), s32[]{:S(2)}) async-start(), calls=%async_computation.13 | async-start | bytes 14598144
  718.9 432.4 %reduce-scatter.13.cloned.1.call-start = ((), (), s32[]{:S(2)}) async-start(), calls=%async_computation.8 | async-start | bytes 10948608 | tf_op jit(solution)/shard_map/reduce_scatter | solution.py:293
  792.7 48.2 %all-to-all-start.1 = ((f32[3,4,1728]{2,0,1:T(4,128)}), f32[3,4,1728]{2,0,1:T(4,128)S(1)}, u32[]{:S(2)}, u32[]{:S(2)}) async-start(f32[3,4,1728]{2,0,1:T(4,128)} %copy.190), calls=%async_computation.1 | async-start | bytes 229376 | tf_op jit(solution)/shard_map/all_to_all | solution.py:280
  867.0 286.1 %copy-start.1 = (bf16[144,1728]{1,0:T(8,128)(2,1)S(1)}, bf16[144,1728]{1,0:T(8,128)(2,1)}, u32[]{:S(2)}) copy-start(bf16[144,1728]{1,0:T(8,128)(2,1)} %param.24) | copy-start | bytes 1492996
  (82 other events, 499.6 us)
Sparse Core Ops, SparseCore 0:
  11.0 70.7 all-gather.15
  84.7 78.4 all-gather.13
  166.1 85.6 all-gather.17
  254.6 90.8 all-gather.19
  599.1 99.5 reduce-scatter.10
  704.5 130.3 reduce-scatter.8
  841.9 161.5 reduce-scatter.14
  1010.7 140.5 reduce-scatter.12

commit v2 on v1

--- a/solution.py
+++ b/solution.py
@@ -1,6 +1,10 @@
+import functools
+
 import jax
 import jax.numpy as jnp
 from jax import lax
+from jax.experimental import pallas as pl
+from jax.experimental.pallas import tpu as pltpu
 from jax.sharding import PartitionSpec as P
 
 D = 1152
@@ -13,6 +17,406 @@
 
 highest = lax.Precision.HIGHEST
 epsilon = 1e-06
+
+
+MESH = pl.DeviceIdType.MESH
+SHARD = 144
+UPPER = 80
+
+
+class Place:
+    def __init__(self):
+        dp, fsdp = lax.axis_index("dp"), lax.axis_index("fsdp")
+        self.z, self.x = lax.div(dp, 2), lax.rem(dp, 2)
+        self.y, self.c = lax.div(fsdp, 2), lax.rem(fsdp, 2)
+        z = self.z
+        self.zs = (z, z + 1 - 2 * lax.rem(z, 2), lax.rem(z + 2, 4), 3 - z)
+
+    def device(self, z=None, x=None, y=None, c=None):
+        z, x = self.z if z is None else z, self.x if x is None else x
+        y, c = self.y if y is None else y, self.c if c is None else c
+        return (2 * z + x, 2 * y + c)
+
+    def meet(self):
+        barrier = pltpu.get_barrier_semaphore()
+        others = [self.device(z=self.zs[k]) for k in (1, 2, 3)]
+        others += [self.device(x=1 - self.x), self.device(y=1 - self.y), self.device(c=1 - self.c)]
+        for other in others:
+            pl.semaphore_signal(barrier, inc=1, device_id=other, device_id_type=MESH)
+        pl.semaphore_wait(barrier, len(others))
+
+
+class Copies:
+    def __init__(self, send_sems, recv_sems):
+        self.send_sems, self.recv_sems, self.made = send_sems, recv_sems, []
+
+    def make(self, source, target, device):
+        index = len(self.made)
+        copy = pltpu.make_async_remote_copy(
+            src_ref=source,
+            dst_ref=target,
+            send_sem=self.send_sems.at[index],
+            recv_sem=self.recv_sems.at[index],
+            device_id=device,
+            device_id_type=MESH,
+        )
+        self.made.append(copy)
+        return copy
+
+
+GATHER_COPIES = 35
+
+
+class Gather:
+    def __init__(self, place, source, slot, send_sems, recv_sems, local_sem, swap):
+        x, y, c, zs = place.x, place.y, place.c, place.zs
+        self.copies = Copies(send_sems, recv_sems)
+        make = self.copies.make
+        first, second = (SHARD - UPPER, UPPER) if swap else (0, UPPER)
+        upper = pl.ds(first, second)
+        lower = pl.ds(0, SHARD - UPPER) if swap else pl.ds(UPPER, SHARD - UPPER)
+        over_x, over_y, beside = (
+            place.device(x=1 - x),
+            place.device(y=1 - y),
+            place.device(c=1 - c),
+        )
+        own = [slot(y, c, zs[k], x) for k in range(4)]
+        held = [source] + own[1:]
+        from_x = [slot(y, c, zs[k], 1 - x) for k in range(4)]
+        from_y = [slot(1 - y, c, zs[k], x) for k in range(4)]
+        across = [slot(1 - y, c, zs[k], 1 - x) for k in range(4)]
+        self.local = pltpu.make_async_copy(source, own[0], local_sem)
+        self.along = [None] + [make(source, own[0], place.device(z=zs[k])) for k in (1, 2, 3)]
+        self.to_x = [make(held[k], own[k], over_x) for k in range(4)]
+        self.to_y = [make(held[k], own[k], over_y) for k in range(4)]
+        self.x_to_y = [make(s.at[upper], s.at[upper], over_y) for s in from_x]
+        self.y_to_x = [make(s.at[lower], s.at[lower], over_x) for s in from_y]
+        self.pair = [make(held[k], own[k], beside) for k in range(4)]
+        self.pair_x = [make(s, s, beside) for s in from_x]
+        self.pair_y = [make(s, s, beside) for s in from_y]
+        self.pair_across = [make(s, s, beside) for s in across]
+
+    def start(self):
+        self.along[1].start()
+        self.to_x[0].start()
+        self.to_y[0].start()
+        self.along[2].start()
+        self.along[3].start()
+        self.pair[0].start()
+        self.local.start()
+
+    def pass_along(self, k):
+        self.along[k].wait_recv()
+        self.to_x[k].start()
+        self.to_y[k].start()
+        self.pair[k].start()
+
+    def pass_across(self, k):
+        self.to_x[k].wait_recv()
+        self.x_to_y[k].start()
+        self.pair_x[k].start()
+        self.to_y[k].wait_recv()
+        self.y_to_x[k].start()
+        self.pair_y[k].start()
+
+    def pass_pair(self, k):
+        self.x_to_y[k].wait_recv()
+        self.y_to_x[k].wait_recv()
+        self.pair_across[k].start()
+
+    def finish(self):
+        self.local.wait()
+        for copy in self.pair + self.pair_x + self.pair_y + self.pair_across:
+            copy.wait_recv()
+        for copy in self.copies.made:
+            copy.wait_send()
+
+
+def gather_kernel(*refs):
+    sources, targets = refs[:3], refs[3:6]
+    send_sems, recv_sems, local_sems = refs[6:]
+    place = Place()
+    place.meet()
+
+    def slot_of(r):
+        if r == 2:
+            return lambda y, c, z, x: targets[r].at[z, x, y, c]
+        return lambda y, c, z, x: targets[r].at[y, c, z, x]
+
+    rounds = [
+        Gather(
+            place,
+            sources[r],
+            slot_of(r),
+            send_sems.at[r],
+            recv_sems.at[r],
+            local_sems.at[r],
+            r % 2 == 1,
+        )
+        for r in range(3)
+    ]
+    rounds[0].start()
+    for k in (1, 2, 3):
+        rounds[0].pass_along(k)
+    for r in range(3):
+        if r < 2:
+            rounds[r + 1].start()
+        for k in range(4):
+            rounds[r].pass_across(k)
+        if r < 2:
+            for k in (1, 2, 3):
+                rounds[r + 1].pass_along(k)
+        for k in range(4):
+            rounds[r].pass_pair(k)
+    for each in rounds:
+        each.finish()
+
+
+def gather_block(qkv_weight, out_weight, up_weight, down_weight):
+    down_rows = lax.all_to_all(down_weight, "fsdp", split_axis=0, concat_axis=1, tiled=True)
+    sources = (jnp.concatenate([qkv_weight, out_weight], axis=1), up_weight, down_rows)
+    shapes = ((2, 2, 4, 2), (2, 2, 4, 2), (4, 2, 2, 2))
+    anywhere = pl.BlockSpec(memory_space=pl.ANY)
+    mixed, ups, downs = pl.pallas_call(
+        gather_kernel,
+        out_shape=[
+            jax.ShapeDtypeStruct(shape + (SHARD, D), jnp.bfloat16) for shape in shapes
+        ],
+        in_specs=[anywhere] * 3,
+        out_specs=[anywhere] * 3,
+        scratch_shapes=[
+            pltpu.SemaphoreType.DMA((3, GATHER_COPIES)),
+            pltpu.SemaphoreType.DMA((3, GATHER_COPIES)),
+            pltpu.SemaphoreType.DMA((3,)),
+        ],
+        compiler_params=pltpu.CompilerParams(collective_id=1, has_side_effects=True),
+    )(*sources)
+    mixed, ups = mixed.reshape(4, D, D), ups.reshape(4, D, D)
+    own = qkv_weight.shape[1]
+    return (
+        mixed[:, :, :own].transpose(1, 0, 2).reshape(D, 3 * D),
+        mixed[:, :, own:].transpose(1, 0, 2).reshape(D, D),
+        ups.transpose(1, 0, 2).reshape(D, FF),
+        downs.reshape(FF, D),
+    )
+
+
+def gather_any(*shards):
+    peers, mates = lax.axis_size("dp"), lax.axis_size("fsdp")
+    results = []
+    for shard in shards:
+        stacked = lax.all_gather(shard, ("dp", "fsdp"), axis=0, tiled=False)
+        rows, columns = shard.shape
+        stacked = stacked.reshape(peers, mates, rows, columns).transpose(0, 2, 1, 3)
+        results.append(stacked.reshape(peers * rows, mates * columns))
+    return results
+
+
+SCATTER_COPIES = 27
+
+
+class Scatter:
+    def __init__(self, place, parts, bufs, out, send_sems, recv_sems, swap):
+        x, y, zs = place.x, place.y, place.zs
+        self.place, self.parts, self.out = place, parts, out
+        self.by_x, self.by_y, self.from_x, self.from_y, self.from_z = bufs
+        self.copies = Copies(send_sems, recv_sems)
+        make = self.copies.make
+        self.upper = (SHARD - UPPER, UPPER) if swap else (0, UPPER)
+        self.lower = (0, SHARD - UPPER) if swap else (UPPER, SHARD - UPPER)
+        a, b = pl.ds(*self.upper), pl.ds(*self.lower)
+        over_x, over_y = place.device(x=1 - x), place.device(y=1 - y)
+        four = range(4)
+        self.across_y = [
+            make(parts.at[1 - y, zs[k], 1 - x, a], self.by_y.at[k, a], over_y) for k in four
+        ]
+        self.across_x = [
+            make(parts.at[1 - y, zs[k], 1 - x, b], self.by_x.at[k, b], over_x) for k in four
+        ]
+        self.x_lower = [make(parts.at[y, zs[k], 1 - x, b], self.from_x.at[k, b], over_x) for k in four]
+        self.y_upper = [make(parts.at[1 - y, zs[k], x, a], self.from_y.at[k, a], over_y) for k in four]
+        self.x_upper = [make(parts.at[y, zs[k], 1 - x, a], self.from_x.at[k, a], over_x) for k in four]
+        self.y_lower = [make(parts.at[1 - y, zs[k], x, b], self.from_y.at[k, b], over_y) for k in four]
+        self.along = [None] + [
+            make(parts.at[y, zs[k], x], self.from_z.at[k - 1], place.device(z=zs[k]))
+            for k in (1, 2, 3)
+        ]
+
+    def start(self, k):
+        self.across_y[k].start()
+        self.across_x[k].start()
+        self.x_lower[k].start()
+        self.y_upper[k].start()
+
+    def add(self, index, rows, terms):
+        for at in range(0, rows[1], 16):
+            here = pl.ds(rows[0] + at, 16)
+            total = self.parts[(*index, here)].astype(jnp.float32)
+            for term, k in terms:
+                total = total + term[k, here].astype(jnp.float32)
+            self.parts[(*index, here)] = total.astype(jnp.bfloat16)
+
+    def pass_across(self, k):
+        x, y, z = self.place.x, self.place.y, self.place.zs[k]
+        self.across_y[k].wait_recv()
+        self.add((y, z, 1 - x), self.upper, ((self.by_y, k),))
+        self.x_upper[k].start()
+        self.across_x[k].wait_recv()
+        self.add((1 - y, z, x), self.lower, ((self.by_x, k),))
+        self.y_lower[k].start()
+
+    def pass_along(self, k):
+        x, y, z = self.place.x, self.place.y, self.place.zs[k]
+        for copy in (self.x_upper[k], self.x_lower[k], self.y_upper[k], self.y_lower[k]):
+            copy.wait_recv()
+        self.add((y, z, x), (0, SHARD), ((self.from_x, k), (self.from_y, k)))
+        if k:
+            self.along[k].start()
+
+    def close(self):
+        x, y, z = self.place.x, self.place.y, self.place.z
+        for k in (1, 2, 3):
+            self.along[k].wait_recv()
+        for at in range(0, SHARD, 16):
+            here = pl.ds(at, 16)
+            total = self.parts[y, z, x, here].astype(jnp.float32)
+            for k in range(3):
+                total = total + self.from_z[k, here].astype(jnp.float32)
+            self.out[here] = total
+
+    def finish(self):
+        for copy in self.copies.made:
+            copy.wait_send()
+
+
+ORDER = (1, 2, 3, 0)
+
+
+def scatter_kernel(*refs):
+    grads, outs = refs[:3], refs[3:6]
+    parts, halves, bufs = refs[6], refs[7], refs[8:13]
+    send_sems, recv_sems, pair_send, pair_recv, local_sems = refs[13:]
+    place = Place()
+    place.meet()
+    rounds, pairs, locals_ = [], [], []
+    for r in range(3):
+        rounds.append(
+            Scatter(
+                place,
+                parts.at[r],
+                [buf.at[r] for buf in bufs],
+                outs[r],
+                send_sems.at[r],
+                recv_sems.at[r],
+                r % 2 == 1,
+            )
+        )
+
+        def blocks(y, c, grad=grads[r], natural=r == 0):
+            return grad.at[:, :, y, c] if natural else grad.at[y, c]
+
+        pairs.append(
+            [
+                pltpu.make_async_remote_copy(
+                    src_ref=blocks(y, 1 - place.c),
+                    dst_ref=halves.at[r, y],
+                    send_sem=pair_send.at[r, y],
+                    recv_sem=pair_recv.at[r, y],
+                    device_id=place.device(c=1 - place.c),
+                    device_id_type=MESH,
+                )
+                for y in range(2)
+            ]
+        )
+        locals_.append(
+            [
+                pltpu.make_async_copy(blocks(y, place.c), parts.at[r, y], local_sems.at[r, y])
+                for y in range(2)
+            ]
+        )
+
+    def pair(r):
+        for y in range(2):
+            pairs[r][y].wait_recv()
+            locals_[r][y].wait()
+
+            def body(i, carry):
+                z, x = lax.div(i, 2), lax.rem(i, 2)
+                for at in range(0, SHARD, 16):
+                    here = pl.ds(at, 16)
+                    total = parts[r, y, z, x, here].astype(jnp.float32)
+                    total = total + halves[r, y, z, x, here].astype(jnp.float32)
+                    parts[r, y, z, x, here] = total.astype(jnp.bfloat16)
+                return carry
+
+            lax.fori_loop(0, 8, body, 0)
+
+    for r in range(3):
+        for y in range(2):
+            pairs[r][y].start()
+            locals_[r][y].start()
+    pair(0)
+    for k in ORDER:
+        rounds[0].start(k)
+    for r in range(3):
+        if r < 2:
+            pair(r + 1)
+        for k in ORDER:
+            rounds[r].pass_across(k)
+        if r < 2:
+            for k in ORDER:
+                rounds[r + 1].start(k)
+        for k in ORDER:
+            rounds[r].pass_along(k)
+        if r:
+            rounds[r - 1].close()
+    rounds[2].close()
+    for r in range(3):
+        rounds[r].finish()
+        for copy in pairs[r]:
+            copy.wait_send()
+
+
+def scatter_block(grad_qkv, grad_out, grad_up, grad_down):
+    def columns(full):
+        return full.reshape(D, 4, -1).transpose(1, 0, 2)
+
+    mixed = jnp.concatenate([columns(grad_qkv), columns(grad_out)], axis=2)
+    blocks = (
+        grad_down.reshape(4, 2, 2, 2, SHARD, D),
+        columns(grad_up).reshape(2, 2, 4, 2, SHARD, D),
+        mixed.reshape(2, 2, 4, 2, SHARD, D),
+    )
+    vmem, dma = pltpu.VMEM, pltpu.SemaphoreType.DMA
+    shares = pl.pallas_call(
+        scatter_kernel,
+        out_shape=[jax.ShapeDtypeStruct((SHARD, D), jnp.float32)] * 3,
+        in_specs=[pl.BlockSpec(memory_space=pl.ANY)] * 3,
+        out_specs=[pl.BlockSpec(memory_space=pltpu.VMEM)] * 3,
+        scratch_shapes=[vmem((3, 2, 4, 2, SHARD, D), jnp.bfloat16)] * 2
+        + [vmem((3, 4, SHARD, D), jnp.bfloat16)] * 4
+        + [vmem((3, 3, SHARD, D), jnp.bfloat16)]
+        + [dma((3, SCATTER_COPIES))] * 2
+        + [dma((3, 2))] * 3,
+        compiler_params=pltpu.CompilerParams(
+            collective_id=2, has_side_effects=True, vmem_limit_bytes=60 * 2**20
+        ),
+    )(*blocks)
+    down = lax.all_to_all(shares[0], "fsdp", split_axis=1, concat_axis=0, tiled=True)
+    own = grad_qkv.shape[1] // 4
+    return (shares[2][:, :own], shares[2][:, own:], shares[1], down)
+
+
+def scatter_any(*grads):
+    peers, mates = lax.axis_size("dp"), lax.axis_size("fsdp")
+    results = []
+    for full in grads:
+        rows, columns = full.shape[0] // peers, full.shape[1] // mates
+        blocks = full.reshape(peers, rows, mates, columns)
+        blocks = blocks.transpose(0, 2, 1, 3).reshape(peers * mates * rows, columns)
+        share = lax.psum_scatter(blocks, ("dp", "fsdp"), scatter_dimension=0, tiled=True)
+        results.append(share.astype(jnp.float32))
+    return results
 
 
 def layer_norm(values):
@@ -63,15 +467,9 @@
     peers = lax.axis_size("dp")
     mates = lax.axis_size("fsdp")
 
-    def gather_matrix(shard):
-        stacked = lax.all_gather(shard, ("dp", "fsdp"), axis=0, tiled=False)
-        rows, columns = shard.shape
-        stacked = stacked.reshape(peers, mates, rows, columns).transpose(0, 2, 1, 3)
-        return stacked.reshape(peers * rows, mates * columns)
-
-    full_qkv, full_out, full_up, full_down = [
-        gather_matrix(shard) for shard in (qkv_weight, out_weight, up_weight, down_weight)
-    ]
+    on_block = peers == 8 and mates == 4
+    gather = gather_block if on_block else gather_any
+    full_qkv, full_out, full_up, full_down = gather(qkv_weight, out_weight, up_weight, down_weight)
     vectors = (query_bias, value_bias, out_bias, up_bias, down_bias)
     packed_bias = lax.all_gather(jnp.concatenate(vectors), "fsdp", axis=0, tiled=False)
     edges = [0]
@@ -286,14 +684,10 @@
         "sd,se->de", cond_slice.astype(jnp.float32), mod_all, precision=highest
     )
 
-    def scatter_matrix(full):
-        rows, columns = full.shape[0] // peers, full.shape[1] // mates
-        blocks = full.astype(jnp.bfloat16).reshape(peers, rows, mates, columns)
-        blocks = blocks.transpose(0, 2, 1, 3).reshape(peers * mates * rows, columns)
-        share = lax.psum_scatter(blocks, ("dp", "fsdp"), scatter_dimension=0, tiled=True)
-        return share.astype(jnp.float32)
-
-    shares = [scatter_matrix(full) for full in (grad_qkv, grad_out, grad_up, grad_down)]
+    scatter = scatter_block if on_block else scatter_any
+    shares = scatter(
+        *[full.astype(jnp.bfloat16) for full in (grad_qkv, grad_out, grad_up, grad_down)]
+    )
     bias_grads = (grad_query_bias, grad_value_bias, grad_out_bias, grad_up_bias, grad_down_bias)
     packed = jnp.concatenate([vector.reshape(mates, -1) for vector in bias_grads], axis=1)
     packed = lax.psum_scatter(packed, "fsdp", scatter_dimension=0, tiled=True)

time: 1170 us -> 1050 us (0.90)
  waiting for transfers between devices: 346 us -> 3.47 us
  Pallas kernels: 0 us -> 326 us
  local copies, waits for them, and re-layouts: 267 us -> 151 us
  starting transfers between devices: 11.8 us -> 29.4 us
  between operations: 16.6 us -> 2.78 us
    pallas_call x0 -> x2, Pallas kernels: none -> 326 us  [the longest x1 175 us: scatter_block(): pl.pallas_call(scatter_kernel, out_shape=[jax.ShapeDtypeStruct((SHARD, D)...]
    reduce_scatter x3 -> x0, waiting for transfers between devices: 146 us -> none  [scatter_matrix(): lax.psum_scatter(blocks, ('dp', 'fsdp'), scatter_dimension=0, tiled=True)]
    unnamed x11 -> x2, waiting for transfers between devices: 132 us -> 0.01 us
    reshape x11 -> x2, local copies, waits for them, and re-layouts: 148 us -> 25.7 us  [the longest x1 15.7 us: gather_block(): mixed, ups = (mixed.reshape(4, D, D), ups.reshape(4, D, D))]
    all_gather x4 -> x0, waiting for transfers between devices: 65 us -> none  [gather_matrix(): stacked = lax.all_gather(shard, ('dp', 'fsdp'), axis=0, tiled=False)]
    transpose x3 -> x0, local copies, waits for them, and re-layouts: 23 us -> none  [scatter_matrix(): blocks = blocks.transpose(0, 2, 1, 3).reshape(peers * mates * rows, columns)]
    slice x0 -> x4, local copies, waits for them, and re-layouts: none -> 16.4 us  [the longest x1 7.19 us: gather_block(): mixed[:, :, :own].transpose(1, 0, 2).reshape(D, 3 * D)]
    concatenate x0 -> x1, local copies, waits for them, and re-layouts: none -> 15.3 us  [scatter_block(): mixed = jnp.concatenate([columns(grad_qkv), columns(grad_out)], axis=2)]
  transfers between devices with their start and end apart: 12 -> 6, of which waited for: 5 -> 1; matrix products, arithmetic and copies ran while one was open for 35% -> 9% of each run, Pallas kernels for 0% -> 17%
where the time goes in v2:
time: 1050 us; the launch traced here: 1030 us
  Pallas kernels  326 us (31%)
  matrix products  307 us (29%)
  local copies, waits for them, and re-layouts  151 us (14%)
  blocking collectives  130 us (12%)
  other arithmetic  81.6 us (8%)
  starting transfers between devices  29.4 us (3%)
    pallas_call x1, Pallas kernels, scatter_block(): pl.pallas_call(scatter_kernel, out_shape=[jax.ShapeDtypeStruct((SHARD, D)...  175 us
    pallas_call x1, Pallas kernels, gather_block(): pl.pallas_call(gather_kernel, out_shape=[jax.ShapeDtypeStruct(shape + (SH...  150 us
    dot_general x4, matrix products, shards(): jnp.einsum('qhd,khd->hqk', grad_piece, values_all[:, heads_here], preferr...  43.9 us
    unnamed x2, blocking collectives  37.9 us
    all_gather x1, blocking collectives, shards(): cond_all = lax.all_gather(cond_act, ('dp', 'fsdp'), axis=0, tiled=True)  36.7 us
    unnamed x210, local copies, waits for them, and re-layouts  35.1 us
    convert_element_type x1, other arithmetic, shards(): grad_scores = (probs * (grad_probs - jnp.sum(probs * grad_probs, axis=-1,...  33.5 us
    dot_general x4, matrix products, attention_scores(): jnp.einsum('qhd,khd->hqk', query_part, key_part, preferred_element_type=j...  32.3 us
  transfers between devices with their start and end apart: 6, of which 1 were waited for; matrix products, arithmetic and copies ran while one was open for 9% of the time, Pallas kernels for 17%

profile of v2, /device:TPU:9, one launch (start us, length us, event | category | flops | bytes accessed | tf_op | source)
XLA Modules:
  0.0 1030.7 jit_solution(11658548149354684068)
XLA Ops:
  1.6 36.7 %all-gather.1 = bf16[32,3,1152]{2,1,0:T(4,128)(2,1)S(1)} all-gather(bf16[1,3,1152]{2,1,0:T(4,128)(2,1)S(1)} %fusion.123), channel_id=1, replica_groups=mesh['dp'=8,'fsdp'=4] {'dp','fsdp'}, dimensions={0}, use_global_device_ids=true | all-gather | bytes 228096 | tf_op jit(solution)/shard_map/all_gather | solution.py:493
  38.9 27.5 %fusion = f32[16,1728]{1,0:T(8,128)S(1)} fusion(f32[96,1728]{1,0:T(8,128)S(1)} %fusion.109), kind=kCustom, calls=%all-reduce-scatter | all-reduce-scatter fusion | flops 221185 | bytes 774656
  75.9 7.5 all-gather.2
  95.3 9.6 copy.147
  143.4 150.1 %shard_map.273 = (bf16[2,2,4,2,144,1152]{5,4,3,2,1,0:T(8,128)(2,1)}, bf16[2,2,4,2,144,1152]{5,4,3,2,1,0:T(8,128)(2,1)}, bf16[4,2,2,2,144,1152]{5,4,3,2,1,0:T(8,128)(2,1)}) custom-call(bf16[144,1152]{1,0:T(8,128)(2,1)} %pad_maximum_fusion.7.refs_0_, bf16[144,1152]{1,0:T(8,128)(2,1)} %refs_1_.1, bf16[144,1152]{1,0:T(8,128)(2,1)} %all_to_all.63.refs_2_), custom_call_target="tpu_custom_call" | custom-call | tf_op jit(solution)/shard_map/pallas_call | solution.py:180
  293.5 7.2 slice.181
  300.7 11.5 %copy.187 = bf16[4,1152,864]{1,2,0:T(8,128)(2,1)} copy(bf16[4,1152,864]{2,1,0:T(8,128)(2,1)} %slice.181) | data formatting | bytes 15925248
  312.3 11.0 %add_convert_fusion = bf16[768,3456]{1,0:T(8,128)(2,1)S(1)} fusion(bf16[768,1152]{1,0:T(8,128)(2,1)} %fusion.39, bf16[1152,3456]{0,1:T(8,128)(2,1)} %bitcast.251, f32[3456]{0:T(1024)S(1)} %pad_maximum_fusion.8), kind=kOutput, calls=%fused_computation.7 | convolution fusion | flops 6120603648 | bytes 15054336 | tf_op jit(solution)/shard_map/dot_general | solution.py:510
  360.0 15.4 %exponential_reduce_fusion.3 = (f32[4,768]{1,0:T(4,128)S(1)}, f32[4,768]{1,0:T(4,128)S(1)}, f32[4,768]{1,0:T(4,128)S(1)}, f32[4,768]{1,0:T(4,128)S(1)}, f32[4,768,768]{1,2,0:T(8,128)}) fusion(f32[4,768,768]{1,2,0:T(8,128)} %get-tuple-element.103, f32[4,768]{1,0:T(4,128)S(1)} %get-tuple-element.102, pred[768,768]{0,1:T(8,128)(4,1)S(1)} %broadcast_compare_fusion, ...), kind=kOutput, calls=%fused_computation.35 | convolution fusion | flops 370397184 | bytes 40611840 | tf_op jit(solution)/shard_map/qhd,khd->hqk/dot_general | solution.py:437
  375.5 9.8 exponential_reduce_fusion.2
  385.4 7.1 convolution_bitcast_fusion.3
  430.2 15.7 %copy.146 = bf16[4,1152,1152]{1,2,0:T(8,128)(2,1)} copy(bf16[4,1152,1152]{2,1,0:T(8,128)(2,1)} %bitcast.247) | data formatting | bytes 21233664 | tf_op jit(solution)/shard_map/reshape | solution.py:194
  446.0 16.9 %multiply_convert_fusion.4 = (bf16[512,4608]{1,0:T(8,128)(2,1)}, f32[512,4608]{1,0:T(8,128)}) fusion(f32[512,4608]{1,0:T(8,128)} %copy.147, f32[4608]{0:T(1024)S(1)} %reshape.325, bf16[512,1152]{1,0:T(8,128)(2,1)S(1)} %convolution_convert_fusion.7, bf16[1152,4608]{0,1:T(8,128)(2,1)} %bitcast.248), kind=kOutput, calls=%fused_computation.24 | convolution fusion | flops 5461770240 | bytes 35407872 | tf_op jit(solution)/shard_map/dot_general | solution.py:561
  462.9 22.7 %convert_reduce_fusion = (f32[4608]{0:T(1024)}, bf16[512,4608]{1,0:T(8,128)(2,1)}) fusion(f32[512,4608]{1,0:T(8,128)} %get-tuple-element.108, f32[4608]{0:T(1024)S(1)} %reshape.325, f32[512,4608]{1,0:T(8,128)} %copy.147, bf16[512,1152]{1,0:T(8,128)(2,1)S(1)} %copy-done.68, bf16[4608,1152]{1,0:T(8,128)(2,1)} %bitcast.305), kind=kOutput, calls=%fused_computation.15 | convolution fusion | flops 5492436480 | bytes 35426304 | tf_op jit(solution)/shard_map/bd,fd->bf/dot_general | solution.py:580
  485.5 18.1 %fusion.157 = (f32[768]{0:T(1024)S(1)}, f32[768]{0:T(1024)S(1)}, f32[768,1152]{1,0:T(8,128)}, f32[768,1152]{1,0:T(8,128)}) fusion(f32[768]{0:T(1024)S(1)} %add_rsqrt_fusion, f32[768,1152]{1,0:T(8,128)} %copy-done.2, f32[768]{0:T(1024)S(1)} %broadcast_multiply_fusion.4, f32[768,1152]{1,0:T(8,128)} %convolution_add_fusion.1, ...), kind=kOutput, calls=%fused_computation.238 | convolution fusion | flops 6348077056 | bytes 29506560 | tf_op jit(solution)/shard_map/tb,bd->td/dot_general | solution.py:588
  503.7 14.6 %fusion.64 = f32[768,1152]{1,0:T(8,128)} fusion(bf16[512,4608]{1,0:T(8,128)(2,1)} %get-tuple-element.107, bf16[4608,1152]{1,0:T(8,128)(2,1)} %bitcast.306, f32[1152]{0:T(1024)S(1)} %copy-done.61, s32[768]{0:T(1024)S(1)} %reduce.2), kind=kOutput, calls=%fused_computation.119 | convolution fusion | flops 6343360512 | bytes 18882048 | tf_op jit(solution)/shard_map/tb,bd->td/dot_general | solution.py:566
  518.3 10.6 %convert_reduce_fusion.2 = (f32[1152]{0:T(1024)}, bf16[768,1152]{1,0:T(8,128)(2,1)S(1)}, f32[768,1152]{1,0:T(8,128)}, bf16[1,768,1152]{2,1,0:T(8,128)(2,1)}) fusion(f32[768,1152]{1,0:T(8,128)} %get-tuple-element.105, f32[768]{0:T(1024)S(1)} %broadcast_multiply_fusion.2, f32[768,1152]{1,0:T(8,128)} %copy-done.2, f32[768]{0:T(1024)S(1)} %broadcast_multiply_fusion.4, ...), kind=kLoop, calls=%fused_computation.76 | loop fusion | flops 13269888 | bytes 26558976 | tf_op jit(solution)/shard_map/reduce_sum | solution.py:595
  557.6 28.6 %multiply_reduce_fusion.3 = (f32[4,768]{1,0:T(4,128)S(1)}, f32[4,768]{1,0:T(4,128)S(1)}, f32[4,768]{1,0:T(4,128)S(1)}, f32[4,768]{1,0:T(4,128)S(1)}, f32[4,768,768]{1,2,0:T(8,128)}) fusion(f32[4,768,768]{1,2,0:T(8,128)} %get-tuple-element.103, f32[4,768]{1,0:T(4,128)S(1)} %get-tuple-element.118, pred[768,768]{0,1:T(8,128)(4,1)S(1)} %broadcast_compare_fusion, ...), kind=kOutput, calls=%fused_computation.23 | convolution fusion | flops 386912256 | bytes 78397440 | tf_op jit(solution)/shard_map/qhd,khd->hqk/dot_general | solution.py:622
  586.2 33.5 %multiply_convert_fusion.3 = (bf16[4,768,768]{1,2,0:T(8,128)(2,1)}, bf16[4,768,768]{1,2,0:T(8,128)(2,1)}, bf16[4,768,768]{1,2,0:T(8,128)(2,1)}, bf16[4,768,768]{1,2,0:T(8,128)(2,1)}) fusion(f32[4,768,768]{1,2,0:T(8,128)} %get-tuple-element.109, f32[4,768,768]{1,2,0:T(8,128)} %get-tuple-element.103, f32[4,768]{1,0:T(4,128)S(1)} %get-tuple-element.68, ...), kind=kLoop, calls=%fused_computation.22 | loop fusion | flops 56623104 | bytes 95059968 | tf_op jit(solution)/shard_map/convert_element_type | solution.py:630
  654.4 8.4 convolution_convert_fusion
  662.9 9.4 convolution_convert_fusion.1
  675.6 11.4 %convolution_convert_fusion.2 = bf16[1152,3456]{1,0:T(8,128)(2,1)} fusion(bf16[768,1152]{1,0:T(8,128)(2,1)} %fusion.39, bf16[768,1152]{0,1:T(8,128)(2,1)} %bitcast.263, bf16[768,1152]{0,1:T(8,128)(2,1)} %bitcast.281, bf16[768,1152]{0,1:T(8,128)(2,1)S(1)} %bitcast.261), kind=kOutput, calls=%fused_computation.2 | convolution fusion | flops 6135201792 | bytes 15040512 | tf_op jit(solution)/shard_map/td,te->de/dot_general | solution.py:662
  687.1 14.1 %fusion.156 = (f32[768]{0:T(1024)S(1)}, f32[768]{0:T(1024)S(1)}, f32[768,1152]{1,0:T(8,128)}, f32[768,1152]{1,0:T(8,128)}) fusion(f32[768]{0:T(1024)S(1)} %copy-done.55, f32[768]{0:T(1024)S(1)} %copy-done.47, bf16[1,768,1152]{2,1,0:T(8,128)(2,1)S(1)} %copy-done.5, f32[768,1152]{1,0:T(8,128)S(1)} %copy-done.10, bf16[1152,3456]{0,1:T(8,128)(2,1)} %bitcast.252, ...), kind=kOutput, calls=%fused_computation.237 | convolution fusion | flops 6137411584 | bytes 25669632 | tf_op jit(solution)/shard_map/te,de->td/dot_general | solution.py:663
  701.2 11.5 %copy.164 = bf16[1152,3456]{0,1:T(8,128)(2,1)} copy(bf16[1152,3456]{1,0:T(8,128)(2,1)} %convolution_convert_fusion.2) | data formatting | bytes 15925248 | tf_op jit(solution)/shard_map/convert_element_type | solution.py:689
  713.1 10.4 %all-reduce.1 = f32[4,2304]{1,0:T(4,128)S(1)} all-reduce(f32[4,2304]{1,0:T(4,128)S(1)} %concatenate.47), channel_id=4, replica_groups=mesh['dp'=8,'fsdp'=4] {'fsdp'}, use_global_device_ids=true, to_apply=%region_29.30.clone | all-reduce | flops 9216 | bytes 73728
  724.2 25.3 %psum.7 = f32[2304]{0:T(1024)S(1)} all-reduce(f32[2304]{0:T(1024)S(1)} %dynamic-slice_reduce_fusion), channel_id=1, replica_groups=mesh['dp'=8,'fsdp'=4] {'dp'}, use_global_device_ids=true, to_apply=%region_30.31 | all-reduce | flops 2304 | bytes 18432 | tf_op jit(solution)/shard_map/psum | solution.py:694
  765.2 11.2 %all-to-all-start.2 = ((f32[3,4,1728]{2,0,1:T(4,128)}), f32[3,4,1728]{2,0,1:T(4,128)S(1)}, u32[]{:S(2)}, u32[]{:S(2)}) async-start(f32[3,4,1728]{2,0,1:T(4,128)} %copy.162), calls=%async_computation.2 | async-start | bytes 229376 | tf_op jit(solution)/shard_map/all_to_all | solution.py:678
  776.4 10.9 %pad_maximum_fusion = bf16[4,1152,1152]{1,2,0:T(8,128)(2,1)} fusion(bf16[4,1152,288]{1,2,0:T(8,128)(2,1)} %bitcast.280, bf16[4,1152,864]{1,2,0:T(8,128)(2,1)} %bitcast.234), kind=kLoop, calls=%fused_computation.6 | loop fusion | flops 21233664 | bytes 21233664 | tf_op jit(solution)/shard_map/concatenate | solution.py:384
  791.1 15.3 %copy.165 = bf16[4,1152,1152]{2,1,0:T(8,128)(2,1)} copy(bf16[4,1152,1152]{1,2,0:T(8,128)(2,1)} %pad_maximum_fusion) | data formatting | bytes 21233664 | tf_op jit(solution)/shard_map/concatenate | solution.py:384
  806.4 9.9 copy.200
  816.3 175.4 %shard_map.274 = (f32[144,1152]{1,0:T(8,128)}, f32[144,1152]{1,0:T(8,128)}, f32[144,1152]{1,0:T(8,128)}) custom-call(bf16[4,2,2,2,144,1152]{5,4,3,2,1,0:T(8,128)(2,1)} %bitcast.250, bf16[2,2,4,2,144,1152]{5,4,3,2,1,0:T(8,128)(2,1)} %bitcast.230, bf16[2,2,4,2,144,1152]{5,4,3,2,1,0:T(8,128)(2,1)} %bitcast.229), custom_call_target="tpu_custom_call" | custom-call | tf_op jit(solution)/shard_map/pallas_call | solution.py:391
  1002.6 22.6 %all-gather.3 = f32[8,12,1728]{2,1,0:T(8,128)S(1)} all-gather(f32[1,12,1728]{2,1,0:T(8,128)S(1)} %reshape.334), channel_id=1, replica_groups=mesh['dp'=8,'fsdp'=4] {'dp'}, dimensions={0}, use_global_device_ids=true | all-gather | bytes 746496 | tf_op jit(solution)/shard_map/all_gather | solution.py:681
  (344 shorter events, 237.7 us)
Async XLA Ops:
  0.6 37.8 %copy-start = (bf16[144,1728]{1,0:T(8,128)(2,1)S(1)}, bf16[144,1728]{1,0:T(8,128)(2,1)}, u32[]{:S(2)}) copy-start(bf16[144,1728]{1,0:T(8,128)(2,1)} %param.24) | copy-start | bytes 1492996
  0.7 84.5 %copy-start.4 = (bf16[1,768,1152]{2,1,0:T(8,128)(2,1)S(1)}, bf16[1,768,1152]{2,1,0:T(8,128)(2,1)}, u32[]{:S(2)}) copy-start(bf16[1,768,1152]{2,1,0:T(8,128)(2,1)} %param.18) | copy-start | bytes 5308420
  38.3 48.3 %copy-start.64 = (s32[1,3,16]{2,0,1:T(1,128)S(1)}, s32[1,3,16]{2,0,1:T(1,128)}, u32[]{:S(2)}) copy-start(s32[1,3,16]{2,0,1:T(1,128)} %param.21) | copy-start | bytes 580
  38.3 48.3 %copy-start.63 = (s32[1,768]{1,0:T(1,128)S(1)}, s32[1,768]{1,0:T(1,128)}, u32[]{:S(2)}) copy-start(s32[1,768]{1,0:T(1,128)} %param.23) | copy-start | bytes 9220
  38.3 48.3 %copy-start.65 = (s32[1,3,16]{2,0,1:T(1,128)S(1)}, s32[1,3,16]{2,0,1:T(1,128)}, u32[]{:S(2)}) copy-start(s32[1,3,16]{2,0,1:T(1,128)} %param.22) | copy-start | bytes 580
  38.5 49.0 %copy-start.35 = (bf16[96,1152]{1,0:T(8,128)(2,1)}, bf16[96,1152]{1,0:T(8,128)(2,1)S(1)}, u32[]{:S(2)}) copy-start(bf16[96,1152]{1,0:T(8,128)(2,1)S(1)} %reshape.331) | copy-start | bytes 663556
  38.5 49.0 %copy-start.45 = (bf16[144,864]{1,0:T(8,128)(2,1)S(1)}, bf16[144,864]{1,0:T(8,128)(2,1)}, u32[]{:S(2)}) copy-start(bf16[144,864]{1,0:T(8,128)(2,1)} %param.26) | copy-start | bytes 746500
  38.8 50.4 %copy-start.62 = (bf16[1728]{0:T(1024)(128)(2,1)S(1)}, bf16[1728]{0:T(1024)(128)(2,1)}, u32[]{:S(2)}) copy-start(bf16[1728]{0:T(1024)(128)(2,1)} %param.25) | copy-start | bytes 10372
  38.8 50.6 %copy-start.44 = (bf16[576,288]{0,1:T(8,128)(2,1)S(1)}, bf16[576,288]{0,1:T(8,128)(2,1)}, u32[]{:S(2)}) copy-start(bf16[576,288]{0,1:T(8,128)(2,1)} %param.33) | copy-start | bytes 995332
  66.4 41.1 %collective-permute-start = (f32[16,1728]{1,0:T(8,128)S(1)}, f32[16,1728]{1,0:T(8,128)}, u32[]{:S(2)}, u32[]{:S(2)}) collective-permute-start(f32[16,1728]{1,0:T(8,128)S(1)} %fusion), channel_id=1, source_target_pairs={{0,4},{4,8},{8,12},{12,16},{16,20},{20,24},{24,28},{1,5},{5,9},{9,... | collective-permute-start | bytes 331784
  69.0 38.5 %collective-permute-start.1 = (f32[12,1728]{1,0:T(8,128)}, f32[12,1728]{1,0:T(8,128)}, u32[]{:S(2)}, u32[]{:S(2)}) collective-permute-start(f32[12,1728]{1,0:T(8,128)} %slice.207), channel_id=1, source_target_pairs={{0,8},{4,12},{8,16},{12,20},{16,24},{20,28},{1,9},{5,13},{9,17},{1... | collective-permute-start | bytes 248840
  84.5 338.9 %copy-start.50 = (s32[3,1]{0,1:T(1,128)}, s32[3,1]{0,1:T(1,128)S(1)}, u32[]{:S(2)}) copy-start(s32[3,1]{0,1:T(1,128)S(1)} %reduce-window.4) | copy-start | bytes 40
  85.1 338.3 %copy-start.52 = (s32[3]{0:T(128)}, s32[3]{0:T(128)S(1)}, u32[]{:S(2)}) copy-start(s32[3]{0:T(128)S(1)} %fusion.129) | copy-start | bytes 40
  85.4 47.4 %copy-start.46 = (f32[768]{0:T(1024)}, f32[768]{0:T(1024)S(1)}, u32[]{:S(2)}) copy-start(f32[768]{0:T(1024)S(1)} %broadcast_multiply_fusion.5) | copy-start | bytes 9220
  89.3 43.6 %copy-start.54 = (f32[768]{0:T(1024)}, f32[768]{0:T(1024)S(1)}, u32[]{:S(2)}) copy-start(f32[768]{0:T(1024)S(1)} %add_rsqrt_fusion.1) | copy-start | bytes 9220
  110.3 6.9 all-to-all-start
  117.2 25.0 %all-to-all-start.1 = ((bf16[4,144,288]{2,1,0:T(8,128)(2,1)}), bf16[4,144,288]{2,1,0:T(8,128)(2,1)S(1)}, u32[]{:S(2)}, u32[]{:S(2)}) async-start(bf16[4,144,288]{2,1,0:T(8,128)(2,1)} %bitcast.9), calls=%async_computation.1 | async-start | bytes 884736 | tf_op jit(solution)/shard_map/all_to_all | solution.py:176
  360.0 15.4 %slice-start = ((s8[9437184]{0:T(1024)(128)(4,1)}), s8[4194304]{0:T(1024)(128)(4,1)S(1)}, s32[]{:S(2)}) async-start(s8[9437184]{0:T(1024)(128)(4,1)} %bitcast.219), calls=%async_computation.4 | async-start | bytes 8388608
  360.0 15.4 %slice-start.1 = ((s8[9437184]{0:T(1024)(128)(4,1)}), s8[4194304]{0:T(1024)(128)(4,1)S(1)}, s32[]{:S(2)}) async-start(s8[9437184]{0:T(1024)(128)(4,1)} %bitcast.219), calls=%async_computation.5 | async-start | bytes 8388608
  360.0 15.4 %slice-start.2 = ((s8[9437184]{0:T(1024)(128)(4,1)}), s8[1048576]{0:T(1024)(128)(4,1)S(1)}, s32[]{:S(2)}) async-start(s8[9437184]{0:T(1024)(128)(4,1)} %bitcast.219), calls=%async_computation.6 | async-start | bytes 2097152
  385.4 14.2 %slice-start.6 = ((s8[9437184]{0:T(1024)(128)(4,1)}), s8[4194304]{0:T(1024)(128)(4,1)S(1)}, s32[]{:S(2)}) async-start(s8[9437184]{0:T(1024)(128)(4,1)} %bitcast.223), calls=%async_computation.10 | async-start | bytes 8388608
  422.9 95.4 %copy-start.48 = (f32[768]{0:T(1024)}, f32[768]{0:T(1024)S(1)}, u32[]{:S(2)}) copy-start(f32[768]{0:T(1024)S(1)} %broadcast_multiply_fusion.4) | copy-start | bytes 9220
  426.2 92.2 %copy-start.56 = (f32[768]{0:T(1024)}, f32[768]{0:T(1024)S(1)}, u32[]{:S(2)}) copy-start(f32[768]{0:T(1024)S(1)} %add_rsqrt_fusion) | copy-start | bytes 9220
  430.2 15.8 %copy-start.70 = (bf16[512,1152]{1,0:T(8,128)(2,1)}, bf16[512,1152]{1,0:T(8,128)(2,1)S(1)}, u32[]{:S(2)}) copy-start(bf16[512,1152]{1,0:T(8,128)(2,1)S(1)} %convolution_convert_fusion.7) | copy-start | bytes 3538948
  445.9 16.9 %copy-start.68 = (bf16[512,1152]{1,0:T(8,128)(2,1)S(1)}, bf16[512,1152]{1,0:T(8,128)(2,1)}, u32[]{:S(2)}) copy-start(bf16[512,1152]{1,0:T(8,128)(2,1)} %get-tuple-element.114) | copy-start | bytes 3538948
  485.5 18.1 %copy-start.61 = (f32[1152]{0:T(1024)S(1)}, f32[1152]{0:T(1024)}, u32[]{:S(2)}) copy-start(f32[1152]{0:T(1024)} %reshape.326) | copy-start | bytes 13828
  503.7 14.7 %copy-start.21 = (bf16[1,768,1152]{2,1,0:T(8,128)(2,1)S(1)}, bf16[1,768,1152]{2,1,0:T(8,128)(2,1)}, u32[]{:S(2)}) copy-start(bf16[1,768,1152]{2,1,0:T(8,128)(2,1)} %param.35) | copy-start | bytes 5308420
  701.1 48.4 %copy-start.51 = (s32[3,1]{0,1:T(1,128)S(1)}, s32[3,1]{0,1:T(1,128)}, u32[]{:S(2)}) copy-start(s32[3,1]{0,1:T(1,128)} %copy-done.50) | copy-start | bytes 40
  701.1 48.4 %copy-start.53 = (s32[3]{0:T(128)S(1)}, s32[3]{0:T(128)}, u32[]{:S(2)}) copy-start(s32[3]{0:T(128)} %copy-done.52) | copy-start | bytes 40
  765.2 232.8 %all-to-all-start.2 = ((f32[3,4,1728]{2,0,1:T(4,128)}), f32[3,4,1728]{2,0,1:T(4,128)S(1)}, u32[]{:S(2)}, u32[]{:S(2)}) async-start(f32[3,4,1728]{2,0,1:T(4,128)} %copy.162), calls=%async_computation.2 | async-start | bytes 229376 | tf_op jit(solution)/shard_map/all_to_all | solution.py:678
  998.0 30.5 %all-to-all-start.3 = ((f32[144,4,288]{2,0,1:T(8,128)}), f32[144,4,288]{2,0,1:T(8,128)S(1)}, u32[]{:S(2)}, u32[]{:S(2)}) async-start(f32[144,4,288]{2,0,1:T(8,128)} %copy.166), calls=%async_computation.3 | async-start | bytes 1769472 | tf_op jit(solution)/shard_map/all_to_all | solution.py:405
  1002.6 28.0 %copy-start.1 = (bf16[144,1728]{1,0:T(8,128)(2,1)S(1)}, bf16[144,1728]{1,0:T(8,128)(2,1)}, u32[]{:S(2)}) copy-start(bf16[144,1728]{1,0:T(8,128)(2,1)} %param.24) | copy-start | bytes 1492996
  (72 other events, 441.6 us)

commit v3 on v2

--- a/solution.py
+++ b/solution.py
@@ -1,4 +1,4 @@
-import functools
+import math
 
 import jax
 import jax.numpy as jnp
@@ -17,6 +17,485 @@
 
 highest = lax.Precision.HIGHEST
 epsilon = 1e-06
+
+
+NT = (((1,), (1,)), ((), ()))
+TN = (((0,), (0,)), ((), ()))
+NN = (((1,), (0,)), ((), ()))
+PLACES = 512
+BLOCK = 256
+BF16, F32 = jnp.bfloat16, jnp.float32
+SOFT = HEAD_DIM**-0.5 * math.log2(math.e)
+QKV_SHARD, OUT_SHARD, PAD_SHARD = 864, 288, 896
+VMEM_BYTES = 60 * 2**20
+
+
+def dot(left, right, dims=NN):
+    return lax.dot_general(left, right, dims, preferred_element_type=F32)
+
+
+def rows_at(i):
+    return pl.ds(pl.multiple_of(i * BLOCK, BLOCK), BLOCK)
+
+
+def per_crop(table, segment):
+    return jnp.where(
+        segment == 0, table[0:1], jnp.where(segment == 1, table[1:2], table[2:3])
+    )
+
+
+def normalise(values):
+    center = values - jnp.mean(values, axis=1, keepdims=True)
+    variance = jnp.mean(center * center, axis=1, keepdims=True)
+    inverse = lax.rsqrt(variance + epsilon)
+    return center * inverse, inverse
+
+
+def crop_sums(segment, values):
+    lanes = lax.broadcasted_iota(jnp.int32, (values.shape[0], 128), 1)
+    member = (lanes == segment).astype(BF16)
+    high = values.astype(BF16)
+    low = (values - high.astype(F32)).astype(BF16)
+    return (dot(member, high, TN) + dot(member, low, TN))[:8]
+
+
+def crop_mask(bias_ref, column_ref, row_ref):
+    for i in range(TOK_DEV // BLOCK):
+        here = pl.ds(i * BLOCK, BLOCK)
+        bias_ref[here, :] = jnp.where(column_ref[here, :] == row_ref[...], 0.0, -1e30).astype(F32)
+
+
+def places_of(slot_row, i):
+    place = lax.broadcasted_iota(jnp.int32, (BLOCK, TOK_DEV), 0) + i * BLOCK
+    return (place == slot_row).astype(BF16)
+
+
+def tokens_of(slot_column):
+    place = lax.broadcasted_iota(jnp.int32, (BLOCK, PLACES), 1)
+    return (place == slot_column).astype(BF16)
+
+
+def head_keep(mask_ref, h, segment):
+    return jnp.where(
+        segment == 0, mask_ref[h, 0], jnp.where(segment == 1, mask_ref[h, 1], mask_ref[h, 2])
+    )
+
+
+def attend_kernel(
+    x_ref, weight_ref, mods_ref, qkv_bias_ref, out_bias_ref, column_ref, row_ref, slot_ref,
+    groups_ref, mask_ref,
+    first_ref, heads_ref, mixed_ref, lse_ref, attn_ref, after_ref, arrived_ref, picked_ref, out_weight_ref,
+    bias_ref, parts_ref, second_ref,
+):
+    crop_mask(bias_ref, column_ref, row_ref)
+
+    def norm(i, carry):
+        here = rows_at(i)
+        segment = column_ref[here, :]
+        normed, _ = normalise(x_ref[here, :].astype(F32))
+        shift, scale = per_crop(mods_ref[0], segment), per_crop(mods_ref[1], segment)
+        first_ref[here, :] = (normed * (1.0 + scale) + shift).astype(BF16)
+        return carry
+
+    lax.fori_loop(0, 3, norm, 0)
+    for j in range(4):
+        out_weight_ref[:, OUT_SHARD * j : OUT_SHARD * (j + 1)] = weight_ref[j, :, QKV_SHARD:]
+
+    def project(i, carry):
+        j = lax.div(i, 3)
+        here = rows_at(lax.rem(i, 3))
+        triple = (dot(first_ref[here, :], weight_ref[j, :, :PAD_SHARD]) + qkv_bias_ref[j]).astype(BF16)
+        zero = jnp.zeros((BLOCK, 128 - HEAD_DIM), BF16)
+        for h in range(12):
+            part = triple[:, HEAD_DIM * h : HEAD_DIM * (h + 1)]
+            heads_ref[12 * j + h, here, :] = jnp.concatenate([part, zero], axis=1)
+        return carry
+
+    lax.fori_loop(0, 12, project, 0)
+
+    def head(h, carry):
+        keys, values = heads_ref[16 + h], heads_ref[32 + h]
+        for i in range(3):
+            here = pl.ds(i * BLOCK, BLOCK)
+            scores = dot(heads_ref[h, here, :], keys, NT) * SOFT + bias_ref[here, :]
+            top = jnp.max(scores, axis=1, keepdims=True)
+            weights = jnp.exp2(scores - top)
+            total = jnp.sum(weights, axis=1, keepdims=True)
+            keep = head_keep(mask_ref, h, column_ref[here, :])
+            parts_ref[h, here, :] = (dot(weights.astype(BF16), values) * (keep / total)).astype(BF16)
+            spread = jnp.broadcast_to(top + jnp.log2(total), (BLOCK, 128))
+            lse_ref[h, :, here] = jnp.transpose(spread)[:1, :]
+        return carry
+
+    lax.fori_loop(0, HEADS, head, 0)
+    for h in range(HEADS):
+        mixed_ref[:, HEAD_DIM * h : HEAD_DIM * (h + 1)] = parts_ref[h][:, :HEAD_DIM]
+
+    def close(i, carry):
+        here = rows_at(i)
+        segment = column_ref[here, :]
+        attn = dot(mixed_ref[here, :], out_weight_ref[...]) + out_bias_ref[...]
+        attn_ref[here, :] = attn
+        after = x_ref[here, :].astype(F32) + per_crop(mods_ref[2], segment) * attn
+        after_ref[here, :] = after
+        normed, _ = normalise(after)
+        shift, scale = per_crop(mods_ref[3], segment), per_crop(mods_ref[4], segment)
+        second_ref[here, :] = (normed * (1.0 + scale) + shift).astype(BF16)
+        return carry
+
+    lax.fori_loop(0, 3, close, 0)
+    for i in range(2):
+        here = pl.ds(i * BLOCK, BLOCK)
+        choice = places_of(slot_ref[...], i)
+        arrived_ref[here, :] = dot(choice, second_ref[...]).astype(BF16)
+        picked_ref[here, :] = dot(choice, groups_ref[...]).astype(BF16)
+
+
+def shape_of(*shape, dtype=BF16):
+    return jax.ShapeDtypeStruct(shape, dtype)
+
+
+IN_VMEM = pl.BlockSpec(memory_space=pltpu.VMEM)
+IN_SMEM = pl.BlockSpec(memory_space=pltpu.SMEM)
+ANYWHERE = pl.BlockSpec(memory_space=pl.ANY)
+
+
+def attend(x, weight, mods, qkv_bias, out_bias, column, row, slot_row, groups, mask):
+    return pl.pallas_call(
+        attend_kernel,
+        out_shape=[
+            shape_of(TOK_DEV, D),
+            shape_of(3 * HEADS, TOK_DEV, 128),
+            shape_of(TOK_DEV, D),
+            shape_of(HEADS, 1, TOK_DEV, dtype=F32),
+            shape_of(TOK_DEV, D, dtype=F32),
+            shape_of(TOK_DEV, D, dtype=F32),
+            shape_of(PLACES, D),
+            shape_of(PLACES, 128),
+            shape_of(D, D),
+        ],
+        in_specs=[IN_VMEM] * 9 + [IN_SMEM],
+        out_specs=[IN_VMEM] * 9,
+        scratch_shapes=[
+            pltpu.VMEM((TOK_DEV, TOK_DEV), F32),
+            pltpu.VMEM((HEADS, TOK_DEV, 128), BF16),
+            pltpu.VMEM((TOK_DEV, D), BF16),
+        ],
+        compiler_params=pltpu.CompilerParams(vmem_limit_bytes=VMEM_BYTES),
+    )(x, weight, mods, qkv_bias, out_bias, column, row, slot_row, groups, mask)
+
+
+ROOT = math.sqrt(2.0 / math.pi)
+
+
+def feed_kernel(
+    up_ref, down_ref, arrived_ref, picked_ref, up_bias_ref, down_bias_ref, cot_ref, after_ref,
+    mods_ref, column_ref, slot_column_ref, slot_row_ref,
+    pull_ref, grad_down_ref, grad_rows_ref, block_out_ref, gate_ref, bias_ref,
+    active_ref, total_ref, branch_ref,
+):
+    step = pl.program_id(0)
+
+    @pl.when(step == 0)
+    def _():
+        for i in range(3):
+            here = pl.ds(i * BLOCK, BLOCK)
+            gate = per_crop(mods_ref[5], column_ref[here, :])
+            block_out_ref[here, :] = (gate * cot_ref[here, :].astype(F32)).astype(BF16)
+        for i in range(2):
+            here = pl.ds(i * BLOCK, BLOCK)
+            choice = places_of(slot_row_ref[...], i)
+            grad_rows_ref[here, :] = dot(choice, block_out_ref[...]).astype(BF16)
+        bias_ref[...] = jnp.sum(grad_rows_ref[...].astype(F32), axis=0, keepdims=True)
+        total_ref[...] = jnp.zeros_like(total_ref)
+
+    @pl.when(step < 4)
+    def _():
+        group = lax.broadcasted_iota(jnp.int32, (128, D), 0) - 4 * step
+        unit = lax.broadcasted_iota(jnp.int32, (128, D), 1)
+        width = FF // GROUPS
+        spread = ((unit >= group * width) & (unit < (group + 1) * width)).astype(BF16)
+        for i in range(2):
+            here = pl.ds(i * BLOCK, BLOCK)
+            hidden = dot(arrived_ref[here, :], up_ref[0]) + up_bias_ref[0]
+            keep = dot(picked_ref[here, :], spread)
+            square = hidden * hidden
+            curve = jnp.tanh(ROOT * hidden * (1.0 + 0.044715 * square))
+            half = 0.5 * (1.0 + curve)
+            slope = half + 0.5 * hidden * (1.0 - curve * curve) * (
+                ROOT * (1.0 + 3.0 * 0.044715 * square)
+            )
+            active_ref[step, here, :] = (hidden * half * keep).astype(BF16)
+            pull_ref[0, here, :] = (slope * keep).astype(BF16)
+
+        def grad(i, carry):
+            here = pl.ds(pl.multiple_of(i * 384, 384), 384)
+            grad_down_ref[0, here, :] = dot(active_ref[step, :, here], grad_rows_ref[...], TN).astype(BF16)
+            return carry
+
+        lax.fori_loop(0, 3, grad, 0)
+
+    @pl.when(step >= 4)
+    def _():
+        for i in range(2):
+            here = pl.ds(i * BLOCK, BLOCK)
+            total_ref[here, :] += dot(active_ref[step - 4, here, :], down_ref[0])
+
+    @pl.when(step == 7)
+    def _():
+        branch_ref[...] = (total_ref[...] + down_bias_ref[...]).astype(BF16)
+        gates = jnp.zeros((8, D), F32)
+        for i in range(3):
+            here = pl.ds(i * BLOCK, BLOCK)
+            segment = column_ref[here, :]
+            branch = dot(tokens_of(slot_column_ref[here, :]), branch_ref[...])
+            gate = per_crop(mods_ref[5], segment)
+            block_out_ref[here, :] = (after_ref[here, :] + gate * branch).astype(BF16)
+            gates = gates + crop_sums(segment, cot_ref[here, :].astype(F32) * branch)
+        gate_ref[...] = gates
+
+
+def whole(*shape):
+    return pl.BlockSpec(shape, lambda i: (0,) * len(shape))
+
+
+def feed(up, down, arrived, picked, up_bias, down_bias, cot, after, mods, column, slot_column, slot_row):
+    early = lambda *tail: pl.BlockSpec((1, *tail), lambda i: (jnp.minimum(i, 3), 0, 0))
+    late = lambda *tail: pl.BlockSpec((1, *tail), lambda i: (jnp.maximum(i - 4, 0), 0, 0))
+    return pl.pallas_call(
+        feed_kernel,
+        grid=(8,),
+        out_shape=[
+            shape_of(4, PLACES, D),
+            shape_of(4, D, D),
+            shape_of(PLACES, D),
+            shape_of(TOK_DEV, D),
+            shape_of(8, D, dtype=F32),
+            shape_of(1, D, dtype=F32),
+        ],
+        in_specs=[
+            early(D, D), late(D, D), whole(PLACES, D), whole(PLACES, 128), early(1, D), whole(1, D),
+            whole(TOK_DEV, D), whole(TOK_DEV, D), whole(6, 8, D), whole(TOK_DEV, 1), whole(TOK_DEV, 1),
+            whole(1, TOK_DEV),
+        ],
+        out_specs=[
+            early(PLACES, D), early(D, D), whole(PLACES, D), whole(TOK_DEV, D), whole(8, D), whole(1, D),
+        ],
+        scratch_shapes=[
+            pltpu.VMEM((4, PLACES, D), BF16),
+            pltpu.VMEM((PLACES, D), F32),
+            pltpu.VMEM((PLACES, D), BF16),
+        ],
+        compiler_params=pltpu.CompilerParams(vmem_limit_bytes=VMEM_BYTES),
+    )(up, down, arrived, picked, up_bias, down_bias, cot, after, mods, column, slot_column, slot_row)
+
+
+def unfeed_kernel(
+    down_ref, up_ref, pull_ref, grad_rows_ref, arrived_ref, after_ref, cot_ref, attn_ref, mods_ref,
+    column_ref, slot_column_ref,
+    grad_up_ref, up_bias_ref, mid_ref, grad_attn_ref, grad_split_ref, sums_ref, out_bias_ref,
+    hidden_ref, total_ref, back_ref,
+):
+    step = pl.program_id(0)
+
+    @pl.when(step == 0)
+    def _():
+        total_ref[...] = jnp.zeros_like(total_ref)
+
+    bias = jnp.zeros((1, D), F32)
+    for i in range(2):
+        here = pl.ds(i * BLOCK, BLOCK)
+        grad = dot(grad_rows_ref[here, :], down_ref[0], NT) * pull_ref[0, here, :].astype(F32)
+        low = grad.astype(BF16)
+        hidden_ref[here, :] = low
+        bias = bias + jnp.sum(low.astype(F32), axis=0, keepdims=True)
+        total_ref[here, :] += dot(low, up_ref[0], NT)
+    up_bias_ref[0] = bias
+
+    def grad_of(i, carry):
+        here = pl.ds(pl.multiple_of(i * 384, 384), 384)
+        grad_up_ref[0, here, :] = dot(arrived_ref[:, here], hidden_ref[...], TN).astype(BF16)
+        return carry
+
+    lax.fori_loop(0, 3, grad_of, 0)
+
+    @pl.when(step == 3)
+    def _():
+        back_ref[...] = total_ref[...].astype(BF16)
+        shifts, scales = jnp.zeros((8, D), F32), jnp.zeros((8, D), F32)
+        gates, out_bias = jnp.zeros((8, D), F32), jnp.zeros((1, D), F32)
+        for i in range(3):
+            here = pl.ds(i * BLOCK, BLOCK)
+            segment = column_ref[here, :]
+            second = dot(tokens_of(slot_column_ref[here, :]), back_ref[...])
+            normed, inverse = normalise(after_ref[here, :])
+            grad = second * (1.0 + per_crop(mods_ref[4], segment))
+            mean = jnp.mean(grad, axis=1, keepdims=True)
+            slant = jnp.mean(grad * normed, axis=1, keepdims=True)
+            mid = cot_ref[here, :].astype(F32) + inverse * (grad - mean - normed * slant)
+            mid_ref[here, :] = mid
+            low = (per_crop(mods_ref[2], segment) * mid).astype(BF16)
+            grad_attn_ref[here, :] = low
+            for j in range(4):
+                grad_split_ref[j, here, :] = low[:, OUT_SHARD * j : OUT_SHARD * (j + 1)]
+            out_bias = out_bias + jnp.sum(low.astype(F32), axis=0, keepdims=True)
+            shifts = shifts + crop_sums(segment, second)
+            scales = scales + crop_sums(segment, second * normed)
+            gates = gates + crop_sums(segment, mid * attn_ref[here, :])
+        sums_ref[0], sums_ref[1], sums_ref[2] = gates, shifts, scales
+        out_bias_ref[...] = out_bias
+
+
+def unfeed(down, up, pull, grad_rows, arrived, after, cot, attn, mods, column, slot_column):
+    block = lambda *tail: pl.BlockSpec((1, *tail), lambda i: (i, 0, 0))
+    return pl.pallas_call(
+        unfeed_kernel,
+        grid=(4,),
+        out_shape=[
+            shape_of(4, D, D),
+            shape_of(4, 1, D, dtype=F32),
+            shape_of(TOK_DEV, D, dtype=F32),
+            shape_of(TOK_DEV, D),
+            shape_of(4, TOK_DEV, OUT_SHARD),
+            shape_of(3, 8, D, dtype=F32),
+            shape_of(1, D, dtype=F32),
+        ],
+        in_specs=[
+            block(D, D), block(D, D), block(PLACES, D), whole(PLACES, D), whole(PLACES, D),
+            whole(TOK_DEV, D), whole(TOK_DEV, D), whole(TOK_DEV, D), whole(6, 8, D), whole(TOK_DEV, 1),
+            whole(TOK_DEV, 1),
+        ],
+        out_specs=[
+            block(D, D), block(1, D), whole(TOK_DEV, D), whole(TOK_DEV, D), whole(4, TOK_DEV, OUT_SHARD),
+            whole(3, 8, D), whole(1, D),
+        ],
+        scratch_shapes=[
+            pltpu.VMEM((PLACES, D), BF16),
+            pltpu.VMEM((PLACES, D), F32),
+            pltpu.VMEM((PLACES, D), BF16),
+        ],
+        compiler_params=pltpu.CompilerParams(vmem_limit_bytes=VMEM_BYTES),
+    )(down, up, pull, grad_rows, arrived, after, cot, attn, mods, column, slot_column)
+
+
+def unattend_kernel(
+    grad_ref, out_weight_ref, heads_ref, lse_ref, column_ref, row_ref, mask_ref,
+    triple_ref, sums_ref,
+    bias_ref, mixed_ref, grads_ref, key_ref, value_ref,
+):
+    crop_mask(bias_ref, column_ref, row_ref)
+
+    def spread(i, carry):
+        here = rows_at(i)
+        segment = column_ref[here, :]
+        mixed = dot(grad_ref[here, :], out_weight_ref[...], NT)
+        zero = jnp.zeros((BLOCK, 128 - HEAD_DIM), BF16)
+        for h in range(HEADS):
+            part = mixed[:, HEAD_DIM * h : HEAD_DIM * (h + 1)] * head_keep(mask_ref, h, segment)
+            mixed_ref[h, here, :] = jnp.concatenate([part.astype(BF16), zero], axis=1)
+        return carry
+
+    lax.fori_loop(0, 3, spread, 0)
+    factor = HEAD_DIM**-0.5
+
+    def head(h, carry):
+        keys, values = heads_ref[16 + h], heads_ref[32 + h]
+        turned = jnp.transpose(keys)
+        for i in range(3):
+            here = pl.ds(i * BLOCK, BLOCK)
+            queries, grads = heads_ref[h, here, :], mixed_ref[h, here, :]
+            scores = dot(keys, queries, NT) * SOFT + bias_ref[:, here]
+            probs = jnp.exp2(scores - lse_ref[h, :, here])
+            product = probs * dot(values, grads, NT)
+            total = jnp.sum(product, axis=0, keepdims=True)
+            low = (product - probs * total).astype(BF16)
+            for_values, for_keys = dot(probs.astype(BF16), grads), dot(low, queries)
+            if i == 0:
+                value_ref[...], key_ref[...] = for_values, for_keys
+            else:
+                value_ref[...] += for_values
+                key_ref[...] += for_keys
+            grads_ref[h, here, :] = jnp.transpose(dot(turned, low) * factor).astype(BF16)
+        grads_ref[16 + h] = (key_ref[...] * factor).astype(BF16)
+        grads_ref[32 + h] = value_ref[...].astype(BF16)
+        return carry
+
+    lax.fori_loop(0, HEADS, head, 0)
+    for j in range(4):
+        triple_ref[j, :, QKV_SHARD:] = jnp.zeros((TOK_DEV, PAD_SHARD - QKV_SHARD), BF16)
+        for h in range(12):
+            triple_ref[j, :, HEAD_DIM * h : HEAD_DIM * (h + 1)] = grads_ref[12 * j + h][:, :HEAD_DIM]
+        sums_ref[j] = jnp.sum(triple_ref[j].astype(F32), axis=0, keepdims=True)
+
+
+def unattend(grad_attn, out_weight, heads, lse, column, row, mask):
+    return pl.pallas_call(
+        unattend_kernel,
+        out_shape=[shape_of(4, TOK_DEV, PAD_SHARD), shape_of(4, 1, PAD_SHARD, dtype=F32)],
+        in_specs=[IN_VMEM] * 6 + [IN_SMEM],
+        out_specs=[IN_VMEM] * 2,
+        scratch_shapes=[
+            pltpu.VMEM((TOK_DEV, TOK_DEV), F32),
+            pltpu.VMEM((HEADS, TOK_DEV, 128), BF16),
+            pltpu.VMEM((3 * HEADS, TOK_DEV, 128), BF16),
+            pltpu.VMEM((TOK_DEV, 128), F32),
+            pltpu.VMEM((TOK_DEV, 128), F32),
+        ],
+        compiler_params=pltpu.CompilerParams(vmem_limit_bytes=VMEM_BYTES),
+    )(grad_attn, out_weight, heads, lse, column, row, mask)
+
+
+def unproject_kernel(
+    weight_ref, triple_ref, split_ref, first_ref, mixed_ref, x_ref, mid_ref, mods_ref, column_ref,
+    grad_ref, grad_in_ref, sums_ref,
+    total_ref,
+):
+    step = pl.program_id(0)
+
+    def grad(i, carry):
+        here = pl.ds(pl.multiple_of(i * 384, 384), 384)
+        part = dot(first_ref[:, here], triple_ref[0], TN).astype(BF16)
+        grad_ref[0, here, :PAD_SHARD] = part
+        grad_ref[0, here, QKV_SHARD:] = dot(mixed_ref[:, here], split_ref[0], TN).astype(BF16)
+        return carry
+
+    lax.fori_loop(0, 3, grad, 0)
+    for i in range(3):
+        here = pl.ds(i * BLOCK, BLOCK)
+        part = dot(triple_ref[0, here, :], weight_ref[0, :, :PAD_SHARD], NT)
+        total_ref[here, :] = jnp.where(step == 0, part, total_ref[here, :] + part)
+
+    @pl.when(step == 3)
+    def _():
+        shifts, scales = jnp.zeros((8, D), F32), jnp.zeros((8, D), F32)
+        for i in range(3):
+            here = pl.ds(i * BLOCK, BLOCK)
+            segment = column_ref[here, :]
+            first = total_ref[here, :]
+            normed, inverse = normalise(x_ref[here, :].astype(F32))
+            grads = first * (1.0 + per_crop(mods_ref[1], segment))
+            mean = jnp.mean(grads, axis=1, keepdims=True)
+            slant = jnp.mean(grads * normed, axis=1, keepdims=True)
+            grad_in_ref[here, :] = mid_ref[here, :] + inverse * (grads - mean - normed * slant)
+            shifts = shifts + crop_sums(segment, first)
+            scales = scales + crop_sums(segment, first * normed)
+        sums_ref[0], sums_ref[1] = shifts, scales
+
+
+def unproject(weight, triple, split, first, mixed, x, mid, mods, column):
+    block = lambda *tail: pl.BlockSpec((1, *tail), lambda i: (i, 0, 0))
+    return pl.pallas_call(
+        unproject_kernel,
+        grid=(4,),
+        out_shape=[shape_of(4, D, D), shape_of(TOK_DEV, D, dtype=F32), shape_of(2, 8, D, dtype=F32)],
+        in_specs=[
+            block(D, D), block(TOK_DEV, PAD_SHARD), block(TOK_DEV, OUT_SHARD), whole(TOK_DEV, D),
+            whole(TOK_DEV, D), whole(TOK_DEV, D), whole(TOK_DEV, D), whole(6, 8, D), whole(TOK_DEV, 1),
+        ],
+        out_specs=[block(D, D), whole(TOK_DEV, D), whole(2, 8, D)],
+        scratch_shapes=[pltpu.VMEM((TOK_DEV, D), F32)],
+        compiler_params=pltpu.CompilerParams(vmem_limit_bytes=VMEM_BYTES),
+    )(weight, triple, split, first, mixed, x, mid, mods, column)
 
 
 MESH = pl.DeviceIdType.MESH
@@ -31,6 +510,18 @@
         self.y, self.c = lax.div(fsdp, 2), lax.rem(fsdp, 2)
         z = self.z
         self.zs = (z, z + 1 - 2 * lax.rem(z, 2), lax.rem(z + 2, 4), 3 - z)
+        self.mates = (
+            self.device(c=1 - self.c),
+            self.device(y=1 - self.y),
+            self.device(y=1 - self.y, c=1 - self.c),
+        )
+        self.mate_index = (
+            2 * self.y + 1 - self.c,
+            2 * (1 - self.y) + self.c,
+            2 * (1 - self.y) + 1 - self.c,
+        )
+        self.index = 2 * self.y + self.c
+        self.peer = 2 * z + self.x
 
     def device(self, z=None, x=None, y=None, c=None):
         z, x = self.z if z is None else z, self.x if x is None else x
@@ -40,7 +531,8 @@
     def meet(self):
         barrier = pltpu.get_barrier_semaphore()
         others = [self.device(z=self.zs[k]) for k in (1, 2, 3)]
-        others += [self.device(x=1 - self.x), self.device(y=1 - self.y), self.device(c=1 - self.c)]
+        others += [self.device(z=self.zs[k], x=1 - self.x) for k in range(4)]
+        others += self.mates
         for other in others:
             pl.semaphore_signal(barrier, inc=1, device_id=other, device_id_type=MESH)
         pl.semaphore_wait(barrier, len(others))
@@ -131,12 +623,19 @@
         for copy in self.copies.made:
             copy.wait_send()
 
-
-def gather_kernel(*refs):
-    sources, targets = refs[:3], refs[3:6]
-    send_sems, recv_sems, local_sems = refs[6:]
+CROPS = 3
+
+
+def gather_kernel(
+    mixed_ref, up_ref, down_ref, cond_ref, ada_ref, ada_bias_ref, bias_ref,
+    mixed_out, up_out, down_out, mods_ref, biases_ref, conds_ref,
+    send_sems, recv_sems, local_sems, small_send, small_recv, local_small,
+    all_cond, own_cond, partial_ref, from_x, from_z, column_ref,
+):
+    sources, targets = (mixed_ref, up_ref, down_ref), (mixed_out, up_out, down_out)
     place = Place()
     place.meet()
+    x, zs = place.x, place.zs
 
     def slot_of(r):
         if r == 2:
@@ -145,71 +644,127 @@
 
     rounds = [
         Gather(
-            place,
-            sources[r],
-            slot_of(r),
-            send_sems.at[r],
-            recv_sems.at[r],
-            local_sems.at[r],
-            r % 2 == 1,
+            place, sources[r], slot_of(r), send_sems.at[r], recv_sems.at[r], local_sems.at[r], r % 2 == 1
         )
         for r in range(3)
     ]
+    small = Copies(small_send, small_recv)
+    to_mates = [small.make(cond_ref, all_cond.at[place.index], mate) for mate in place.mates]
+    to_mates += [small.make(bias_ref, biases_ref.at[place.index], mate) for mate in place.mates]
+    others = [(k, far) for k in range(4) for far in (0, 1) if k or far]
+    to_peers = []
+    for k, far in others:
+        there = 1 - x if far else x
+        to_peers.append(
+            small.make(
+                own_cond.at[2 * zs[k] + there],
+                conds_ref.at[place.peer],
+                place.device(z=zs[k], x=there),
+            )
+        )
+    over_x = [
+        small.make(partial_ref.at[2 * zs[k] + 1 - x], from_x.at[k], place.device(x=1 - x))
+        for k in range(4)
+    ]
+    along = [
+        small.make(partial_ref.at[2 * zs[k] + x], from_z.at[k - 1], place.device(z=zs[k]))
+        for k in (1, 2, 3)
+    ]
+    finals = [
+        small.make(column_ref.at[other], mods_ref.at[place.index], mate)
+        for other, mate in zip(place.mate_index, place.mates)
+    ]
+    own_bias = pltpu.make_async_copy(bias_ref, biases_ref.at[place.index], local_small.at[0])
+
+    for copy in to_mates:
+        copy.start()
+    own_bias.start()
     rounds[0].start()
+    all_cond[place.index] = cond_ref[...]
+    own_cond[...] = jnp.zeros_like(own_cond)
+    for copy in to_mates:
+        copy.wait_recv()
+    for j in range(4):
+        own_cond[:, CROPS * j : CROPS * (j + 1), :] = all_cond[j, :, :CROPS, :]
+    for copy in to_peers:
+        copy.start()
+    conds_ref[place.peer] = own_cond[place.peer]
+    rounds[0].pass_along(1)
+    for copy in to_peers:
+        copy.wait_recv()
+    for i in range(8):
+        partial_ref[i] = dot(conds_ref[i][:, :SHARD].astype(BF16), ada_ref[...])
+    for copy in over_x:
+        copy.start()
+    rounds[0].pass_along(2)
+    rounds[0].pass_along(3)
+    for k in range(4):
+        over_x[k].wait_recv()
+        partial_ref[2 * zs[k] + x] += from_x[k]
+    for copy in along:
+        copy.start()
+    rounds[1].start()
+    for k in range(2):
+        rounds[0].pass_across(k)
+    for copy in along:
+        copy.wait_recv()
+    total = partial_ref[place.peer] + from_z[0] + from_z[1] + from_z[2] + ada_bias_ref[...]
+    column_ref[...] = jnp.zeros_like(column_ref)
+    for j in range(4):
+        column_ref[j, :CROPS, :] = total[CROPS * j : CROPS * (j + 1)]
+    for copy in finals:
+        copy.start()
+    mods_ref[place.index] = column_ref[place.index]
+    for k in range(2, 4):
+        rounds[0].pass_across(k)
     for k in (1, 2, 3):
-        rounds[0].pass_along(k)
-    for r in range(3):
-        if r < 2:
-            rounds[r + 1].start()
-        for k in range(4):
-            rounds[r].pass_across(k)
-        if r < 2:
-            for k in (1, 2, 3):
-                rounds[r + 1].pass_along(k)
-        for k in range(4):
-            rounds[r].pass_pair(k)
+        rounds[1].pass_along(k)
+    for k in range(4):
+        rounds[0].pass_pair(k)
+    rounds[2].start()
+    for k in range(4):
+        rounds[1].pass_across(k)
+    for k in (1, 2, 3):
+        rounds[2].pass_along(k)
+    for k in range(4):
+        rounds[1].pass_pair(k)
+    for k in range(4):
+        rounds[2].pass_across(k)
+    for k in range(4):
+        rounds[2].pass_pair(k)
+    for copy in finals:
+        copy.wait_recv()
+    own_bias.wait()
     for each in rounds:
         each.finish()
-
-
-def gather_block(qkv_weight, out_weight, up_weight, down_weight):
-    down_rows = lax.all_to_all(down_weight, "fsdp", split_axis=0, concat_axis=1, tiled=True)
-    sources = (jnp.concatenate([qkv_weight, out_weight], axis=1), up_weight, down_rows)
+    for copy in small.made:
+        copy.wait_send()
+
+
+def gather_all(mixed, up, down, cond, ada, ada_bias, bias):
     shapes = ((2, 2, 4, 2), (2, 2, 4, 2), (4, 2, 2, 2))
-    anywhere = pl.BlockSpec(memory_space=pl.ANY)
-    mixed, ups, downs = pl.pallas_call(
+    vmem, dma = pltpu.VMEM, pltpu.SemaphoreType.DMA
+    wide = ada.shape[1]
+    return pl.pallas_call(
         gather_kernel,
-        out_shape=[
-            jax.ShapeDtypeStruct(shape + (SHARD, D), jnp.bfloat16) for shape in shapes
+        out_shape=[shape_of(*shape, SHARD, D) for shape in shapes]
+        + [shape_of(4, 8, wide, dtype=F32), shape_of(4, 32, 128), shape_of(8, 16, 256, dtype=F32)],
+        in_specs=[ANYWHERE] * 3 + [IN_VMEM] * 4,
+        out_specs=[ANYWHERE] * 3 + [IN_VMEM] * 3,
+        scratch_shapes=[dma((3, GATHER_COPIES))] * 2
+        + [dma((3,)), dma((23,)), dma((23,)), dma((1,))]
+        + [
+            vmem((4, 8, 8, 256), F32),
+            vmem((8, 16, 256), F32),
+            vmem((8, 16, wide), F32),
+            vmem((4, 16, wide), F32),
+            vmem((3, 16, wide), F32),
+            vmem((4, 8, wide), F32),
         ],
-        in_specs=[anywhere] * 3,
-        out_specs=[anywhere] * 3,
-        scratch_shapes=[
-            pltpu.SemaphoreType.DMA((3, GATHER_COPIES)),
-            pltpu.SemaphoreType.DMA((3, GATHER_COPIES)),
-            pltpu.SemaphoreType.DMA((3,)),
-        ],
-        compiler_params=pltpu.CompilerParams(collective_id=1, has_side_effects=True),
-    )(*sources)
-    mixed, ups = mixed.reshape(4, D, D), ups.reshape(4, D, D)
-    own = qkv_weight.shape[1]
-    return (
-        mixed[:, :, :own].transpose(1, 0, 2).reshape(D, 3 * D),
-        mixed[:, :, own:].transpose(1, 0, 2).reshape(D, D),
-        ups.transpose(1, 0, 2).reshape(D, FF),
-        downs.reshape(FF, D),
-    )
-
-
-def gather_any(*shards):
-    peers, mates = lax.axis_size("dp"), lax.axis_size("fsdp")
-    results = []
-    for shard in shards:
-        stacked = lax.all_gather(shard, ("dp", "fsdp"), axis=0, tiled=False)
-        rows, columns = shard.shape
-        stacked = stacked.reshape(peers, mates, rows, columns).transpose(0, 2, 1, 3)
-        results.append(stacked.reshape(peers * rows, mates * columns))
-    return results
+        compiler_params=pltpu.CompilerParams(
+            collective_id=1, has_side_effects=True, vmem_limit_bytes=VMEM_BYTES
+        ),
+    )(mixed, up, down, cond, ada, ada_bias, bias)
 
 
 SCATTER_COPIES = 27
@@ -292,12 +847,47 @@
 ORDER = (1, 2, 3, 0)
 
 
+def close_ada(conds_ref, every, ada_ref, sums_ref):
+    total = jnp.zeros(ada_ref.shape, F32)
+    rows = jnp.zeros((16, ada_ref.shape[1]), F32)
+    for i in range(0, 8, 2):
+        rows = rows + every[i] + every[i + 1]
+        cond = jnp.concatenate([conds_ref[i][:, :SHARD], conds_ref[i + 1][:, :SHARD]], axis=0)
+        rest = jnp.concatenate([every[i], every[i + 1]], axis=0)
+        for _ in range(3):
+            part = rest.astype(BF16)
+            total = total + dot(cond.astype(BF16), part, TN)
+            rest = rest - part.astype(F32)
+    ada_ref[...] = total
+    sums_ref[...] = jnp.zeros_like(sums_ref)
+    sums_ref[0:1, :] = jnp.sum(rows[:12], axis=0, keepdims=True)
+    sums_ref[1:3, :] = rows[12:14]
+
+
 def scatter_kernel(*refs):
-    grads, outs = refs[:3], refs[3:6]
-    parts, halves, bufs = refs[6], refs[7], refs[8:13]
-    send_sems, recv_sems, pair_send, pair_recv, local_sems = refs[13:]
+    grads, mod_ref, conds_ref = refs[:3], refs[3], refs[4]
+    outs, ada_ref, sums_ref = refs[5:8], refs[8], refs[9]
+    parts, halves, bufs = refs[10], refs[11], refs[12:17]
+    send_sems, recv_sems, pair_send, pair_recv, local_sems = refs[17:22]
+    small_send, small_recv, from_mates, packed, every = refs[22:]
     place = Place()
     place.meet()
+    small = Copies(small_send, small_recv)
+    to_mates = [
+        small.make(mod_ref.at[other], from_mates.at[place.index], mate)
+        for other, mate in zip(place.mate_index, place.mates)
+    ]
+    along = [
+        small.make(packed, every.at[place.peer], place.device(z=place.zs[k])) for k in (1, 2, 3)
+    ]
+    over_x = [
+        small.make(
+            every.at[2 * place.zs[k] + place.x],
+            every.at[2 * place.zs[k] + place.x],
+            place.device(x=1 - place.x),
+        )
+        for k in range(4)
+    ]
     rounds, pairs, locals_ = [], [], []
     for r in range(3):
         rounds.append(
@@ -355,12 +945,29 @@
         for y in range(2):
             pairs[r][y].start()
             locals_[r][y].start()
+    for copy in to_mates:
+        copy.start()
+    from_mates[place.index] = mod_ref[place.index]
+    packed[...] = jnp.zeros_like(packed)
     pair(0)
+    for copy in to_mates:
+        copy.wait_recv()
+    for j in range(4):
+        packed[CROPS * j : CROPS * (j + 1), :] = from_mates[j, :CROPS, :]
+        packed[12:14, :] += from_mates[j, CROPS : CROPS + 2, :]
+    for copy in along:
+        copy.start()
+    every[place.peer] = packed[...]
     for k in ORDER:
         rounds[0].start(k)
+    pair(1)
+    for copy in along:
+        copy.wait_recv()
+    for copy in over_x:
+        copy.start()
     for r in range(3):
-        if r < 2:
-            pair(r + 1)
+        if r == 1:
+            pair(2)
         for k in ORDER:
             rounds[r].pass_across(k)
         if r < 2:
@@ -368,6 +975,10 @@
                 rounds[r + 1].start(k)
         for k in ORDER:
             rounds[r].pass_along(k)
+        if r == 0:
+            for copy in over_x:
+                copy.wait_recv()
+            close_ada(conds_ref, every, ada_ref, sums_ref)
         if r:
             rounds[r - 1].close()
     rounds[2].close()
@@ -375,48 +986,120 @@
         rounds[r].finish()
         for copy in pairs[r]:
             copy.wait_send()
-
-
-def scatter_block(grad_qkv, grad_out, grad_up, grad_down):
-    def columns(full):
-        return full.reshape(D, 4, -1).transpose(1, 0, 2)
-
-    mixed = jnp.concatenate([columns(grad_qkv), columns(grad_out)], axis=2)
+    for copy in small.made:
+        copy.wait_send()
+
+
+def scatter_all(grad_down, grad_up, grad_mixed, mod_grads, conds):
     blocks = (
         grad_down.reshape(4, 2, 2, 2, SHARD, D),
-        columns(grad_up).reshape(2, 2, 4, 2, SHARD, D),
-        mixed.reshape(2, 2, 4, 2, SHARD, D),
+        grad_up.reshape(2, 2, 4, 2, SHARD, D),
+        grad_mixed.reshape(2, 2, 4, 2, SHARD, D),
     )
     vmem, dma = pltpu.VMEM, pltpu.SemaphoreType.DMA
-    shares = pl.pallas_call(
+    wide = mod_grads.shape[2]
+    return pl.pallas_call(
         scatter_kernel,
-        out_shape=[jax.ShapeDtypeStruct((SHARD, D), jnp.float32)] * 3,
-        in_specs=[pl.BlockSpec(memory_space=pl.ANY)] * 3,
-        out_specs=[pl.BlockSpec(memory_space=pltpu.VMEM)] * 3,
-        scratch_shapes=[vmem((3, 2, 4, 2, SHARD, D), jnp.bfloat16)] * 2
-        + [vmem((3, 4, SHARD, D), jnp.bfloat16)] * 4
-        + [vmem((3, 3, SHARD, D), jnp.bfloat16)]
+        out_shape=[shape_of(SHARD, D, dtype=F32)] * 3
+        + [shape_of(SHARD, wide, dtype=F32), shape_of(8, wide, dtype=F32)],
+        in_specs=[ANYWHERE] * 3 + [IN_VMEM] * 2,
+        out_specs=[IN_VMEM] * 5,
+        scratch_shapes=[vmem((3, 2, 4, 2, SHARD, D), BF16)] * 2
+        + [vmem((3, 4, SHARD, D), BF16)] * 4
+        + [vmem((3, 3, SHARD, D), BF16)]
         + [dma((3, SCATTER_COPIES))] * 2
-        + [dma((3, 2))] * 3,
+        + [dma((3, 2))] * 3
+        + [dma((10,))] * 2
+        + [vmem((4, 8, wide), F32), vmem((16, wide), F32), vmem((8, 16, wide), F32)],
         compiler_params=pltpu.CompilerParams(
-            collective_id=2, has_side_effects=True, vmem_limit_bytes=60 * 2**20
+            collective_id=2, has_side_effects=True, vmem_limit_bytes=VMEM_BYTES
         ),
-    )(*blocks)
-    down = lax.all_to_all(shares[0], "fsdp", split_axis=1, concat_axis=0, tiled=True)
-    own = grad_qkv.shape[1] // 4
-    return (shares[2][:, :own], shares[2][:, own:], shares[1], down)
-
-
-def scatter_any(*grads):
-    peers, mates = lax.axis_size("dp"), lax.axis_size("fsdp")
-    results = []
-    for full in grads:
-        rows, columns = full.shape[0] // peers, full.shape[1] // mates
-        blocks = full.reshape(peers, rows, mates, columns)
-        blocks = blocks.transpose(0, 2, 1, 3).reshape(peers * mates * rows, columns)
-        share = lax.psum_scatter(blocks, ("dp", "fsdp"), scatter_dimension=0, tiled=True)
-        results.append(share.astype(jnp.float32))
-    return results
+    )(*blocks, mod_grads, conds)
+
+
+def block_shards(
+    block_in, condition, lengths, head_mask, group_mask, buffer_slot, ada_weight, ada_bias, qkv_weight,
+    query_bias, value_bias, out_weight, out_bias, up_weight, up_bias, down_weight, down_bias, cotangent,
+):
+    x, cot = block_in[0], cotangent[0]
+    finish = jnp.cumsum(lengths[0])
+    position = jnp.arange(TOK_DEV, dtype=jnp.int32)
+    segment = jnp.sum((position[:, None] >= finish[None, :]).astype(jnp.int32), axis=1)
+    column, row = segment[:, None], segment[None, :]
+    slot = buffer_slot[0].astype(jnp.int32)
+    slot_column, slot_row = slot[:, None], slot[None, :]
+    mask = head_mask[0].T.astype(F32)
+    chosen = (segment[:, None] == jnp.arange(CROPS)[None, :])[:, :, None]
+    groups = jnp.sum(jnp.where(chosen, group_mask[0].astype(F32)[None], 0.0), axis=1)
+    groups = jnp.pad(groups, ((0, 0), (0, 128 - GROUPS))).astype(BF16)
+    cond = jax.nn.silu(condition[0].astype(F32)).astype(BF16).astype(F32)
+    cond = cond.reshape(CROPS, 8, SHARD).transpose(1, 0, 2)
+    cond = jnp.pad(cond, ((0, 0), (0, 8 - CROPS), (0, 256 - SHARD)))
+    vectors = jnp.concatenate([query_bias, value_bias, out_bias, up_bias, down_bias])
+    packed = jnp.pad(vectors.reshape(18, 128), ((0, 14), (0, 0)))
+    down_rows = lax.all_to_all(down_weight, "fsdp", split_axis=0, concat_axis=1, tiled=True)
+    mixed_block = jnp.concatenate([qkv_weight, out_weight], axis=1)
+    mixed_weight, up, down, mods, biases, conds = gather_all(
+        mixed_block, up_weight, down_rows, cond, ada_weight, ada_bias.astype(F32)[None], packed
+    )
+    mixed_weight, up, down = mixed_weight.reshape(4, D, D), up.reshape(4, D, D), down.reshape(4, D, D)
+    mods = mods.transpose(1, 0, 2).reshape(8, 6, D).transpose(1, 0, 2)
+    biases = biases[:, :18].reshape(4, 2304).astype(F32)
+    edges = (0, 288, 576, 864, 2016, 2304)
+    bias_query, bias_value, bias_out, bias_up, bias_down = [
+        biases[:, low:high].reshape(1, -1) for low, high in zip(edges[:-1], edges[1:])
+    ]
+    qkv_bias = jnp.concatenate([bias_query, jnp.zeros_like(bias_query), bias_value], axis=1)
+    qkv_bias = jnp.pad(qkv_bias.reshape(4, 1, QKV_SHARD), ((0, 0), (0, 0), (0, PAD_SHARD - QKV_SHARD)))
+    first, heads, mixed, lse, attn, after, arrived, picked, full_out = attend(
+        x, mixed_weight, mods, qkv_bias, bias_out, column, row, slot_row, groups, mask
+    )
+    pull, grad_down, grad_rows, block_out, gate_two, grad_down_bias = feed(
+        up, down, arrived, picked, bias_up.reshape(4, 1, D), bias_down, cot, after, mods, column,
+        slot_column, slot_row,
+    )
+    grad_up, grad_up_bias, mid, grad_attn, grad_split, sums, grad_out_bias = unfeed(
+        down, up, pull, grad_rows, arrived, after, cot, attn, mods, column, slot_column
+    )
+    triple, triple_sums = unattend(grad_attn, full_out, heads, lse, column, row, mask)
+    grad_mixed, grad_in, first_sums = unproject(
+        mixed_weight, triple, grad_split, first, mixed, x, mid, mods, column
+    )
+    triple_sums = triple_sums[:, 0, :QKV_SHARD].reshape(3 * D)
+    mod_grads = jnp.concatenate(
+        [first_sums[0], first_sums[1], sums[0], sums[1], sums[2], gate_two], axis=1
+    )[:CROPS]
+    mod_grads = mod_grads.reshape(CROPS, 4, -1).transpose(1, 0, 2)
+    bias_grads = (
+        triple_sums[:D], triple_sums[2 * D :], grad_out_bias, grad_up_bias, grad_down_bias,
+    )
+    bias_grads = jnp.concatenate([vector.reshape(4, -1) for vector in bias_grads], axis=1)
+    wide = mod_grads.shape[2]
+    bias_grads = jnp.pad(bias_grads, ((0, 0), (0, 5 * wide - 2304))).reshape(4, 5, wide)
+    mod_grads = jnp.concatenate([mod_grads, bias_grads], axis=1)
+    share_down, share_up, share_mixed, grad_ada, totals = scatter_all(
+        grad_down, grad_up, grad_mixed, mod_grads, conds
+    )
+    share_down = lax.all_to_all(share_down, "fsdp", split_axis=1, concat_axis=0, tiled=True)
+    bias_totals = totals[1:3].reshape(-1)
+    grad_query, grad_value, grad_out, grad_ups, grad_downs = [
+        bias_totals[low:high] for low, high in zip(edges[:-1], edges[1:])
+    ]
+    return (
+        block_out[None],
+        grad_in[None],
+        grad_ada,
+        totals[0],
+        share_mixed[:, :QKV_SHARD],
+        grad_query,
+        grad_value,
+        share_mixed[:, QKV_SHARD:],
+        grad_out,
+        share_up,
+        grad_ups,
+        share_down,
+        grad_downs,
+    )
 
 
 def layer_norm(values):
@@ -467,9 +1150,15 @@
     peers = lax.axis_size("dp")
     mates = lax.axis_size("fsdp")
 
-    on_block = peers == 8 and mates == 4
-    gather = gather_block if on_block else gather_any
-    full_qkv, full_out, full_up, full_down = gather(qkv_weight, out_weight, up_weight, down_weight)
+    def gather_matrix(shard):
+        stacked = lax.all_gather(shard, ("dp", "fsdp"), axis=0, tiled=False)
+        rows, columns = shard.shape
+        stacked = stacked.reshape(peers, mates, rows, columns).transpose(0, 2, 1, 3)
+        return stacked.reshape(peers * rows, mates * columns)
+
+    full_qkv, full_out, full_up, full_down = [
+        gather_matrix(shard) for shard in (qkv_weight, out_weight, up_weight, down_weight)
+    ]
     vectors = (query_bias, value_bias, out_bias, up_bias, down_bias)
     packed_bias = lax.all_gather(jnp.concatenate(vectors), "fsdp", axis=0, tiled=False)
     edges = [0]
@@ -684,10 +1373,14 @@
         "sd,se->de", cond_slice.astype(jnp.float32), mod_all, precision=highest
     )
 
-    scatter = scatter_block if on_block else scatter_any
-    shares = scatter(
-        *[full.astype(jnp.bfloat16) for full in (grad_qkv, grad_out, grad_up, grad_down)]
-    )
+    def scatter_matrix(full):
+        rows, columns = full.shape[0] // peers, full.shape[1] // mates
+        blocks = full.astype(jnp.bfloat16).reshape(peers, rows, mates, columns)
+        blocks = blocks.transpose(0, 2, 1, 3).reshape(peers * mates * rows, columns)
+        share = lax.psum_scatter(blocks, ("dp", "fsdp"), scatter_dimension=0, tiled=True)
+        return share.astype(jnp.float32)
+
+    shares = [scatter_matrix(full) for full in (grad_qkv, grad_out, grad_up, grad_down)]
     bias_grads = (grad_query_bias, grad_value_bias, grad_out_bias, grad_up_bias, grad_down_bias)
     packed = jnp.concatenate([vector.reshape(mates, -1) for vector in bias_grads], axis=1)
     packed = lax.psum_scatter(packed, "fsdp", scatter_dimension=0, tiled=True)
@@ -731,8 +1424,9 @@
         P("fsdp"),
         P(("dp", "fsdp"), None, None),
     )
+    on_block = dict(mesh.shape) == {"dp": 8, "fsdp": 4}
     return jax.shard_map(
-        shards,
+        block_shards if on_block else shards,
         mesh=mesh,
         in_specs=placed,
         out_specs=(

time: 1050 us -> 629 us (0.60)
  matrix products: 307 us -> 0 us
  Pallas kernels: 326 us -> 563 us
  blocking collectives: 130 us -> 0 us
  local copies, waits for them, and re-layouts: 151 us -> 33.1 us
  other arithmetic: 81.6 us -> 7.03 us
  starting transfers between devices: 29.4 us -> 9.15 us
    dot_general x55 -> x0, matrix products: 307 us -> none  [the longest x4 43.9 us: shards(): jnp.einsum('qhd,khd->hqk', grad_piece, values_all[:, heads_here], preferr...]
    pallas_call x2 -> x7, Pallas kernels: 326 us -> 563 us  [the longest x1 174 us: scatter_all(): pl.pallas_call(scatter_kernel, out_shape=[shape_of(SHARD, D, dtype=F32)]...]
    all_gather x3 -> x0, blocking collectives: 66.8 us -> none  [the longest x1 36.7 us: shards(): cond_all = lax.all_gather(cond_act, ('dp', 'fsdp'), axis=0, tiled=True)]
    unnamed x2 -> x0, blocking collectives: 37.9 us -> none
    convert_element_type x9 -> x2, other arithmetic: 38.5 us -> 1.37 us  [the longest x1 0.68 us: block_shards(): group_mask[0].astype(F32)[None]]
    reshape x8 -> x13, local copies, waits for them, and re-layouts: 36.2 us -> 3.1 us  [the longest x4 1.54 us: block_shards(): biases[:, low:high].reshape(1, -1)]
    unnamed x210 -> x28, local copies, waits for them, and re-layouts: 35.1 us -> 6.57 us
    slice x10 -> x12, local copies, waits for them, and re-layouts: 31.9 us -> 6.24 us  [the longest x1 1.44 us: block_shards(): totals[0]]
  transfers between devices with their start and end apart: 6 -> 2, of which waited for: 1 -> 1; matrix products, arithmetic and copies ran while one was open for 9% -> 3% of each run, Pallas kernels for 17% -> 0%
where the time goes in v3:
time: 629 us; the launch traced here: 620 us
  Pallas kernels  563 us (90%)
  local copies, waits for them, and re-layouts  33.1 us (5%)
  starting transfers between devices  9.15 us (1%)
  other arithmetic  7.03 us (1%)
  waiting for transfers between devices  6.53 us (1%)
    pallas_call x1, Pallas kernels, scatter_all(): pl.pallas_call(scatter_kernel, out_shape=[shape_of(SHARD, D, dtype=F32)]...  174 us
    pallas_call x1, Pallas kernels, gather_all(): pl.pallas_call(gather_kernel, out_shape=[shape_of(*shape, SHARD, D) for s...  166 us
    pallas_call x1, Pallas kernels, attend(): pl.pallas_call(attend_kernel, out_shape=[shape_of(TOK_DEV, D), shape_of(3...  56.8 us
    pallas_call x1, Pallas kernels, unattend(): pl.pallas_call(unattend_kernel, out_shape=[shape_of(4, TOK_DEV, PAD_SHARD...  48.5 us
    pallas_call x1, Pallas kernels, unfeed(): pl.pallas_call(unfeed_kernel, grid=(4,), out_shape=[shape_of(4, D, D), sh...  41.1 us
    pallas_call x1, Pallas kernels, feed(): pl.pallas_call(feed_kernel, grid=(8,), out_shape=[shape_of(4, PLACES, D),...  41.1 us
    pallas_call x1, Pallas kernels, unproject(): pl.pallas_call(unproject_kernel, grid=(4,), out_shape=[shape_of(4, D, D),...  35.8 us
  transfers between devices with their start and end apart: 2, of which 1 were waited for; matrix products, arithmetic and copies ran while one was open for 3% of the time, Pallas kernels for 0%

profile of v3, /device:TPU:9, one launch (start us, length us, event | category | flops | bytes accessed | tf_op | source)
XLA Modules:
  0.0 620.0 jit_solution(18416647583999556875)
XLA Ops:
  0.7 2.0 copy.69
  2.6 4.1 all-to-all-start
  7.4 0.8 reduce-window.8
  8.4 0.8 reshape.169
  10.5 0.9 broadcast_in_dim.60.column_ref
  12.8 1.3 reshape.170.ada_bias_ref
  14.2 3.5 concatenate.19
  19.1 1.6 copy.81.slot_column_ref
  20.7 1.7 pad_maximum_fusion.mixed_ref
  22.7 1.0 all_to_all.31.down_ref
  23.7 166.1 %shard_map.273 = (bf16[2,2,4,2,144,1152]{5,4,3,2,1,0:T(8,128)(2,1)}, bf16[2,2,4,2,144,1152]{5,4,3,2,1,0:T(8,128)(2,1)}, bf16[4,2,2,2,144,1152]{5,4,3,2,1,0:T(8,1...) custom-call(bf16[144,1152]{1,0:T(8,128)(2,1)} %pad_maximum_fusion.mixed_ref, ...), custom_call_target="tpu_custom_call" | custom-call | tf_op jit(solution)/shard_map/pallas_call | solution.py:748
  193.6 1.0 copy.75
  195.6 56.8 %shard_map.274 = (bf16[768,1152]{1,0:T(8,128)(2,1)}, bf16[48,768,128]{2,1,0:T(8,128)(2,1)}, bf16[768,1152]{1,0:T(8,128)(2,1)}, f32[16,1,768]{2,1,0:T(1,128)}, f3...) custom-call(bf16[768,1152]{1,0:T(8,128)(2,1)} %bitcast.63, ...), custom_call_target="tpu_custom_call" | custom-call | tf_op jit(solution)/shard_map/pallas_call | solution.py:164
  252.4 41.1 %shard_map.275 = (bf16[4,512,1152]{2,1,0:T(8,128)(2,1)}, bf16[4,1152,1152]{2,1,0:T(8,128)(2,1)}, bf16[512,1152]{1,0:T(8,128)(2,1)}, bf16[768,1152]{1,0:T(8,128)(...) custom-call(bf16[4,1152,1152]{2,1,0:T(8,128)(2,1)} %bitcast.52, bf16[4,1152,1152]{2,1,0:T(8,128)(2,1)} %bitcast.54, ...), custom_call_target="tpu_custom_call" | custom-call | tf_op jit(solution)/shard_map/pallas_call | solution.py:265
  293.5 41.1 %shard_map.276 = (bf16[4,1152,1152]{2,1,0:T(8,128)(2,1)}, f32[4,1,1152]{2,1,0:T(1,128)}, f32[768,1152]{1,0:T(8,128)}, bf16[768,1152]{1,0:T(8,128)(2,1)}, bf16[4,...) custom-call(bf16[4,1152,1152]{2,1,0:T(8,128)(2,1)} %bitcast.55, bf16[4,1152,1152]{2,1,0:T(8,128)(2,1)} %bitcast.53, ...), custom_call_target="tpu_custom_call" | custom-call | tf_op jit(solution)/shard_map/pallas_call | solution.py:351
  335.5 48.5 %shard_map.277 = (bf16[4,768,896]{2,1,0:T(8,128)(2,1)}, f32[4,1,896]{2,1,0:T(1,128)}) custom-call(bf16[768,1152]{1,0:T(8,128)(2,1)} %get-tuple-element.63.grad_ref, bf16[1152,1152]{1,0:T(8,128)(2,1)} %get-tuple-element.64.out_weight_ref, bf16[48,768,128]{2,1,0:T(8,128)(2,1)} %get-tuple-element.65.heads_ref, f32[16,1,768]{2,1,0:T(1,128)} %get-tuple-element.66.lse_ref, ...), custom_call_target="tpu_custom_call" | custom-call | tf_op jit(solution)/shard_map/pallas_call | solution.py:432
  384.1 0.8 slice_reduce_fusion
  385.2 35.8 %shard_map.278 = (bf16[4,1152,1152]{2,1,0:T(8,128)(2,1)}, f32[768,1152]{1,0:T(8,128)}, f32[2,8,1152]{2,1,0:T(8,128)}) custom-call(bf16[4,1152,1152]{2,1,0:T(8,128)(2,1)} %bitcast.57, bf16[4,768,896]{2,1,0:T(8,128)(2,1)} %get-tuple-element.67.triple_ref, bf16[4,768,288]{2,1,0:T(8,128)(2,1)} %get-tuple-element.68.split_ref, ...), custom_call_target="tpu_custom_call" | custom-call | tf_op jit(solution)/shard_map/pallas_call | solution.py:487
  421.1 0.8 bitcast_dynamic-update-slice_fusion.4
  421.8 0.8 bitcast_dynamic-update-slice_fusion.3
  423.6 173.6 %shard_map.279 = (f32[144,1152]{1,0:T(8,128)}, f32[144,1152]{1,0:T(8,128)}, f32[144,1152]{1,0:T(8,128)}, f32[144,1728]{1,0:T(8,128)}, f32[8,1728]{1,0:T(8,128)}) custom-call(bf16[4,2,2,2,144,1152]{5,4,3,2,1,0:T(8,128)(2,1)} %bitcast.58, bf16[2,2,4,2,144,1152]{5,4,3,2,1,0:T(8,128)(2,1)} %bitcast.59, bf16[2,2,4,2,144,1152]{5,4,3,2,1,0:T(8,128)(2,1)} %bitcast.60, ...), custom_call_target="tpu_custom_call" | custom-call | tf_op jit(solution)/shard_map/pallas_call | solution.py:1001
  597.2 1.7 all_to_all.32
  598.9 1.0 copy.87
  599.9 5.0 all-to-all-start.1
  604.9 0.8 slice.97
  605.7 0.8 slice.93
  606.6 0.8 slice.94
  608.1 1.4 slice_reduce_fusion.1
  610.2 6.5 %all-to-all-done.1 = f32[144,4,288]{2,0,1:T(8,128)S(1)} async-done(((f32[144,4,288]{2,0,1:T(8,128)}), f32[144,4,288]{2,0,1:T(8,128)S(1)}, u32[]{:S(2)}, u32[]{:S(2)}) %all-to-all-start.1) | async-done | bytes 663584 | tf_op jit(solution)/shard_map/all_to_all | solution.py:1083
  616.8 1.2 copy.88
  617.9 1.0 copy.122
  618.9 0.8 copy.123
  (68 shorter events, 13.6 us)
Async XLA Ops:
  0.6 20.1 %copy-start.3 = (bf16[144,864]{1,0:T(8,128)(2,1)S(1)}, bf16[144,864]{1,0:T(8,128)(2,1)}, u32[]{:S(2)}) copy-start(bf16[144,864]{1,0:T(8,128)(2,1)} %param.26) | copy-start | bytes 746500
  2.6 19.8 %all-to-all-start = ((bf16[4,144,288]{2,1,0:T(8,128)(2,1)}), bf16[4,144,288]{2,1,0:T(8,128)(2,1)S(1)}, u32[]{:S(2)}, u32[]{:S(2)}) async-start(bf16[4,144,288]{2,1,0:T(8,128)(2,1)} %bitcast), calls=%async_computation | async-start | bytes 884736 | tf_op jit(solution)/shard_map/all_to_all | solution.py:1040
  293.5 42.0 %copy-start.7 = (f32[1,1152]{1,0:T(1,128)S(1)}, f32[1,1152]{1,0:T(1,128)}, u32[]{:S(2)}) copy-start(f32[1,1152]{1,0:T(1,128)} %get-tuple-element.82) | copy-start | bytes 13828
  335.5 49.4 %copy-start.6 = (f32[4,1,1152]{2,1,0:T(1,128)S(1)}, f32[4,1,1152]{2,1,0:T(1,128)}, u32[]{:S(2)}) copy-start(f32[4,1,1152]{2,1,0:T(1,128)} %get-tuple-element.81) | copy-start | bytes 55300
  385.2 37.4 %copy-start.4 = (f32[3,8,1152]{2,1,0:T(8,128)S(1)}, f32[3,8,1152]{2,1,0:T(8,128)}, u32[]{:S(2)}) copy-start(f32[3,8,1152]{2,1,0:T(8,128)} %get-tuple-element.77) | copy-start | bytes 331780
  385.2 37.4 %copy-start.5 = (f32[8,1152]{1,0:T(8,128)S(1)}, f32[8,1152]{1,0:T(8,128)}, u32[]{:S(2)}) copy-start(f32[8,1152]{1,0:T(8,128)} %get-tuple-element.78) | copy-start | bytes 110596
  597.2 7.8 %copy-start.1 = (f32[144,1152]{1,0:T(8,128)S(1)}, f32[144,1152]{1,0:T(8,128)}, u32[]{:S(2)}) copy-start(f32[144,1152]{1,0:T(8,128)} %get-tuple-element.86) | copy-start | bytes 1990660
  598.9 19.0 %copy-start = (f32[144,1728]{1,0:T(8,128)S(1)}, f32[144,1728]{1,0:T(8,128)}, u32[]{:S(2)}) copy-start(f32[144,1728]{1,0:T(8,128)} %get-tuple-element.153) | copy-start | bytes 2985988
  599.9 19.0 %copy-start.2 = (f32[144,1152]{1,0:T(8,128)S(1)}, f32[144,1152]{1,0:T(8,128)}, u32[]{:S(2)}) copy-start(f32[144,1152]{1,0:T(8,128)} %get-tuple-element.160) | copy-start | bytes 1990660
  599.9 16.9 %all-to-all-start.1 = ((f32[144,4,288]{2,0,1:T(8,128)}), f32[144,4,288]{2,0,1:T(8,128)S(1)}, u32[]{:S(2)}, u32[]{:S(2)}) async-start(f32[144,4,288]{2,0,1:T(8,128)} %copy.87), calls=%async_computation.1 | async-start | bytes 1769472 | tf_op jit(solution)/shard_map/all_to_all | solution.py:1083

commit v4 on v1

--- a/solution.py
+++ b/solution.py
@@ -1,6 +1,10 @@
+import math
+
 import jax
 import jax.numpy as jnp
 from jax import lax
+from jax.experimental import pallas as pl
+from jax.experimental.pallas import tpu as pltpu
 from jax.sharding import PartitionSpec as P
 
 D = 1152
@@ -13,6 +17,1393 @@
 
 highest = lax.Precision.HIGHEST
 epsilon = 1e-06
+
+
+NT = (((1,), (1,)), ((), ()))
+TN = (((0,), (0,)), ((), ()))
+NN = (((1,), (0,)), ((), ()))
+PLACES = 512
+BLOCK = 256
+BF16, F32 = jnp.bfloat16, jnp.float32
+SOFT = HEAD_DIM**-0.5 * math.log2(math.e)
+QKV_SHARD, OUT_SHARD, PAD_SHARD = 864, 288, 896
+VMEM_BYTES = 60 * 2**20
+
+
+def dot(left, right, dims=NN):
+    return lax.dot_general(left, right, dims, preferred_element_type=F32)
+
+
+def rows_at(i):
+    return pl.ds(pl.multiple_of(i * BLOCK, BLOCK), BLOCK)
+
+
+def per_crop(table, segment):
+    return jnp.where(
+        segment == 0, table[0:1], jnp.where(segment == 1, table[1:2], table[2:3])
+    )
+
+
+def normalise(values):
+    center = values - jnp.mean(values, axis=1, keepdims=True)
+    variance = jnp.mean(center * center, axis=1, keepdims=True)
+    inverse = lax.rsqrt(variance + epsilon)
+    return center * inverse, inverse
+
+
+def crop_sums(segment, values):
+    lanes = lax.broadcasted_iota(jnp.int32, (values.shape[0], 128), 1)
+    member = (lanes == segment).astype(BF16)
+    high = values.astype(BF16)
+    low = (values - high.astype(F32)).astype(BF16)
+    return (dot(member, high, TN) + dot(member, low, TN))[:8]
+
+
+def crop_mask(bias_ref, column_ref, row_ref):
+    for i in range(TOK_DEV // BLOCK):
+        here = pl.ds(i * BLOCK, BLOCK)
+        bias_ref[here, :] = jnp.where(column_ref[here, :] == row_ref[...], 0.0, -1e30).astype(F32)
+
+
+def places_of(slot_row, i):
+    place = lax.broadcasted_iota(jnp.int32, (BLOCK, TOK_DEV), 0) + i * BLOCK
+    return (place == slot_row).astype(BF16)
+
+
+def tokens_of(slot_column):
+    place = lax.broadcasted_iota(jnp.int32, (BLOCK, PLACES), 1)
+    return (place == slot_column).astype(BF16)
+
+
+def head_keep(mask_ref, h, segment):
+    return jnp.where(
+        segment == 0, mask_ref[h, 0], jnp.where(segment == 1, mask_ref[h, 1], mask_ref[h, 2])
+    )
+
+
+MESH = pl.DeviceIdType.MESH
+SHARD = 144
+UPPER = 80
+
+
+class Place:
+    def __init__(self):
+        dp, fsdp = lax.axis_index("dp"), lax.axis_index("fsdp")
+        self.z, self.x = lax.div(dp, 2), lax.rem(dp, 2)
+        self.y, self.c = lax.div(fsdp, 2), lax.rem(fsdp, 2)
+        z = self.z
+        self.zs = (z, z + 1 - 2 * lax.rem(z, 2), lax.rem(z + 2, 4), 3 - z)
+        self.mates = (
+            self.device(c=1 - self.c),
+            self.device(y=1 - self.y),
+            self.device(y=1 - self.y, c=1 - self.c),
+        )
+        self.mate_index = (
+            2 * self.y + 1 - self.c,
+            2 * (1 - self.y) + self.c,
+            2 * (1 - self.y) + 1 - self.c,
+        )
+        self.index = 2 * self.y + self.c
+        self.peer = 2 * z + self.x
+
+    def device(self, z=None, x=None, y=None, c=None):
+        z, x = self.z if z is None else z, self.x if x is None else x
+        y, c = self.y if y is None else y, self.c if c is None else c
+        return (2 * z + x, 2 * y + c)
+
+    def meet(self):
+        barrier = pltpu.get_barrier_semaphore()
+        others = [self.device(z=self.zs[k]) for k in (1, 2, 3)]
+        others += [self.device(z=self.zs[k], x=1 - self.x) for k in range(4)]
+        others += self.mates
+        for other in others:
+            pl.semaphore_signal(barrier, inc=1, device_id=other, device_id_type=MESH)
+        pl.semaphore_wait(barrier, len(others))
+
+
+class Copies:
+    def __init__(self, send_sems, recv_sems):
+        self.send_sems, self.recv_sems, self.made = send_sems, recv_sems, []
+
+    def make(self, source, target, device):
+        index = len(self.made)
+        copy = pltpu.make_async_remote_copy(
+            src_ref=source,
+            dst_ref=target,
+            send_sem=self.send_sems.at[index],
+            recv_sem=self.recv_sems.at[index],
+            device_id=device,
+            device_id_type=MESH,
+        )
+        self.made.append(copy)
+        return copy
+
+
+GATHER_COPIES = 35
+
+
+class Gather:
+    def __init__(self, place, source, slot, send_sems, recv_sems, local_sem, swap):
+        x, y, c, zs = place.x, place.y, place.c, place.zs
+        self.copies = Copies(send_sems, recv_sems)
+        make = self.copies.make
+        first, second = (SHARD - UPPER, UPPER) if swap else (0, UPPER)
+        upper = pl.ds(first, second)
+        lower = pl.ds(0, SHARD - UPPER) if swap else pl.ds(UPPER, SHARD - UPPER)
+        over_x, over_y, beside = (
+            place.device(x=1 - x),
+            place.device(y=1 - y),
+            place.device(c=1 - c),
+        )
+        own = [slot(y, c, zs[k], x) for k in range(4)]
+        held = [source] + own[1:]
+        from_x = [slot(y, c, zs[k], 1 - x) for k in range(4)]
+        from_y = [slot(1 - y, c, zs[k], x) for k in range(4)]
+        across = [slot(1 - y, c, zs[k], 1 - x) for k in range(4)]
+        self.local = pltpu.make_async_copy(source, own[0], local_sem)
+        self.along = [None] + [make(source, own[0], place.device(z=zs[k])) for k in (1, 2, 3)]
+        self.to_x = [make(held[k], own[k], over_x) for k in range(4)]
+        self.to_y = [make(held[k], own[k], over_y) for k in range(4)]
+        self.x_to_y = [make(s.at[upper], s.at[upper], over_y) for s in from_x]
+        self.y_to_x = [make(s.at[lower], s.at[lower], over_x) for s in from_y]
+        self.pair = [make(held[k], own[k], beside) for k in range(4)]
+        self.pair_x = [make(s, s, beside) for s in from_x]
+        self.pair_y = [make(s, s, beside) for s in from_y]
+        self.pair_across = [make(s, s, beside) for s in across]
+
+    def start(self):
+        self.along[1].start()
+        self.to_x[0].start()
+        self.to_y[0].start()
+        self.along[2].start()
+        self.along[3].start()
+        self.pair[0].start()
+        self.local.start()
+
+    def pass_along(self, k):
+        self.along[k].wait_recv()
+        self.to_x[k].start()
+        self.to_y[k].start()
+        self.pair[k].start()
+
+    def pass_across(self, k):
+        self.to_x[k].wait_recv()
+        self.x_to_y[k].start()
+        self.pair_x[k].start()
+        self.to_y[k].wait_recv()
+        self.y_to_x[k].start()
+        self.pair_y[k].start()
+
+    def pass_pair(self, k):
+        self.x_to_y[k].wait_recv()
+        self.y_to_x[k].wait_recv()
+        self.pair_across[k].start()
+
+    def finish(self):
+        self.local.wait()
+        for copy in self.pair + self.pair_x + self.pair_y + self.pair_across:
+            copy.wait_recv()
+        for copy in self.copies.made:
+            copy.wait_send()
+
+
+class Column:
+    def __init__(self, place, source, column, send_sems, recv_sems, local_sem):
+        copies = Copies(send_sems, recv_sems)
+        self.local = pltpu.make_async_copy(source, column.at[place.z], local_sem)
+        self.along = [
+            copies.make(source, column.at[place.z], place.device(z=place.zs[k])) for k in (1, 2, 3)
+        ]
+
+    def start(self):
+        for copy in self.along:
+            copy.start()
+        self.local.start()
+
+    def finish(self):
+        for copy in self.along:
+            copy.wait()
+        self.local.wait()
+
+
+SPREAD_COPIES = 32
+
+
+class Spread:
+    def __init__(self, place, column, slot, send_sems, recv_sems, local_sems):
+        x, y, c, zs = place.x, place.y, place.c, place.zs
+        self.copies = Copies(send_sems, recv_sems)
+        make = self.copies.make
+        upper, lower = pl.ds(0, UPPER), pl.ds(UPPER, SHARD - UPPER)
+        over_x, over_y, beside = place.device(x=1 - x), place.device(y=1 - y), place.mates[0]
+        four = range(4)
+        held = [column.at[zs[k]] for k in four]
+        own = [slot(y, c, zs[k], x) for k in four]
+        from_x = [slot(y, c, zs[k], 1 - x) for k in four]
+        from_y = [slot(1 - y, c, zs[k], x) for k in four]
+        across = [slot(1 - y, c, zs[k], 1 - x) for k in four]
+        first = [upper, lower, upper, lower]
+        second = [lower, upper, lower, upper]
+        self.local = [pltpu.make_async_copy(held[k], own[k], local_sems.at[k]) for k in four]
+        self.to_x = [make(held[k], own[k], over_x) for k in four]
+        self.to_y = [make(held[k], own[k], over_y) for k in four]
+        self.x_to_y = [make(from_x[k].at[first[k]], from_x[k].at[first[k]], over_y) for k in four]
+        self.y_to_x = [make(from_y[k].at[second[k]], from_y[k].at[second[k]], over_x) for k in four]
+        self.pair = [make(held[k], own[k], beside) for k in four]
+        self.pair_x = [make(s, s, beside) for s in from_x]
+        self.pair_y = [make(s, s, beside) for s in from_y]
+        self.pair_across = [make(s, s, beside) for s in across]
+
+    def start(self):
+        for k in range(4):
+            self.to_x[k].start()
+            self.to_y[k].start()
+        for k in range(4):
+            self.pair[k].start()
+            self.local[k].start()
+
+    def pass_across(self, k):
+        self.to_x[k].wait_recv()
+        self.x_to_y[k].start()
+        self.pair_x[k].start()
+        self.to_y[k].wait_recv()
+        self.y_to_x[k].start()
+        self.pair_y[k].start()
+
+    def pass_pair(self, k):
+        self.x_to_y[k].wait_recv()
+        self.y_to_x[k].wait_recv()
+        self.pair_across[k].start()
+
+    def finish(self):
+        for copy in self.local:
+            copy.wait()
+        for copy in self.pair + self.pair_x + self.pair_y + self.pair_across:
+            copy.wait_recv()
+        for copy in self.copies.made:
+            copy.wait_send()
+
+
+SCATTER_COPIES = 24
+
+
+class Scatter:
+    def __init__(self, place, parts, bufs, column, send_sems, recv_sems):
+        x, y, zs = place.x, place.y, place.zs
+        self.place, self.parts, self.column = place, parts, column
+        self.by_x, self.by_y, self.from_x, self.from_y = [bufs.at[k] for k in range(4)]
+        self.copies = Copies(send_sems, recv_sems)
+        make = self.copies.make
+        self.upper, self.lower = (0, UPPER), (UPPER, SHARD - UPPER)
+        a, b = pl.ds(*self.upper), pl.ds(*self.lower)
+        over_x, over_y = place.device(x=1 - x), place.device(y=1 - y)
+        four = range(4)
+        self.across_y = [
+            make(parts.at[1 - y, zs[k], 1 - x, a], self.by_y.at[k, a], over_y) for k in four
+        ]
+        self.across_x = [
+            make(parts.at[1 - y, zs[k], 1 - x, b], self.by_x.at[k, b], over_x) for k in four
+        ]
+        self.x_lower = [make(parts.at[y, zs[k], 1 - x, b], self.from_x.at[k, b], over_x) for k in four]
+        self.y_upper = [make(parts.at[1 - y, zs[k], x, a], self.from_y.at[k, a], over_y) for k in four]
+        self.x_upper = [make(self.by_y.at[k, a], self.from_x.at[k, a], over_x) for k in four]
+        self.y_lower = [make(self.by_x.at[k, b], self.from_y.at[k, b], over_y) for k in four]
+
+    def start(self, k):
+        self.across_y[k].start()
+        self.across_x[k].start()
+
+    def follow(self, k):
+        self.x_lower[k].start()
+        self.y_upper[k].start()
+
+    def add(self, target, k, index, rows):
+        for at in range(0, rows[1], 16):
+            here = pl.ds(rows[0] + at, 16)
+            total = self.parts[(*index, here)].astype(F32) + target[k, here].astype(F32)
+            target[k, here] = total.astype(BF16)
+
+    def pass_across(self, k):
+        x, y, z = self.place.x, self.place.y, self.place.zs[k]
+        self.across_y[k].wait_recv()
+        self.add(self.by_y, k, (y, z, 1 - x), self.upper)
+        self.x_upper[k].start()
+        self.across_x[k].wait_recv()
+        self.add(self.by_x, k, (1 - y, z, x), self.lower)
+        self.y_lower[k].start()
+
+    def collect(self, k):
+        x, y, z = self.place.x, self.place.y, self.place.zs[k]
+        for copy in (self.x_upper[k], self.x_lower[k], self.y_upper[k], self.y_lower[k]):
+            copy.wait_recv()
+        for at in range(0, SHARD, 16):
+            here = pl.ds(at, 16)
+            total = self.parts[y, z, x, here].astype(F32) + self.from_x[k, here].astype(F32)
+            self.column[k, here] = (total + self.from_y[k, here].astype(F32)).astype(BF16)
+
+    def finish(self):
+        for copy in self.copies.made:
+            copy.wait_send()
+
+
+class Along:
+    def __init__(self, place, column, from_z, out, send_sems, recv_sems):
+        copies = Copies(send_sems, recv_sems)
+        self.column, self.from_z, self.out = column, from_z, out
+        self.copies = [
+            copies.make(column.at[k], from_z.at[k - 1], place.device(z=place.zs[k])) for k in (1, 2, 3)
+        ]
+
+    def start(self, k):
+        self.copies[k - 1].start()
+
+    def close(self):
+        for copy in self.copies:
+            copy.wait()
+        for at in range(0, SHARD, 16):
+            here = pl.ds(at, 16)
+            total = self.column[0, here].astype(F32)
+            for k in range(3):
+                total = total + self.from_z[k, here].astype(F32)
+            self.out[here] = total
+
+
+ORDER = (1, 2, 3, 0)
+DMA = pltpu.SemaphoreType.DMA
+
+
+def add_rows(target, rows, left, right):
+    def body(i, carry):
+        here = pl.ds(pl.multiple_of(16 * i, 16), 16)
+        target(here, (left(here).astype(F32) + right(here).astype(F32)).astype(BF16))
+        return carry
+
+    lax.fori_loop(0, rows // 16, body, 0)
+
+
+class Pair:
+    def __init__(self, place, buffers, parts, send_sems, recv_sems):
+        self.place, self.buffers, self.parts = place, buffers, parts
+        self.send_sems, self.recv_sems = send_sems, recv_sems
+
+    def copy(self, m):
+        y = lax.div(m, 2)
+        return pltpu.make_async_remote_copy(
+            src_ref=self.buffers.at[lax.rem(m, 2)],
+            dst_ref=self.parts.at[y],
+            send_sem=self.send_sems.at[y],
+            recv_sem=self.recv_sems.at[y],
+            device_id=self.place.mates[0],
+            device_id_type=MESH,
+        )
+
+    def send(self, m):
+        @pl.when(lax.rem(m, 2) != self.place.c)
+        def _():
+            self.copy(m).start()
+
+    def free(self, m):
+        @pl.when(lax.rem(m, 2) != self.place.c)
+        def _():
+            self.copy(m).wait_send()
+
+    def take(self, m):
+        @pl.when(lax.rem(m, 2) == self.place.c)
+        def _():
+            y, buffer = lax.div(m, 2), lax.rem(m, 2)
+            self.copy(m).wait_recv()
+
+            def store(here, value):
+                self.parts[y, here] = value
+
+            add_rows(
+                store, D, lambda here: self.buffers[buffer, here], lambda here: self.parts[y, here]
+            )
+
+
+def attend_kernel(
+    x_ref, weight_ref, mods_ref, qkv_bias_ref, out_bias_ref, column_ref, row_ref, slot_ref,
+    groups_ref, mask_ref, up_ref, down_ref,
+    first_ref, heads_ref, mixed_ref, lse_ref, attn_ref, after_ref, arrived_ref, picked_ref, out_weight_ref,
+    up_out, down_out,
+    bias_ref, parts_ref, second_ref,
+    send_sems, recv_sems, local_sems, down_send, down_recv, down_local,
+):
+    place = Place()
+    place.meet()
+    ups = Spread(
+        place, up_ref, lambda y, c, z, x: up_out.at[y, c, z, x], send_sems, recv_sems, local_sems
+    )
+    downs = Column(place, down_ref, down_out, down_send, down_recv, down_local.at[0])
+    ups.start()
+    downs.start()
+    crop_mask(bias_ref, column_ref, row_ref)
+
+    def norm(i, carry):
+        here = rows_at(i)
+        segment = column_ref[here, :]
+        normed, _ = normalise(x_ref[here, :].astype(F32))
+        shift, scale = per_crop(mods_ref[0], segment), per_crop(mods_ref[1], segment)
+        first_ref[here, :] = (normed * (1.0 + scale) + shift).astype(BF16)
+        return carry
+
+    lax.fori_loop(0, 3, norm, 0)
+    for j in range(4):
+        out_weight_ref[:, OUT_SHARD * j : OUT_SHARD * (j + 1)] = weight_ref[j, :, QKV_SHARD:]
+
+    def project(i, carry):
+        j = lax.div(i, 3)
+        here = rows_at(lax.rem(i, 3))
+        triple = (dot(first_ref[here, :], weight_ref[j, :, :PAD_SHARD]) + qkv_bias_ref[j]).astype(BF16)
+        zero = jnp.zeros((BLOCK, 128 - HEAD_DIM), BF16)
+        for h in range(12):
+            part = triple[:, HEAD_DIM * h : HEAD_DIM * (h + 1)]
+            heads_ref[12 * j + h, here, :] = jnp.concatenate([part, zero], axis=1)
+        return carry
+
+    lax.fori_loop(0, 12, project, 0)
+
+    def head(h, carry):
+        for k in range(4):
+
+            @pl.when(h == 7 + k)
+            def _():
+                ups.pass_across(k)
+
+        keys, values = heads_ref[16 + h], heads_ref[32 + h]
+        for i in range(3):
+            here = pl.ds(i * BLOCK, BLOCK)
+            scores = dot(heads_ref[h, here, :], keys, NT) * SOFT + bias_ref[here, :]
+            top = jnp.max(scores, axis=1, keepdims=True)
+            weights = jnp.exp2(scores - top)
+            total = jnp.sum(weights, axis=1, keepdims=True)
+            keep = head_keep(mask_ref, h, column_ref[here, :])
+            parts_ref[h, here, :] = (dot(weights.astype(BF16), values) * (keep / total)).astype(BF16)
+            spread = jnp.broadcast_to(top + jnp.log2(total), (BLOCK, 128))
+            lse_ref[h, :, here] = jnp.transpose(spread)[:1, :]
+        return carry
+
+    lax.fori_loop(0, HEADS, head, 0)
+    for h in range(HEADS):
+        mixed_ref[:, HEAD_DIM * h : HEAD_DIM * (h + 1)] = parts_ref[h][:, :HEAD_DIM]
+    for k in range(4):
+        ups.pass_pair(k)
+
+    def close(i, carry):
+        here = rows_at(i)
+        segment = column_ref[here, :]
+        attn = dot(mixed_ref[here, :], out_weight_ref[...]) + out_bias_ref[...]
+        attn_ref[here, :] = attn.astype(BF16)
+        after = x_ref[here, :].astype(F32) + per_crop(mods_ref[2], segment) * attn
+        after_ref[here, :] = after
+        normed, _ = normalise(after)
+        shift, scale = per_crop(mods_ref[3], segment), per_crop(mods_ref[4], segment)
+        second_ref[here, :] = (normed * (1.0 + scale) + shift).astype(BF16)
+        return carry
+
+    lax.fori_loop(0, 3, close, 0)
+    for i in range(2):
+        here = pl.ds(i * BLOCK, BLOCK)
+        choice = places_of(slot_ref[...], i)
+        arrived_ref[here, :] = dot(choice, second_ref[...]).astype(BF16)
+        picked_ref[here, :] = dot(choice, groups_ref[...]).astype(BF16)
+    ups.finish()
+    downs.finish()
+
+
+def shape_of(*shape, dtype=BF16):
+    return jax.ShapeDtypeStruct(shape, dtype)
+
+
+def talking(number):
+    return pltpu.CompilerParams(
+        collective_id=number, has_side_effects=True, vmem_limit_bytes=VMEM_BYTES
+    )
+
+
+IN_VMEM = pl.BlockSpec(memory_space=pltpu.VMEM)
+IN_SMEM = pl.BlockSpec(memory_space=pltpu.SMEM)
+ANYWHERE = pl.BlockSpec(memory_space=pl.ANY)
+
+
+def attend(x, weight, mods, qkv_bias, out_bias, column, row, slot_row, groups, mask, up, down):
+    return pl.pallas_call(
+        attend_kernel,
+        out_shape=[
+            shape_of(TOK_DEV, D),
+            shape_of(3 * HEADS, TOK_DEV, 128),
+            shape_of(TOK_DEV, D),
+            shape_of(HEADS, 1, TOK_DEV, dtype=F32),
+            shape_of(TOK_DEV, D),
+            shape_of(TOK_DEV, D, dtype=F32),
+            shape_of(PLACES, D),
+            shape_of(PLACES, 128),
+            shape_of(D, D),
+            shape_of(2, 2, 4, 2, SHARD, D),
+            shape_of(4, SHARD, D),
+        ],
+        in_specs=[IN_VMEM] * 9 + [IN_SMEM] + [ANYWHERE] * 2,
+        out_specs=[IN_VMEM] * 9 + [ANYWHERE] * 2,
+        scratch_shapes=[
+            pltpu.VMEM((TOK_DEV, TOK_DEV), F32),
+            pltpu.VMEM((HEADS, TOK_DEV, 128), BF16),
+            pltpu.VMEM((TOK_DEV, D), BF16),
+            DMA((SPREAD_COPIES,)),
+            DMA((SPREAD_COPIES,)),
+            DMA((4,)),
+            DMA((3,)),
+            DMA((3,)),
+            DMA((1,)),
+        ],
+        compiler_params=talking(2),
+    )(x, weight, mods, qkv_bias, out_bias, column, row, slot_row, groups, mask, up, down)
+
+
+ROOT = math.sqrt(2.0 / math.pi)
+
+
+def feed_kernel(
+    up_ref, arrived_ref, picked_ref, up_bias_ref, down_bias_ref, cot_ref, after_ref,
+    mods_ref, column_ref, slot_column_ref, slot_row_ref, down_ref,
+    pull_ref, grad_rows_ref, block_out_ref, gate_ref, bias_ref, parts_ref, down_out,
+    active_ref, total_ref, branch_ref, buffers_ref, halves_ref, tiles_ref,
+    send_sems, recv_sems, local_sems, pair_send, pair_recv, tile_sems,
+):
+    step = pl.program_id(0)
+    place = Place()
+    downs = Spread(
+        place, down_ref, lambda y, c, z, x: down_out.at[z, x, y, c], send_sems, recv_sems, local_sems
+    )
+
+    def rows_of(x, y, c):
+        return pl.ds(pl.multiple_of((4 * x + 2 * y + c) * SHARD, 16), SHARD)
+
+    def pair(m, x, y):
+        return pltpu.make_async_remote_copy(
+            src_ref=buffers_ref.at[lax.rem(m, 2), rows_of(x, y, 1 - place.c)],
+            dst_ref=halves_ref.at[y, m, x],
+            send_sem=pair_send.at[m, x, y],
+            recv_sem=pair_recv.at[m, x, y],
+            device_id=place.mates[0],
+            device_id_type=MESH,
+        )
+
+    def take(m):
+        for x in range(2):
+            for y in range(2):
+                pair(m, x, y).wait_recv()
+                own = rows_of(x, y, place.c)
+                mine = buffers_ref.at[lax.rem(m, 2), own]
+                for at in range(0, SHARD, 16):
+                    here = pl.ds(at, 16)
+                    total = mine[here].astype(F32) + halves_ref[y, m, x, here].astype(F32)
+                    parts_ref[y, m, x, here] = total.astype(BF16)
+
+    def free(m):
+        for x in range(2):
+            for y in range(2):
+                pair(m, x, y).wait_send()
+
+    def tile(m):
+        return [
+            pltpu.make_async_copy(
+                down_out.at[m, x, y],
+                tiles_ref.at[lax.rem(m, 2), x, y],
+                tile_sems.at[lax.rem(m, 2), x, y],
+            )
+            for x in range(2)
+            for y in range(2)
+        ]
+
+    @pl.when(step == 0)
+    def _():
+        place.meet()
+        downs.start()
+        for i in range(3):
+            here = pl.ds(i * BLOCK, BLOCK)
+            gate = per_crop(mods_ref[5], column_ref[here, :])
+            block_out_ref[here, :] = (gate * cot_ref[here, :].astype(F32)).astype(BF16)
+        for i in range(2):
+            here = pl.ds(i * BLOCK, BLOCK)
+            choice = places_of(slot_row_ref[...], i)
+            grad_rows_ref[here, :] = dot(choice, block_out_ref[...]).astype(BF16)
+        bias_ref[...] = jnp.sum(grad_rows_ref[...].astype(F32), axis=0, keepdims=True)
+        total_ref[...] = jnp.zeros_like(total_ref)
+
+    @pl.when(step < 4)
+    def _():
+        group = lax.broadcasted_iota(jnp.int32, (128, D), 0) - 4 * step
+        unit = lax.broadcasted_iota(jnp.int32, (128, D), 1)
+        width = FF // GROUPS
+        spread = ((unit >= group * width) & (unit < (group + 1) * width)).astype(BF16)
+        for i in range(2):
+            here = pl.ds(i * BLOCK, BLOCK)
+            hidden = dot(arrived_ref[here, :], up_ref[0]) + up_bias_ref[0]
+            keep = dot(picked_ref[here, :], spread)
+            square = hidden * hidden
+            curve = jnp.tanh(ROOT * hidden * (1.0 + 0.044715 * square))
+            half = 0.5 * (1.0 + curve)
+            slope = half + 0.5 * hidden * (1.0 - curve * curve) * (
+                ROOT * (1.0 + 3.0 * 0.044715 * square)
+            )
+            active_ref[step, here, :] = (hidden * half * keep).astype(BF16)
+            pull_ref[0, here, :] = (slope * keep).astype(BF16)
+
+        def grad(i, carry):
+            here = pl.ds(pl.multiple_of(i * 384, 384), 384)
+            part = dot(active_ref[step, :, here], grad_rows_ref[...], TN).astype(BF16)
+            buffers_ref[lax.rem(step, 2), here, :] = part
+            return carry
+
+        @pl.when(step >= 2)
+        def _():
+            free(step - 2)
+
+        lax.fori_loop(0, 3, grad, 0)
+        for x in range(2):
+            for y in range(2):
+                pair(step, x, y).start()
+
+    @pl.when((step >= 1) & (step < 5))
+    def _():
+        take(step - 1)
+
+    @pl.when(step == 3)
+    def _():
+        for k in range(4):
+            downs.pass_across(k)
+
+    @pl.when(step == 4)
+    def _():
+        free(2)
+        free(3)
+        for k in range(4):
+            downs.pass_pair(k)
+        downs.finish()
+        for m in (0, 1):
+            for copy in tile(m):
+                copy.start()
+
+    @pl.when(step >= 4)
+    def _():
+        m = step - 4
+        for copy in tile(m):
+            copy.wait()
+        weights = tiles_ref[lax.rem(m, 2)].reshape(D, D)
+        for i in range(2):
+            here = pl.ds(i * BLOCK, BLOCK)
+            total_ref[here, :] += dot(active_ref[m, here, :], weights)
+
+        @pl.when(m < 2)
+        def _():
+            for copy in tile(m + 2):
+                copy.start()
+
+    @pl.when(step == 7)
+    def _():
+        branch_ref[...] = (total_ref[...] + down_bias_ref[...]).astype(BF16)
+        gates = jnp.zeros((8, D), F32)
+        for i in range(3):
+            here = pl.ds(i * BLOCK, BLOCK)
+            segment = column_ref[here, :]
+            branch = dot(tokens_of(slot_column_ref[here, :]), branch_ref[...])
+            gate = per_crop(mods_ref[5], segment)
+            block_out_ref[here, :] = (after_ref[here, :] + gate * branch).astype(BF16)
+            gates = gates + crop_sums(segment, cot_ref[here, :].astype(F32) * branch)
+        gate_ref[...] = gates
+
+
+def whole(*shape):
+    return pl.BlockSpec(shape, lambda i: (0,) * len(shape), pipeline_mode=pl.Buffered(1))
+
+
+def feed(up, arrived, picked, up_bias, down_bias, cot, after, mods, column, slot_column, slot_row, down):
+    early = lambda *tail: pl.BlockSpec((1, *tail), lambda i: (jnp.minimum(i, 3), 0, 0))
+    return pl.pallas_call(
+        feed_kernel,
+        grid=(8,),
+        out_shape=[
+            shape_of(4, PLACES, D),
+            shape_of(PLACES, D),
+            shape_of(TOK_DEV, D),
+            shape_of(8, D, dtype=F32),
+            shape_of(1, D, dtype=F32),
+            shape_of(2, 4, 2, SHARD, D),
+            shape_of(4, 2, 2, 2, SHARD, D),
+        ],
+        in_specs=[
+            early(D, D), whole(PLACES, D), whole(PLACES, 128), early(1, D), whole(1, D),
+            whole(TOK_DEV, D), whole(TOK_DEV, D), whole(6, 8, D), whole(TOK_DEV, 1), whole(TOK_DEV, 1),
+            whole(1, TOK_DEV), ANYWHERE,
+        ],
+        out_specs=[
+            early(PLACES, D), whole(PLACES, D), whole(TOK_DEV, D), whole(8, D), whole(1, D),
+            whole(2, 4, 2, SHARD, D), ANYWHERE,
+        ],
+        scratch_shapes=[
+            pltpu.VMEM((4, PLACES, D), BF16),
+            pltpu.VMEM((PLACES, D), F32),
+            pltpu.VMEM((PLACES, D), BF16),
+            pltpu.VMEM((2, D, D), BF16),
+            pltpu.VMEM((2, 4, 2, SHARD, D), BF16),
+            pltpu.VMEM((2, 2, 2, 2, SHARD, D), BF16),
+            DMA((SPREAD_COPIES,)),
+            DMA((SPREAD_COPIES,)),
+            DMA((4,)),
+            DMA((4, 2, 2)),
+            DMA((4, 2, 2)),
+            DMA((2, 2, 2)),
+        ],
+        compiler_params=talking(3),
+    )(up, arrived, picked, up_bias, down_bias, cot, after, mods, column, slot_column, slot_row, down)
+
+
+def unfeed_kernel(
+    down_ref, up_ref, pull_ref, grad_rows_ref, arrived_ref, after_ref, cot_ref, attn_ref, mods_ref,
+    column_ref, slot_column_ref, given_ref,
+    up_bias_ref, mid_ref, grad_attn_ref, sums_ref, out_bias_ref, parts_out, plane_ref,
+    hidden_ref, total_ref, back_ref, buffers_ref, parts_ref, bufs_ref,
+    send_sems, recv_sems, pair_send, pair_recv, out_sem,
+):
+    step = pl.program_id(0)
+    place = Place()
+    scatter = Scatter(place, given_ref, bufs_ref, plane_ref, send_sems, recv_sems)
+    pair = Pair(place, buffers_ref, parts_ref, pair_send, pair_recv)
+
+    @pl.when(step == 0)
+    def _():
+        place.meet()
+        for k in ORDER:
+            scatter.start(k)
+        total_ref[...] = jnp.zeros_like(total_ref)
+
+    bias = jnp.zeros((1, D), F32)
+    for i in range(2):
+        here = pl.ds(i * BLOCK, BLOCK)
+        grad = dot(grad_rows_ref[here, :], down_ref[0], NT) * pull_ref[0, here, :].astype(F32)
+        low = grad.astype(BF16)
+        hidden_ref[here, :] = low
+        bias = bias + jnp.sum(low.astype(F32), axis=0, keepdims=True)
+        total_ref[here, :] += dot(low, up_ref[0], NT)
+    up_bias_ref[0] = bias
+
+    def grad_of(i, carry):
+        here = pl.ds(pl.multiple_of(i * 384, 384), 384)
+        part = dot(arrived_ref[:, here], hidden_ref[...], TN).astype(BF16)
+        buffers_ref[lax.rem(step, 2), here, :] = part
+        return carry
+
+    @pl.when(step >= 2)
+    def _():
+        pair.free(step - 2)
+
+    lax.fori_loop(0, 3, grad_of, 0)
+    pair.send(step)
+
+    @pl.when(step >= 1)
+    def _():
+        pair.take(step - 1)
+
+    @pl.when(step == 0)
+    def _():
+        for k in ORDER:
+            scatter.follow(k)
+
+    for here_step, ks in ((1, (1, 2)), (2, (3, 0))):
+
+        @pl.when(step == here_step)
+        def _():
+            for k in ks:
+                scatter.pass_across(k)
+
+    @pl.when(step == 3)
+    def _():
+        back_ref[...] = total_ref[...].astype(BF16)
+        shifts, scales = jnp.zeros((8, D), F32), jnp.zeros((8, D), F32)
+        gates, out_bias = jnp.zeros((8, D), F32), jnp.zeros((1, D), F32)
+        for i in range(3):
+            here = pl.ds(i * BLOCK, BLOCK)
+            segment = column_ref[here, :]
+            second = dot(tokens_of(slot_column_ref[here, :]), back_ref[...])
+            normed, inverse = normalise(after_ref[here, :])
+            grad = second * (1.0 + per_crop(mods_ref[4], segment))
+            mean = jnp.mean(grad, axis=1, keepdims=True)
+            slant = jnp.mean(grad * normed, axis=1, keepdims=True)
+            mid = cot_ref[here, :].astype(F32) + inverse * (grad - mean - normed * slant)
+            mid_ref[here, :] = mid
+            low = (per_crop(mods_ref[2], segment) * mid).astype(BF16)
+            grad_attn_ref[here, :] = low
+            out_bias = out_bias + jnp.sum(low.astype(F32), axis=0, keepdims=True)
+            shifts = shifts + crop_sums(segment, second)
+            scales = scales + crop_sums(segment, second * normed)
+            gates = gates + crop_sums(segment, mid * attn_ref[here, :].astype(F32))
+        sums_ref[0], sums_ref[1], sums_ref[2] = gates, shifts, scales
+        out_bias_ref[...] = out_bias
+        pair.free(2)
+        pair.free(3)
+        pair.take(3)
+        leave = pltpu.make_async_copy(parts_ref, parts_out, out_sem.at[0])
+        leave.start()
+        for k in ORDER:
+            scatter.collect(k)
+        scatter.finish()
+        leave.wait()
+
+
+def unfeed(down, up, pull, grad_rows, arrived, after, cot, attn, mods, column, slot_column, given):
+    block = lambda *tail: pl.BlockSpec((1, *tail), lambda i: (i, 0, 0))
+    return pl.pallas_call(
+        unfeed_kernel,
+        grid=(4,),
+        out_shape=[
+            shape_of(4, 1, D, dtype=F32),
+            shape_of(TOK_DEV, D, dtype=F32),
+            shape_of(TOK_DEV, D),
+            shape_of(3, 8, D, dtype=F32),
+            shape_of(1, D, dtype=F32),
+            shape_of(2, D, D),
+            shape_of(4, SHARD, D),
+        ],
+        in_specs=[
+            block(D, D), block(D, D), block(PLACES, D), whole(PLACES, D), whole(PLACES, D),
+            whole(TOK_DEV, D), whole(TOK_DEV, D), whole(TOK_DEV, D), whole(6, 8, D), whole(TOK_DEV, 1),
+            whole(TOK_DEV, 1), whole(2, 4, 2, SHARD, D),
+        ],
+        out_specs=[
+            block(1, D), whole(TOK_DEV, D), whole(TOK_DEV, D), whole(3, 8, D), whole(1, D), ANYWHERE, whole(4, SHARD, D),
+        ],
+        scratch_shapes=[
+            pltpu.VMEM((PLACES, D), BF16),
+            pltpu.VMEM((PLACES, D), F32),
+            pltpu.VMEM((PLACES, D), BF16),
+            pltpu.VMEM((2, D, D), BF16),
+            pltpu.VMEM((2, D, D), BF16),
+            pltpu.VMEM((4, 4, SHARD, D), BF16),
+            DMA((SCATTER_COPIES,)),
+            DMA((SCATTER_COPIES,)),
+            DMA((2,)),
+            DMA((2,)),
+            DMA((1,)),
+        ],
+        compiler_params=talking(4),
+    )(down, up, pull, grad_rows, arrived, after, cot, attn, mods, column, slot_column, given)
+
+
+def unattend_kernel(
+    grad_ref, out_weight_ref, heads_ref, lse_ref, column_ref, row_ref, given_ref, plane_ref, mask_ref,
+    triple_ref, sums_ref, share_ref, plane_out, split_ref,
+    bias_ref, mixed_ref, grads_ref, key_ref, value_ref, bufs_ref, from_z_ref,
+    send_sems, recv_sems, along_send, along_recv,
+):
+    place = Place()
+    place.meet()
+    scatter = Scatter(place, given_ref, bufs_ref, plane_out, send_sems, recv_sems)
+    along = Along(place, plane_ref, from_z_ref, share_ref, along_send, along_recv)
+    for k in ORDER:
+        scatter.start(k)
+    for k in (1, 2, 3):
+        along.start(k)
+    crop_mask(bias_ref, column_ref, row_ref)
+
+    def spread(i, carry):
+        here = rows_at(i)
+        segment = column_ref[here, :]
+        mixed = dot(grad_ref[here, :], out_weight_ref[...], NT)
+        zero = jnp.zeros((BLOCK, 128 - HEAD_DIM), BF16)
+        for h in range(HEADS):
+            part = mixed[:, HEAD_DIM * h : HEAD_DIM * (h + 1)] * head_keep(mask_ref, h, segment)
+            mixed_ref[h, here, :] = jnp.concatenate([part.astype(BF16), zero], axis=1)
+        return carry
+
+    lax.fori_loop(0, 3, spread, 0)
+    factor = HEAD_DIM**-0.5
+
+    def head(h, carry):
+        @pl.when(h == 1)
+        def _():
+            for k in ORDER:
+                scatter.follow(k)
+
+        for at, k in enumerate(ORDER):
+
+            @pl.when(h == 4 + at)
+            def _():
+                scatter.pass_across(k)
+
+        keys, values = heads_ref[16 + h], heads_ref[32 + h]
+        turned = jnp.transpose(keys)
+        for i in range(3):
+            here = pl.ds(i * BLOCK, BLOCK)
+            queries, grads = heads_ref[h, here, :], mixed_ref[h, here, :]
+            scores = dot(keys, queries, NT) * SOFT + bias_ref[:, here]
+            probs = jnp.exp2(scores - lse_ref[h, :, here])
+            product = probs * dot(values, grads, NT)
+            total = jnp.sum(product, axis=0, keepdims=True)
+            low = (product - probs * total).astype(BF16)
+            for_values, for_keys = dot(probs.astype(BF16), grads), dot(low, queries)
+            if i == 0:
+                value_ref[...], key_ref[...] = for_values, for_keys
+            else:
+                value_ref[...] += for_values
+                key_ref[...] += for_keys
+            grads_ref[h, here, :] = jnp.transpose(dot(turned, low) * factor).astype(BF16)
+        grads_ref[16 + h] = (key_ref[...] * factor).astype(BF16)
+        grads_ref[32 + h] = value_ref[...].astype(BF16)
+        return carry
+
+    lax.fori_loop(0, HEADS, head, 0)
+    for j in range(4):
+        triple_ref[j, :, QKV_SHARD:] = jnp.zeros((TOK_DEV, PAD_SHARD - QKV_SHARD), BF16)
+        for h in range(12):
+            triple_ref[j, :, HEAD_DIM * h : HEAD_DIM * (h + 1)] = grads_ref[12 * j + h][:, :HEAD_DIM]
+        sums_ref[j] = jnp.sum(triple_ref[j].astype(F32), axis=0, keepdims=True)
+    for j in range(4):
+        split_ref[j] = grad_ref[:, OUT_SHARD * j : OUT_SHARD * (j + 1)]
+    along.close()
+    for k in ORDER:
+        scatter.collect(k)
+    scatter.finish()
+
+
+def unattend(grad_attn, out_weight, heads, lse, column, row, given, plane, mask):
+    return pl.pallas_call(
+        unattend_kernel,
+        out_shape=[
+            shape_of(4, TOK_DEV, PAD_SHARD),
+            shape_of(4, 1, PAD_SHARD, dtype=F32),
+            shape_of(SHARD, D, dtype=F32),
+            shape_of(4, SHARD, D),
+            shape_of(4, TOK_DEV, OUT_SHARD),
+        ],
+        in_specs=[IN_VMEM] * 8 + [IN_SMEM],
+        out_specs=[IN_VMEM] * 5,
+        scratch_shapes=[
+            pltpu.VMEM((TOK_DEV, TOK_DEV), F32),
+            pltpu.VMEM((HEADS, TOK_DEV, 128), BF16),
+            pltpu.VMEM((3 * HEADS, TOK_DEV, 128), BF16),
+            pltpu.VMEM((TOK_DEV, 128), F32),
+            pltpu.VMEM((TOK_DEV, 128), F32),
+            pltpu.VMEM((4, 4, SHARD, D), BF16),
+            pltpu.VMEM((3, SHARD, D), BF16),
+            DMA((SCATTER_COPIES,)),
+            DMA((SCATTER_COPIES,)),
+            DMA((3,)),
+            DMA((3,)),
+        ],
+        compiler_params=talking(5),
+    )(grad_attn, out_weight, heads, lse, column, row, given, plane, mask)
+
+
+def unproject_kernel(
+    weight_ref, triple_ref, split_ref, first_ref, mixed_ref, x_ref, mid_ref, mods_ref, column_ref,
+    plane_up_ref, rest_ref, conds_ref,
+    grad_in_ref, share_up_ref, share_ref, ada_ref, sums_ref,
+    total_ref, buffers_ref, parts_ref, bufs_ref, plane_ref, up_z_ref, from_z_ref,
+    mod_ref, mates_ref, packed_ref, every_ref,
+    send_sems, recv_sems, pair_send, pair_recv, up_send, up_recv, along_send, along_recv,
+    small_send, small_recv,
+):
+    step = pl.program_id(0)
+    place = Place()
+    pair = Pair(place, buffers_ref, parts_ref, pair_send, pair_recv)
+    blocks = parts_ref.reshape(2, 4, 2, SHARD, D)
+    scatter = Scatter(place, blocks, bufs_ref, plane_ref, send_sems, recv_sems)
+    along_up = Along(place, plane_up_ref, up_z_ref, share_up_ref, up_send, up_recv)
+    along = Along(place, plane_ref, from_z_ref, share_ref, along_send, along_recv)
+    small = Copies(small_send, small_recv)
+    to_mates = [
+        small.make(mod_ref.at[other], mates_ref.at[place.index], mate)
+        for other, mate in zip(place.mate_index, place.mates)
+    ]
+    to_z = [
+        small.make(packed_ref, every_ref.at[place.peer], place.device(z=place.zs[k]))
+        for k in (1, 2, 3)
+    ]
+    to_x = []
+    for k in range(4):
+        held = every_ref.at[2 * place.zs[k] + place.x]
+        to_x.append(small.make(held, held, place.device(x=1 - place.x)))
+
+    @pl.when(step == 0)
+    def _():
+        place.meet()
+        for k in (1, 2, 3):
+            along_up.start(k)
+
+    @pl.when(step < 4)
+    def _():
+        def grad(i, carry):
+            here = pl.ds(pl.multiple_of(i * 384, 384), 384)
+            buffer = lax.rem(step, 2)
+            part = dot(first_ref[:, here], triple_ref[0], TN).astype(BF16)
+            buffers_ref[buffer, here, :PAD_SHARD] = part
+            part = dot(mixed_ref[:, here], split_ref[0], TN).astype(BF16)
+            buffers_ref[buffer, here, QKV_SHARD:] = part
+            return carry
+
+        @pl.when(step >= 2)
+        def _():
+            pair.free(step - 2)
+
+        lax.fori_loop(0, 3, grad, 0)
+        pair.send(step)
+
+    @pl.when((step >= 1) & (step < 5))
+    def _():
+        pair.take(step - 1)
+
+    @pl.when(step == 4)
+    def _():
+        pair.free(2)
+        pair.free(3)
+        for k in ORDER:
+            scatter.start(k)
+
+    @pl.when(step == 5)
+    def _():
+        for k in ORDER:
+            scatter.follow(k)
+
+    @pl.when(step >= 4)
+    def _():
+        for i in range(3):
+            here = pl.ds(i * BLOCK, BLOCK)
+            part = dot(triple_ref[0, here, :], weight_ref[0, :, :PAD_SHARD], NT)
+            total_ref[here, :] = jnp.where(step == 4, part, total_ref[here, :] + part)
+
+    @pl.when(step == 7)
+    def _():
+        for k in ORDER[:2]:
+            scatter.pass_across(k)
+        shifts, scales = jnp.zeros((8, D), F32), jnp.zeros((8, D), F32)
+        for i in range(3):
+            here = pl.ds(i * BLOCK, BLOCK)
+            segment = column_ref[here, :]
+            first = total_ref[here, :]
+            normed, inverse = normalise(x_ref[here, :].astype(F32))
+            grads = first * (1.0 + per_crop(mods_ref[1], segment))
+            mean = jnp.mean(grads, axis=1, keepdims=True)
+            slant = jnp.mean(grads * normed, axis=1, keepdims=True)
+            grad_in_ref[here, :] = mid_ref[here, :] + inverse * (grads - mean - normed * slant)
+            shifts = shifts + crop_sums(segment, first)
+            scales = scales + crop_sums(segment, first * normed)
+        mod_ref[...] = rest_ref[...]
+        mod_ref[0, :CROPS, :D] = shifts[:CROPS]
+        mod_ref[0, :CROPS, D:] = scales[:CROPS, : D // 2]
+        mod_ref[1, :CROPS, : D // 2] = scales[:CROPS, D // 2 :]
+        for copy in to_mates:
+            copy.start()
+        mates_ref[place.index] = mod_ref[place.index]
+        for k in ORDER[2:]:
+            scatter.pass_across(k)
+        for copy in to_mates:
+            copy.wait_recv()
+        packed_ref[...] = jnp.zeros_like(packed_ref)
+        for j in range(4):
+            packed_ref[CROPS * j : CROPS * (j + 1), :] = mates_ref[j, :CROPS, :]
+            packed_ref[12:14, :] += mates_ref[j, CROPS : CROPS + 2, :]
+        for copy in to_z:
+            copy.start()
+        every_ref[place.peer] = packed_ref[...]
+        along_up.close()
+        for copy in to_z:
+            copy.wait_recv()
+        for copy in to_x:
+            copy.start()
+        for k in ORDER[:3]:
+            scatter.collect(k)
+            along.start(k)
+        for copy in to_x:
+            copy.wait_recv()
+        close_ada(conds_ref, every_ref, ada_ref, sums_ref)
+        scatter.collect(0)
+        along.close()
+        scatter.finish()
+        for copy in small.made:
+            copy.wait_send()
+
+
+def unproject(weight, triple, split, first, mixed, x, mid, mods, column, plane_up, rest, conds):
+    block = lambda *tail: pl.BlockSpec((1, *tail), lambda i: (lax.rem(i, 4), 0, 0))
+    early = lambda *tail: pl.BlockSpec((1, *tail), lambda i: (jnp.minimum(i, 3), 0, 0))
+    late = lambda *tail: pl.BlockSpec((1, *tail), lambda i: (jnp.maximum(i - 4, 0), 0, 0))
+    wide = rest.shape[2]
+    vmem = pltpu.VMEM
+    return pl.pallas_call(
+        unproject_kernel,
+        grid=(8,),
+        out_shape=[
+            shape_of(TOK_DEV, D, dtype=F32),
+            shape_of(SHARD, D, dtype=F32),
+            shape_of(SHARD, D, dtype=F32),
+            shape_of(SHARD, wide, dtype=F32),
+            shape_of(8, wide, dtype=F32),
+        ],
+        in_specs=[
+            late(D, D), block(TOK_DEV, PAD_SHARD), early(TOK_DEV, OUT_SHARD), whole(TOK_DEV, D),
+            whole(TOK_DEV, D), whole(TOK_DEV, D), whole(TOK_DEV, D), whole(6, 8, D), whole(TOK_DEV, 1),
+            whole(4, SHARD, D), whole(4, 8, wide), whole(8, 16, 256),
+        ],
+        out_specs=[
+            whole(TOK_DEV, D), whole(SHARD, D), whole(SHARD, D), whole(SHARD, wide), whole(8, wide),
+        ],
+        scratch_shapes=[
+            vmem((TOK_DEV, D), F32),
+            vmem((2, D, D), BF16),
+            vmem((2, D, D), BF16),
+            vmem((4, 4, SHARD, D), BF16),
+            vmem((4, SHARD, D), BF16),
+            vmem((3, SHARD, D), BF16),
+            vmem((3, SHARD, D), BF16),
+            vmem((4, 8, wide), F32),
+            vmem((4, 8, wide), F32),
+            vmem((16, wide), F32),
+            vmem((8, 16, wide), F32),
+            DMA((SCATTER_COPIES,)),
+            DMA((SCATTER_COPIES,)),
+            DMA((2,)),
+            DMA((2,)),
+            DMA((3,)),
+            DMA((3,)),
+            DMA((3,)),
+            DMA((3,)),
+            DMA((10,)),
+            DMA((10,)),
+        ],
+        compiler_params=talking(6),
+    )(weight, triple, split, first, mixed, x, mid, mods, column, plane_up, rest, conds)
+
+
+CROPS = 3
+
+
+def gather_kernel(
+    mixed_ref, up_ref, cond_ref, ada_ref, ada_bias_ref, bias_ref,
+    mixed_out, up_out, mods_ref, biases_ref, conds_ref,
+    send_sems, recv_sems, local_sem, up_send, up_recv, up_local, small_send, small_recv, local_small,
+    all_cond, own_cond, partial_ref, from_x, from_z, column_ref,
+):
+    place = Place()
+    place.meet()
+    x, zs = place.x, place.zs
+
+    first = Gather(
+        place,
+        mixed_ref,
+        lambda y, c, z, x: mixed_out.at[y, c, z, x],
+        send_sems,
+        recv_sems,
+        local_sem.at[0],
+        False,
+    )
+    ups = Column(place, up_ref, up_out, up_send, up_recv, up_local.at[0])
+    small = Copies(small_send, small_recv)
+    to_mates = [small.make(cond_ref, all_cond.at[place.index], mate) for mate in place.mates]
+    to_mates += [small.make(bias_ref, biases_ref.at[place.index], mate) for mate in place.mates]
+    others = [(k, far) for k in range(4) for far in (0, 1) if k or far]
+    to_peers = []
+    for k, far in others:
+        there = 1 - x if far else x
+        to_peers.append(
+            small.make(
+                own_cond.at[2 * zs[k] + there],
+                conds_ref.at[place.peer],
+                place.device(z=zs[k], x=there),
+            )
+        )
+    over_x = [
+        small.make(partial_ref.at[2 * zs[k] + 1 - x], from_x.at[k], place.device(x=1 - x))
+        for k in range(4)
+    ]
+    along = [
+        small.make(partial_ref.at[2 * zs[k] + x], from_z.at[k - 1], place.device(z=zs[k]))
+        for k in (1, 2, 3)
+    ]
+    finals = [
+        small.make(column_ref.at[other], mods_ref.at[place.index], mate)
+        for other, mate in zip(place.mate_index, place.mates)
+    ]
+    own_bias = pltpu.make_async_copy(bias_ref, biases_ref.at[place.index], local_small.at[0])
+
+    for copy in to_mates:
+        copy.start()
+    own_bias.start()
+    first.start()
+    all_cond[place.index] = cond_ref[...]
+    own_cond[...] = jnp.zeros_like(own_cond)
+    for copy in to_mates:
+        copy.wait_recv()
+    for j in range(4):
+        own_cond[:, CROPS * j : CROPS * (j + 1), :] = all_cond[j, :, :CROPS, :]
+    for copy in to_peers:
+        copy.start()
+    conds_ref[place.peer] = own_cond[place.peer]
+    first.pass_along(1)
+    for copy in to_peers:
+        copy.wait_recv()
+    for i in range(8):
+        partial_ref[i] = dot(conds_ref[i][:, :SHARD].astype(BF16), ada_ref[...])
+    for copy in over_x:
+        copy.start()
+    first.pass_along(2)
+    first.pass_along(3)
+    for k in range(4):
+        over_x[k].wait_recv()
+        partial_ref[2 * zs[k] + x] += from_x[k]
+    for copy in along:
+        copy.start()
+    for k in range(2):
+        first.pass_across(k)
+    for copy in along:
+        copy.wait_recv()
+    total = partial_ref[place.peer] + from_z[0] + from_z[1] + from_z[2] + ada_bias_ref[...]
+    column_ref[...] = jnp.zeros_like(column_ref)
+    for j in range(4):
+        column_ref[j, :CROPS, :] = total[CROPS * j : CROPS * (j + 1)]
+    for copy in finals:
+        copy.start()
+    mods_ref[place.index] = column_ref[place.index]
+    for k in range(2, 4):
+        first.pass_across(k)
+    ups.start()
+    for k in range(4):
+        first.pass_pair(k)
+    for copy in finals:
+        copy.wait_recv()
+    own_bias.wait()
+    first.finish()
+    ups.finish()
+    for copy in small.made:
+        copy.wait_send()
+
+
+def gather_all(mixed, up, cond, ada, ada_bias, bias):
+    vmem = pltpu.VMEM
+    wide = ada.shape[1]
+    return pl.pallas_call(
+        gather_kernel,
+        out_shape=[shape_of(2, 2, 4, 2, SHARD, D), shape_of(4, SHARD, D)]
+        + [shape_of(4, 8, wide, dtype=F32), shape_of(4, 32, 128), shape_of(8, 16, 256, dtype=F32)],
+        in_specs=[ANYWHERE] * 2 + [IN_VMEM] * 4,
+        out_specs=[ANYWHERE] * 2 + [IN_VMEM] * 3,
+        scratch_shapes=[DMA((GATHER_COPIES,))] * 2
+        + [DMA((1,)), DMA((3,)), DMA((3,)), DMA((1,)), DMA((23,)), DMA((23,)), DMA((1,))]
+        + [
+            vmem((4, 8, 8, 256), F32),
+            vmem((8, 16, 256), F32),
+            vmem((8, 16, wide), F32),
+            vmem((4, 16, wide), F32),
+            vmem((3, 16, wide), F32),
+            vmem((4, 8, wide), F32),
+        ],
+        compiler_params=pltpu.CompilerParams(
+            collective_id=1, has_side_effects=True, vmem_limit_bytes=VMEM_BYTES
+        ),
+    )(mixed, up, cond, ada, ada_bias, bias)
+
+
+def close_ada(conds_ref, every, ada_ref, sums_ref):
+    total = jnp.zeros(ada_ref.shape, F32)
+    rows = jnp.zeros((16, ada_ref.shape[1]), F32)
+    for i in range(0, 8, 2):
+        rows = rows + every[i] + every[i + 1]
+        cond = jnp.concatenate([conds_ref[i][:, :SHARD], conds_ref[i + 1][:, :SHARD]], axis=0)
+        rest = jnp.concatenate([every[i], every[i + 1]], axis=0)
+        for _ in range(3):
+            part = rest.astype(BF16)
+            total = total + dot(cond.astype(BF16), part, TN)
+            rest = rest - part.astype(F32)
+    ada_ref[...] = total
+    sums_ref[...] = jnp.zeros_like(sums_ref)
+    sums_ref[0:1, :] = jnp.sum(rows[:12], axis=0, keepdims=True)
+    sums_ref[1:3, :] = rows[12:14]
+
+
+def block_shards(
+    block_in, condition, lengths, head_mask, group_mask, buffer_slot, ada_weight, ada_bias, qkv_weight,
+    query_bias, value_bias, out_weight, out_bias, up_weight, up_bias, down_weight, down_bias, cotangent,
+):
+    x, cot = block_in[0], cotangent[0]
+    finish = jnp.cumsum(lengths[0])
+    position = jnp.arange(TOK_DEV, dtype=jnp.int32)
+    segment = jnp.sum((position[:, None] >= finish[None, :]).astype(jnp.int32), axis=1)
+    column, row = segment[:, None], segment[None, :]
+    slot = buffer_slot[0].astype(jnp.int32)
+    slot_column, slot_row = slot[:, None], slot[None, :]
+    mask = head_mask[0].T.astype(F32)
+    chosen = (segment[:, None] == jnp.arange(CROPS)[None, :])[:, :, None]
+    groups = jnp.sum(jnp.where(chosen, group_mask[0].astype(F32)[None], 0.0), axis=1)
+    groups = jnp.pad(groups, ((0, 0), (0, 128 - GROUPS))).astype(BF16)
+    cond = jax.nn.silu(condition[0].astype(F32)).astype(BF16).astype(F32)
+    cond = cond.reshape(CROPS, 8, SHARD).transpose(1, 0, 2)
+    cond = jnp.pad(cond, ((0, 0), (0, 8 - CROPS), (0, 256 - SHARD)))
+    vectors = jnp.concatenate([query_bias, value_bias, out_bias, up_bias, down_bias])
+    packed = jnp.pad(vectors.reshape(18, 128), ((0, 14), (0, 0)))
+    down_rows = lax.all_to_all(down_weight, "fsdp", split_axis=0, concat_axis=1, tiled=True)
+    mixed_block = jnp.concatenate([qkv_weight, out_weight], axis=1)
+    mixed_weight, up_column, mods, biases, conds = gather_all(
+        mixed_block, up_weight, cond, ada_weight, ada_bias.astype(F32)[None], packed
+    )
+    mixed_weight = mixed_weight.reshape(4, D, D)
+    mods = mods.transpose(1, 0, 2).reshape(8, 6, D).transpose(1, 0, 2)
+    biases = biases[:, :18].reshape(4, 2304).astype(F32)
+    edges = (0, 288, 576, 864, 2016, 2304)
+    bias_query, bias_value, bias_out, bias_up, bias_down = [
+        biases[:, low:high].reshape(1, -1) for low, high in zip(edges[:-1], edges[1:])
+    ]
+    qkv_bias = jnp.concatenate([bias_query, jnp.zeros_like(bias_query), bias_value], axis=1)
+    qkv_bias = jnp.pad(qkv_bias.reshape(4, 1, QKV_SHARD), ((0, 0), (0, 0), (0, PAD_SHARD - QKV_SHARD)))
+    first, heads, mixed, lse, attn, after, arrived, picked, full_out, up, down_column = attend(
+        x, mixed_weight, mods, qkv_bias, bias_out, column, row, slot_row, groups, mask, up_column,
+        down_rows,
+    )
+    up = up.reshape(4, D, D)
+    pull, grad_rows, block_out, gate_two, grad_down_bias, parts_down, down = feed(
+        up, arrived, picked, bias_up.reshape(4, 1, D), bias_down, cot, after, mods, column,
+        slot_column, slot_row, down_column,
+    )
+    down = down.reshape(4, D, D)
+    grad_up_bias, mid, grad_attn, sums, grad_out_bias, parts_up, plane_down = unfeed(
+        down, up, pull, grad_rows, arrived, after, cot, attn, mods, column, slot_column, parts_down
+    )
+    triple, triple_sums, share_down, plane_up, grad_split = unattend(
+        grad_attn, full_out, heads, lse, column, row, parts_up.reshape(2, 4, 2, SHARD, D), plane_down,
+        mask,
+    )
+    triple_sums = triple_sums[:, 0, :QKV_SHARD].reshape(3 * D)
+    blank = jnp.zeros((8, 2 * D), F32)
+    mod_grads = jnp.concatenate([blank, sums[0], sums[1], sums[2], gate_two], axis=1)[:CROPS]
+    mod_grads = mod_grads.reshape(CROPS, 4, -1).transpose(1, 0, 2)
+    bias_grads = (
+        triple_sums[:D], triple_sums[2 * D :], grad_out_bias, grad_up_bias, grad_down_bias,
+    )
+    bias_grads = jnp.concatenate([vector.reshape(4, -1) for vector in bias_grads], axis=1)
+    wide = mod_grads.shape[2]
+    bias_grads = jnp.pad(bias_grads, ((0, 0), (0, 5 * wide - 2304))).reshape(4, 5, wide)
+    rest = jnp.concatenate([mod_grads, bias_grads], axis=1)
+    grad_in, share_up, share_mixed, grad_ada, totals = unproject(
+        mixed_weight, triple, grad_split, first, mixed, x, mid, mods, column, plane_up, rest, conds
+    )
+    share_down = lax.all_to_all(share_down, "fsdp", split_axis=1, concat_axis=0, tiled=True)
+    bias_totals = totals[1:3].reshape(-1)
+    grad_query, grad_value, grad_out, grad_ups, grad_downs = [
+        bias_totals[low:high] for low, high in zip(edges[:-1], edges[1:])
+    ]
+    return (
+        block_out[None],
+        grad_in[None],
+        grad_ada,
+        totals[0],
+        share_mixed[:, :QKV_SHARD],
+        grad_query,
+        grad_value,
+        share_mixed[:, QKV_SHARD:],
+        grad_out,
+        share_up,
+        grad_ups,
+        share_down,
+        grad_downs,
+    )
 
 
 def layer_norm(values):
@@ -337,8 +1728,9 @@
         P("fsdp"),
         P(("dp", "fsdp"), None, None),
     )
+    on_block = dict(mesh.shape) == {"dp": 8, "fsdp": 4}
     return jax.shard_map(
-        shards,
+        block_shards if on_block else shards,
         mesh=mesh,
         in_specs=placed,
         out_specs=(

time: 1170 us -> 527 us (0.45)
  the two profiles are of different devices: /device:TPU:9 before, /device:TPU:8 now
where the time goes in v4:
time: 527 us; the launch traced here: 518 us
  Pallas kernels  466 us (88%)
  local copies, waits for them, and re-layouts  39.2 us (7%)
  starting transfers between devices  7.22 us (1%)
    pallas_call x1, Pallas kernels, unproject(): pl.pallas_call(unproject_kernel, grid=(8,), out_shape=[shape_of(TOK_DEV,...  117 us
    pallas_call x1, Pallas kernels, gather_all(): pl.pallas_call(gather_kernel, out_shape=[shape_of(2, 2, 4, 2, SHARD, D),...  96.1 us
    pallas_call x1, Pallas kernels, feed(): pl.pallas_call(feed_kernel, grid=(8,), out_shape=[shape_of(4, PLACES, D),...  68.2 us
    pallas_call x1, Pallas kernels, attend(): pl.pallas_call(attend_kernel, out_shape=[shape_of(TOK_DEV, D), shape_of(3...  66 us
    pallas_call x1, Pallas kernels, unfeed(): pl.pallas_call(unfeed_kernel, grid=(4,), out_shape=[shape_of(4, 1, D, dty...  60.3 us
    pallas_call x1, Pallas kernels, unattend(): pl.pallas_call(unattend_kernel, out_shape=[shape_of(4, TOK_DEV, PAD_SHARD...  58.8 us
    unnamed x49, local copies, waits for them, and re-layouts  14.9 us
  transfers between devices with their start and end apart: 2, of which 0 were waited for; matrix products, arithmetic and copies ran while one was open for 4% of the time, Pallas kernels for 41%

profile of v4, /device:TPU:8, one launch (start us, length us, event | category | flops | bytes accessed | tf_op | source)
XLA Modules:
  0.0 518.2 jit_solution(9289741366310655644)
XLA Ops:
  0.7 2.0 copy.77
  2.8 3.5 all-to-all-start
  6.2 0.8 reduce-window.8
  7.2 0.9 broadcast_in_dim.64.column_ref
  8.7 0.8 reshape.161
  10.2 1.3 reshape.162.ada_bias_ref
  11.5 0.8 pad_maximum_fusion.mixed_ref
  13.0 96.1 %shard_map.273 = (bf16[2,2,4,2,144,1152]{5,4,3,2,1,0:T(8,128)(2,1)}, bf16[4,144,1152]{2,1,0:T(8,128)(2,1)}, f32[4,8,1728]{2,1,0:T(8,128)}, bf16[4,32,128]{2,1,0:T(8,128)(2,1)}, f32[8,16,256]{2,1,0:T(8,128)}) custom-call(bf16[144,1152]{1,0:T(8,128)(2,1)} %pad_maximum_fusion.mixed_ref, bf16[144,1152]{1,0:T(8,128)(2,1)} %up_ref.1, ...), custom_call_target="tpu_custom_call" | custom-call | tf_op jit(solution)/shard_map/pallas_call | solution.py:1283
  111.7 1.0 copy.73
  116.7 0.9 copy.81.slot_column_ref
  117.8 1.0 all_to_all.31.down_ref
  118.8 66.0 %shard_map.274 = (bf16[768,1152]{1,0:T(8,128)(2,1)}, bf16[48,768,128]{2,1,0:T(8,128)(2,1)}, bf16[768,1152]{1,0:T(8,128)(2,1)}, f32[16,1,768]{2,1,0:T(1,128)}, bf...) custom-call(bf16[768,1152]{1,0:T(8,128)(2,1)} %bitcast.51, ...), custom_call_target="tpu_custom_call" | custom-call | tf_op jit(solution)/shard_map/pallas_call | solution.py:530
  184.8 68.2 %shard_map.275 = (bf16[4,512,1152]{2,1,0:T(8,128)(2,1)}, bf16[512,1152]{1,0:T(8,128)(2,1)}, bf16[768,1152]{1,0:T(8,128)(2,1)}, f32[8,1152]{1,0:T(8,128)}, f32[1,...) custom-call(bf16[4,1152,1152]{2,1,0:T(8,128)(2,1)} %bitcast.48, ...), custom_call_target="tpu_custom_call" | custom-call | tf_op jit(solution)/shard_map/pallas_call | solution.py:722
  253.1 60.3 %shard_map.276 = (f32[4,1,1152]{2,1,0:T(1,128)}, f32[768,1152]{1,0:T(8,128)}, bf16[768,1152]{1,0:T(8,128)(2,1)}, f32[3,8,1152]{2,1,0:T(8,128)}, f32[1,1152]{1,0:...) custom-call(bf16[4,1152,1152]{2,1,0:T(8,128)(2,1)} %bitcast.50, bf16[4,1152,1152]{2,1,0:T(8,128)(2,1)} %bitcast.49, ...), custom_call_target="tpu_custom_call" | custom-call | tf_op jit(solution)/shard_map/pallas_call | solution.py:855
  313.4 0.8 bitcast_dynamic-update-slice_fusion.2
  314.2 0.8 bitcast_dynamic-update-slice_fusion.1
  314.9 0.8 bitcast_dynamic-update-slice_fusion
  315.9 58.8 %shard_map.277 = (bf16[4,768,896]{2,1,0:T(8,128)(2,1)}, f32[4,1,896]{2,1,0:T(1,128)}, f32[144,1152]{1,0:T(8,128)}, bf16[4,144,1152]{2,1,0:T(8,128)(2,1)}, bf16[4,768,288]{2,1,0:T(8,128)(2,1)}) custom-call(bf16[768,1152]{1,0:T(8,128)(2,1)} %get-tuple-element.68.grad_ref, bf16[1152,1152]{1,0:T(8,128)(2,1)} %get-tuple-element.69.out_weight_ref, ...), custom_call_target="tpu_custom_call" | custom-call | tf_op jit(solution)/shard_map/pallas_call | solution.py:969
  376.1 1.7 all_to_all.32
  377.8 1.0 copy.87
  378.7 3.8 all-to-all-start.1
  383.2 116.8 %shard_map.278 = (f32[768,1152]{1,0:T(8,128)}, f32[144,1152]{1,0:T(8,128)}, f32[144,1152]{1,0:T(8,128)}, f32[144,1728]{1,0:T(8,128)}, f32[8,1728]{1,0:T(8,128)}) custom-call(bf16[4,1152,1152]{2,1,0:T(8,128)(2,1)} %bitcast.47, bf16[4,768,896]{2,1,0:T(8,128)(2,1)} %get-tuple-element.74.triple_ref, bf16[4,768,288]{2,1,0:T(8,128)(2,1)} %get-tuple-element.75.split_ref, ...), custom_call_target="tpu_custom_call" | custom-call | tf_op jit(solution)/shard_map/pallas_call | solution.py:1132
  500.0 1.9 slice.85
  501.9 1.7 slice.89
  503.6 0.8 slice.86
  505.2 1.4 slice_reduce_fusion.1
  507.3 0.9 copy-done.1
  508.2 2.5 copy.88
  510.7 2.8 copy.123
  513.5 1.8 copy.124
  515.5 1.0 copy.125
  516.9 0.8 copy.126
  (88 shorter events, 13.0 us)
Async XLA Ops:
  0.6 10.8 %copy-start.4 = (bf16[144,864]{1,0:T(8,128)(2,1)S(1)}, bf16[144,864]{1,0:T(8,128)(2,1)}, u32[]{:S(2)}) copy-start(bf16[144,864]{1,0:T(8,128)(2,1)} %param.26) | copy-start | bytes 746500
  0.7 10.8 %copy-start.5 = (bf16[144,288]{1,0:T(8,128)(2,1)S(1)}, bf16[144,288]{1,0:T(8,128)(2,1)}, u32[]{:S(2)}) copy-start(bf16[144,288]{1,0:T(8,128)(2,1)} %param.29) | copy-start | bytes 248836
  0.7 11.6 %copy-start.14 = (bf16[288]{0:T(512)(128)(2,1)S(1)}, bf16[288]{0:T(512)(128)(2,1)}, u32[]{:S(2)}) copy-start(bf16[288]{0:T(512)(128)(2,1)} %param.27) | copy-start | bytes 1732
  0.7 11.6 %copy-start.15 = (bf16[288]{0:T(512)(128)(2,1)S(1)}, bf16[288]{0:T(512)(128)(2,1)}, u32[]{:S(2)}) copy-start(bf16[288]{0:T(512)(128)(2,1)} %param.28) | copy-start | bytes 1732
  0.7 11.6 %copy-start.16 = (bf16[288]{0:T(512)(128)(2,1)S(1)}, bf16[288]{0:T(512)(128)(2,1)}, u32[]{:S(2)}) copy-start(bf16[288]{0:T(512)(128)(2,1)} %param.30) | copy-start | bytes 1732
  0.7 11.6 %copy-start.11 = (bf16[1152]{0:T(1024)(128)(2,1)S(1)}, bf16[1152]{0:T(1024)(128)(2,1)}, u32[]{:S(2)}) copy-start(bf16[1152]{0:T(1024)(128)(2,1)} %param.32) | copy-start | bytes 6916
  0.7 11.6 %copy-start.17 = (bf16[288]{0:T(512)(128)(2,1)S(1)}, bf16[288]{0:T(512)(128)(2,1)}, u32[]{:S(2)}) copy-start(bf16[288]{0:T(512)(128)(2,1)} %param.34) | copy-start | bytes 1732
  2.8 114.9 %all-to-all-start = ((bf16[4,144,288]{2,1,0:T(8,128)(2,1)}), bf16[4,144,288]{2,1,0:T(8,128)(2,1)S(1)}, u32[]{:S(2)}, u32[]{:S(2)}) async-start(bf16[4,144,288]{2,1,0:T(8,128)(2,1)} %bitcast.10), calls=%async_computation | async-start | bytes 884736 | tf_op jit(solution)/shard_map/all_to_all | solution.py:1342
  6.2 107.5 %copy-start.12 = (s32[1,3,16]{2,0,1:T(1,128)S(1)}, s32[1,3,16]{2,0,1:T(1,128)}, u32[]{:S(2)}) copy-start(s32[1,3,16]{2,0,1:T(1,128)} %param.22) | copy-start | bytes 580
  9.5 105.2 %copy-start.13 = (s32[1,3,16]{2,0,1:T(1,128)S(1)}, s32[1,3,16]{2,0,1:T(1,128)}, u32[]{:S(2)}) copy-start(s32[1,3,16]{2,0,1:T(1,128)} %param.21) | copy-start | bytes 580
  9.5 107.2 %copy-start.7 = (s32[1,768]{1,0:T(1,128)S(1)}, s32[1,768]{1,0:T(1,128)}, u32[]{:S(2)}) copy-start(s32[1,768]{1,0:T(1,128)} %slot_row_ref.1) | copy-start | bytes 9220
  253.1 62.6 %copy-start.6 = (f32[8,1152]{1,0:T(8,128)S(1)}, f32[8,1152]{1,0:T(8,128)}, u32[]{:S(2)}) copy-start(f32[8,1152]{1,0:T(8,128)} %get-tuple-element.81) | copy-start | bytes 110596
  315.9 59.7 %copy-start.8 = (f32[4,1,1152]{2,1,0:T(1,128)S(1)}, f32[4,1,1152]{2,1,0:T(1,128)}, u32[]{:S(2)}) copy-start(f32[4,1,1152]{2,1,0:T(1,128)} %get-tuple-element.84) | copy-start | bytes 55300
  315.9 59.7 %copy-start.10 = (f32[1,1152]{1,0:T(1,128)S(1)}, f32[1,1152]{1,0:T(1,128)}, u32[]{:S(2)}) copy-start(f32[1,1152]{1,0:T(1,128)} %get-tuple-element.83) | copy-start | bytes 13828
  315.9 59.8 %copy-start.9 = (f32[1,1152]{1,0:T(1,128)S(1)}, f32[1,1152]{1,0:T(1,128)}, u32[]{:S(2)}) copy-start(f32[1,1152]{1,0:T(1,128)} %get-tuple-element.85) | copy-start | bytes 13828
  378.7 128.6 %all-to-all-start.1 = ((f32[144,4,288]{2,0,1:T(8,128)}), f32[144,4,288]{2,0,1:T(8,128)S(1)}, u32[]{:S(2)}, u32[]{:S(2)}) async-start(f32[144,4,288]{2,0,1:T(8,128)} %copy.87), calls=%async_computation.1 | async-start | bytes 1769472 | tf_op jit(solution)/shard_map/all_to_all | solution.py:1387
  507.3 0.9 copy-start.1
  508.2 5.3 %copy-start = (f32[768,1152]{1,0:T(8,128)S(1)}, f32[768,1152]{1,0:T(8,128)}, u32[]{:S(2)}) copy-start(f32[768,1152]{1,0:T(8,128)} %get-tuple-element.87) | copy-start | bytes 10616836
  513.5 2.0 copy-start.2
  515.5 1.5 copy-start.3

commit v5 on v4

--- a/solution.py
+++ b/solution.py
@@ -76,9 +76,10 @@
 
 
 def head_keep(mask_ref, h, segment):
-    return jnp.where(
-        segment == 0, mask_ref[h, 0], jnp.where(segment == 1, mask_ref[h, 1], mask_ref[h, 2])
-    )
+    keep = jnp.where(
+        segment == 0, mask_ref[0, h], jnp.where(segment == 1, mask_ref[1, h], mask_ref[2, h])
+    )
+    return keep.astype(F32)
 
 
 MESH = pl.DeviceIdType.MESH
@@ -422,10 +423,11 @@
 
 
 def attend_kernel(
-    x_ref, weight_ref, mods_ref, qkv_bias_ref, out_bias_ref, column_ref, row_ref, slot_ref,
+    x_ref, weight_in, mods_ref, qkv_bias_ref, out_bias_ref, column_ref, row_ref, slot_ref,
     groups_ref, mask_ref, up_ref, down_ref,
-    first_ref, heads_ref, mixed_ref, lse_ref, attn_ref, after_ref, arrived_ref, picked_ref, out_weight_ref,
+    first_out, heads_out, mixed_out, lse_ref, attn_ref, after_ref, arrived_ref, picked_ref, weight_out,
     up_out, down_out,
+    weight_ref, first_ref, heads_ref, mixed_ref, out_weight_ref, load_sems, save_sems,
     bias_ref, parts_ref, second_ref,
     send_sems, recv_sems, local_sems, down_send, down_recv, down_local,
 ):
@@ -435,7 +437,23 @@
         place, up_ref, lambda y, c, z, x: up_out.at[y, c, z, x], send_sems, recv_sems, local_sems
     )
     downs = Column(place, down_ref, down_out, down_send, down_recv, down_local.at[0])
+    loads = [
+        pltpu.make_async_copy(weight_in.at[j], weight_ref.at[j], load_sems.at[j]) for j in range(4)
+    ]
+    saves = [
+        pltpu.make_async_copy(source, target, save_sems.at[n])
+        for n, (source, target) in enumerate(
+            (
+                (first_ref, first_out),
+                (heads_ref, heads_out),
+                (out_weight_ref, weight_out),
+                (mixed_ref, mixed_out),
+            )
+        )
+    ]
     ups.start()
+    for copy in loads:
+        copy.start()
     downs.start()
     crop_mask(bias_ref, column_ref, row_ref)
 
@@ -448,8 +466,12 @@
         return carry
 
     lax.fori_loop(0, 3, norm, 0)
+    saves[0].start()
+    for copy in loads:
+        copy.wait()
     for j in range(4):
         out_weight_ref[:, OUT_SHARD * j : OUT_SHARD * (j + 1)] = weight_ref[j, :, QKV_SHARD:]
+    saves[2].start()
 
     def project(i, carry):
         j = lax.div(i, 3)
@@ -462,6 +484,7 @@
         return carry
 
     lax.fori_loop(0, 12, project, 0)
+    saves[1].start()
 
     def head(h, carry):
         for k in range(4):
@@ -486,6 +509,7 @@
     lax.fori_loop(0, HEADS, head, 0)
     for h in range(HEADS):
         mixed_ref[:, HEAD_DIM * h : HEAD_DIM * (h + 1)] = parts_ref[h][:, :HEAD_DIM]
+    saves[3].start()
     for k in range(4):
         ups.pass_pair(k)
 
@@ -509,6 +533,8 @@
         picked_ref[here, :] = dot(choice, groups_ref[...]).astype(BF16)
     ups.finish()
     downs.finish()
+    for copy in saves:
+        copy.wait()
 
 
 def shape_of(*shape, dtype=BF16):
@@ -542,9 +568,16 @@
             shape_of(2, 2, 4, 2, SHARD, D),
             shape_of(4, SHARD, D),
         ],
-        in_specs=[IN_VMEM] * 9 + [IN_SMEM] + [ANYWHERE] * 2,
-        out_specs=[IN_VMEM] * 9 + [ANYWHERE] * 2,
+        in_specs=[IN_VMEM, ANYWHERE] + [IN_VMEM] * 7 + [IN_SMEM] + [ANYWHERE] * 2,
+        out_specs=[ANYWHERE] * 3 + [IN_VMEM] * 5 + [ANYWHERE] * 3,
         scratch_shapes=[
+            pltpu.VMEM((4, D, D), BF16),
+            pltpu.VMEM((TOK_DEV, D), BF16),
+            pltpu.VMEM((3 * HEADS, TOK_DEV, 128), BF16),
+            pltpu.VMEM((TOK_DEV, D), BF16),
+            pltpu.VMEM((D, D), BF16),
+            DMA((4,)),
+            DMA((4,)),
             pltpu.VMEM((TOK_DEV, TOK_DEV), F32),
             pltpu.VMEM((HEADS, TOK_DEV, 128), BF16),
             pltpu.VMEM((TOK_DEV, D), BF16),
@@ -890,8 +923,9 @@
 
 
 def unattend_kernel(
-    grad_ref, out_weight_ref, heads_ref, lse_ref, column_ref, row_ref, given_ref, plane_ref, mask_ref,
-    triple_ref, sums_ref, share_ref, plane_out, split_ref,
+    grad_ref, weight_in, heads_in, lse_ref, column_ref, row_ref, given_in, plane_ref, mask_ref,
+    triple_ref, sums_ref, share_ref, plane_out, split_out,
+    out_weight_ref, heads_ref, given_ref, split_ref, load_sems,
     bias_ref, mixed_ref, grads_ref, key_ref, value_ref, bufs_ref, from_z_ref,
     send_sems, recv_sems, along_send, along_recv,
 ):
@@ -899,10 +933,24 @@
     place.meet()
     scatter = Scatter(place, given_ref, bufs_ref, plane_out, send_sems, recv_sems)
     along = Along(place, plane_ref, from_z_ref, share_ref, along_send, along_recv)
+    loads = [
+        pltpu.make_async_copy(source, target, load_sems.at[n])
+        for n, (source, target) in enumerate(
+            ((given_in, given_ref), (weight_in, out_weight_ref), (heads_in, heads_ref))
+        )
+    ]
+    save = pltpu.make_async_copy(split_ref, split_out, load_sems.at[3])
+    for copy in loads:
+        copy.start()
+    for k in (1, 2, 3):
+        along.start(k)
+    for j in range(4):
+        split_ref[j] = grad_ref[:, OUT_SHARD * j : OUT_SHARD * (j + 1)]
+    save.start()
+    loads[0].wait()
     for k in ORDER:
         scatter.start(k)
-    for k in (1, 2, 3):
-        along.start(k)
+    loads[1].wait()
     crop_mask(bias_ref, column_ref, row_ref)
 
     def spread(i, carry):
@@ -917,6 +965,7 @@
 
     lax.fori_loop(0, 3, spread, 0)
     factor = HEAD_DIM**-0.5
+    loads[2].wait()
 
     def head(h, carry):
         @pl.when(h == 1)
@@ -957,8 +1006,7 @@
         for h in range(12):
             triple_ref[j, :, HEAD_DIM * h : HEAD_DIM * (h + 1)] = grads_ref[12 * j + h][:, :HEAD_DIM]
         sums_ref[j] = jnp.sum(triple_ref[j].astype(F32), axis=0, keepdims=True)
-    for j in range(4):
-        split_ref[j] = grad_ref[:, OUT_SHARD * j : OUT_SHARD * (j + 1)]
+    save.wait()
     along.close()
     for k in ORDER:
         scatter.collect(k)
@@ -975,9 +1023,14 @@
             shape_of(4, SHARD, D),
             shape_of(4, TOK_DEV, OUT_SHARD),
         ],
-        in_specs=[IN_VMEM] * 8 + [IN_SMEM],
-        out_specs=[IN_VMEM] * 5,
+        in_specs=[IN_VMEM] + [ANYWHERE] * 2 + [IN_VMEM] * 3 + [ANYWHERE, IN_VMEM, IN_SMEM],
+        out_specs=[IN_VMEM] * 4 + [ANYWHERE],
         scratch_shapes=[
+            pltpu.VMEM((D, D), BF16),
+            pltpu.VMEM((3 * HEADS, TOK_DEV, 128), BF16),
+            pltpu.VMEM((2, 4, 2, SHARD, D), BF16),
+            pltpu.VMEM((4, TOK_DEV, OUT_SHARD), BF16),
+            DMA((4,)),
             pltpu.VMEM((TOK_DEV, TOK_DEV), F32),
             pltpu.VMEM((HEADS, TOK_DEV, 128), BF16),
             pltpu.VMEM((3 * HEADS, TOK_DEV, 128), BF16),
@@ -996,10 +1049,10 @@
 
 def unproject_kernel(
     weight_ref, triple_ref, split_ref, first_ref, mixed_ref, x_ref, mid_ref, mods_ref, column_ref,
-    plane_up_ref, rest_ref, conds_ref,
-    grad_in_ref, share_up_ref, share_ref, ada_ref, sums_ref,
-    total_ref, buffers_ref, parts_ref, bufs_ref, plane_ref, up_z_ref, from_z_ref,
-    mod_ref, mates_ref, packed_ref, every_ref,
+    plane_up_ref, rest_ref, conds_ref, down_ref,
+    grad_in_ref, share_up_ref, qkv_ref, out_ref, ada_ref, sums_ref, share_down_ref,
+    share_ref, turn_ref, turned_ref, total_ref, buffers_ref, parts_ref, bufs_ref, plane_ref, up_z_ref, from_z_ref,
+    mod_ref, mates_ref, rows_ref, packed_ref, every_ref,
     send_sems, recv_sems, pair_send, pair_recv, up_send, up_recv, along_send, along_recv,
     small_send, small_recv,
 ):
@@ -1015,20 +1068,25 @@
         small.make(mod_ref.at[other], mates_ref.at[place.index], mate)
         for other, mate in zip(place.mate_index, place.mates)
     ]
-    to_z = [
-        small.make(packed_ref, every_ref.at[place.peer], place.device(z=place.zs[k]))
-        for k in (1, 2, 3)
+    to_peers = []
+    for k in range(4):
+        for there in (place.x, 1 - place.x) if k else (1 - place.x,):
+            other = place.device(z=place.zs[k], x=there)
+            to_peers.append(small.make(packed_ref, every_ref.at[place.peer], other))
+    swaps = [
+        small.make(turn_ref.at[other], turned_ref.at[place.index], mate)
+        for other, mate in zip(place.mate_index, place.mates)
     ]
-    to_x = []
-    for k in range(4):
-        held = every_ref.at[2 * place.zs[k] + place.x]
-        to_x.append(small.make(held, held, place.device(x=1 - place.x)))
-
     @pl.when(step == 0)
     def _():
         place.meet()
-        for k in (1, 2, 3):
+        for k in (2, 3, 1):
             along_up.start(k)
+        for j in range(4):
+            turn_ref[j] = down_ref[:, OUT_SHARD * j : OUT_SHARD * (j + 1)]
+        for copy in swaps:
+            copy.start()
+        turned_ref[place.index] = turn_ref[place.index]
 
     @pl.when(step < 4)
     def _():
@@ -1056,13 +1114,18 @@
     def _():
         pair.free(2)
         pair.free(3)
-        for k in ORDER:
-            scatter.start(k)
-
-    @pl.when(step == 5)
-    def _():
-        for k in ORDER:
-            scatter.follow(k)
+        scatter.start(2)
+        scatter.follow(2)
+        scatter.start(3)
+
+    for at, now, then in ((5, 2, 3), (6, 3, 1), (7, 1, 0)):
+
+        @pl.when(step == at)
+        def _():
+            scatter.pass_across(now)
+            scatter.follow(then)
+            if at < 7:
+                scatter.start(1 if at == 5 else 0)
 
     @pl.when(step >= 4)
     def _():
@@ -1073,8 +1136,9 @@
 
     @pl.when(step == 7)
     def _():
-        for k in ORDER[:2]:
-            scatter.pass_across(k)
+        scatter.collect(2)
+        along.start(2)
+        scatter.pass_across(0)
         shifts, scales = jnp.zeros((8, D), F32), jnp.zeros((8, D), F32)
         for i in range(3):
             here = pl.ds(i * BLOCK, BLOCK)
@@ -1094,36 +1158,37 @@
         for copy in to_mates:
             copy.start()
         mates_ref[place.index] = mod_ref[place.index]
-        for k in ORDER[2:]:
-            scatter.pass_across(k)
+        scatter.collect(3)
+        along.start(3)
         for copy in to_mates:
             copy.wait_recv()
-        packed_ref[...] = jnp.zeros_like(packed_ref)
+        rows_ref[...] = jnp.zeros_like(rows_ref)
         for j in range(4):
-            packed_ref[CROPS * j : CROPS * (j + 1), :] = mates_ref[j, :CROPS, :]
-            packed_ref[12:14, :] += mates_ref[j, CROPS : CROPS + 2, :]
-        for copy in to_z:
+            rows_ref[CROPS * j : CROPS * (j + 1), :] = mates_ref[j, :CROPS, :]
+            rows_ref[12:14, :] += mates_ref[j, CROPS : CROPS + 2, :]
+        packed_ref[...] = rows_ref[...].astype(BF16)
+        for copy in to_peers:
             copy.start()
         every_ref[place.peer] = packed_ref[...]
+        scatter.collect(1)
+        along.start(1)
         along_up.close()
-        for copy in to_z:
+        for copy in swaps:
             copy.wait_recv()
-        for copy in to_x:
-            copy.start()
-        for k in ORDER[:3]:
-            scatter.collect(k)
-            along.start(k)
-        for copy in to_x:
+        share_down_ref[...] = turned_ref[...]
+        scatter.collect(0)
+        for copy in to_peers:
             copy.wait_recv()
         close_ada(conds_ref, every_ref, ada_ref, sums_ref)
-        scatter.collect(0)
         along.close()
+        qkv_ref[...] = share_ref[:, :QKV_SHARD]
+        out_ref[...] = share_ref[:, QKV_SHARD:]
         scatter.finish()
         for copy in small.made:
             copy.wait_send()
 
 
-def unproject(weight, triple, split, first, mixed, x, mid, mods, column, plane_up, rest, conds):
+def unproject(weight, triple, split, first, mixed, x, mid, mods, column, plane_up, rest, conds, down):
     block = lambda *tail: pl.BlockSpec((1, *tail), lambda i: (lax.rem(i, 4), 0, 0))
     early = lambda *tail: pl.BlockSpec((1, *tail), lambda i: (jnp.minimum(i, 3), 0, 0))
     late = lambda *tail: pl.BlockSpec((1, *tail), lambda i: (jnp.maximum(i - 4, 0), 0, 0))
@@ -1135,19 +1200,25 @@
         out_shape=[
             shape_of(TOK_DEV, D, dtype=F32),
             shape_of(SHARD, D, dtype=F32),
-            shape_of(SHARD, D, dtype=F32),
+            shape_of(SHARD, QKV_SHARD, dtype=F32),
+            shape_of(SHARD, OUT_SHARD, dtype=F32),
             shape_of(SHARD, wide, dtype=F32),
             shape_of(8, wide, dtype=F32),
+            shape_of(4, SHARD, OUT_SHARD, dtype=F32),
         ],
         in_specs=[
             late(D, D), block(TOK_DEV, PAD_SHARD), early(TOK_DEV, OUT_SHARD), whole(TOK_DEV, D),
             whole(TOK_DEV, D), whole(TOK_DEV, D), whole(TOK_DEV, D), whole(6, 8, D), whole(TOK_DEV, 1),
-            whole(4, SHARD, D), whole(4, 8, wide), whole(8, 16, 256),
+            whole(4, SHARD, D), whole(4, 8, wide), whole(8, 16, 256), whole(SHARD, D),
         ],
         out_specs=[
-            whole(TOK_DEV, D), whole(SHARD, D), whole(SHARD, D), whole(SHARD, wide), whole(8, wide),
+            whole(TOK_DEV, D), whole(SHARD, D), whole(SHARD, QKV_SHARD), whole(SHARD, OUT_SHARD),
+            whole(SHARD, wide), whole(8, wide), whole(4, SHARD, OUT_SHARD),
         ],
         scratch_shapes=[
+            vmem((SHARD, D), F32),
+            vmem((4, SHARD, OUT_SHARD), F32),
+            vmem((4, SHARD, OUT_SHARD), F32),
             vmem((TOK_DEV, D), F32),
             vmem((2, D, D), BF16),
             vmem((2, D, D), BF16),
@@ -1158,7 +1229,8 @@
             vmem((4, 8, wide), F32),
             vmem((4, 8, wide), F32),
             vmem((16, wide), F32),
-            vmem((8, 16, wide), F32),
+            vmem((16, wide), BF16),
+            vmem((8, 16, wide), BF16),
             DMA((SCATTER_COPIES,)),
             DMA((SCATTER_COPIES,)),
             DMA((2,)),
@@ -1167,26 +1239,29 @@
             DMA((3,)),
             DMA((3,)),
             DMA((3,)),
-            DMA((10,)),
-            DMA((10,)),
+            DMA((13,)),
+            DMA((13,)),
         ],
         compiler_params=talking(6),
-    )(weight, triple, split, first, mixed, x, mid, mods, column, plane_up, rest, conds)
+    )(weight, triple, split, first, mixed, x, mid, mods, column, plane_up, rest, conds, down)
 
 
 CROPS = 3
 
 
 def gather_kernel(
-    mixed_ref, up_ref, cond_ref, ada_ref, ada_bias_ref, bias_ref,
-    mixed_out, up_out, mods_ref, biases_ref, conds_ref,
+    qkv_ref, out_ref, up_ref, down_ref, cond_ref, ada_ref, vectors_ref, slot_ref, groups_ref, lengths_ref,
+    mixed_out, up_out, down_out, mods_ref, conds_ref, qkv_bias_ref, up_bias_ref, out_bias_ref,
+    down_bias_ref, column_ref, row_ref, slot_column_ref, token_groups_ref,
     send_sems, recv_sems, local_sem, up_send, up_recv, up_local, small_send, small_recv, local_small,
-    all_cond, own_cond, partial_ref, from_x, from_z, column_ref,
+    mixed_ref, stage_ref, own_small, all_small, own_cond, partial_ref, from_x, from_z, rows_ref, tables_ref,
+    query_ref, value_ref,
 ):
     place = Place()
     place.meet()
     x, zs = place.x, place.zs
-
+    mixed_ref[:, :QKV_SHARD] = qkv_ref[...]
+    mixed_ref[:, QKV_SHARD:] = out_ref[...]
     first = Gather(
         place,
         mixed_ref,
@@ -1198,8 +1273,7 @@
     )
     ups = Column(place, up_ref, up_out, up_send, up_recv, up_local.at[0])
     small = Copies(small_send, small_recv)
-    to_mates = [small.make(cond_ref, all_cond.at[place.index], mate) for mate in place.mates]
-    to_mates += [small.make(bias_ref, biases_ref.at[place.index], mate) for mate in place.mates]
+    to_mates = [small.make(own_small, all_small.at[place.index], mate) for mate in place.mates]
     others = [(k, far) for k in range(4) for far in (0, 1) if k or far]
     to_peers = []
     for k, far in others:
@@ -1220,99 +1294,161 @@
         for k in (1, 2, 3)
     ]
     finals = [
-        small.make(column_ref.at[other], mods_ref.at[place.index], mate)
+        small.make(rows_ref.at[other], tables_ref.at[place.index], mate)
         for other, mate in zip(place.mate_index, place.mates)
     ]
-    own_bias = pltpu.make_async_copy(bias_ref, biases_ref.at[place.index], local_small.at[0])
-
+
+    def down_rows(index):
+        return down_ref.at[pl.ds(pl.multiple_of(index * SHARD, 16), SHARD)]
+
+    swaps = [
+        small.make(down_rows(other), stage_ref.at[place.index], mate)
+        for other, mate in zip(place.mate_index, place.mates)
+    ]
+    own_stage = pltpu.make_async_copy(
+        down_rows(place.index), stage_ref.at[place.index], local_small.at[0]
+    )
+
+    first.start()
+    cond = cond_ref[...].astype(F32)
+    own_small[...] = jnp.zeros_like(own_small)
+    own_small[:CROPS, :] = (cond / (1.0 + jnp.exp(-cond))).astype(BF16).astype(F32)
+    own_small[CROPS : CROPS + 1, :] = vectors_ref[:, :D]
+    own_small[CROPS + 1 : CROPS + 2, :] = vectors_ref[:, D : 2 * D]
     for copy in to_mates:
         copy.start()
-    own_bias.start()
-    first.start()
-    all_cond[place.index] = cond_ref[...]
+    own_stage.start()
+    all_small[place.index] = own_small[...]
     own_cond[...] = jnp.zeros_like(own_cond)
     for copy in to_mates:
         copy.wait_recv()
-    for j in range(4):
-        own_cond[:, CROPS * j : CROPS * (j + 1), :] = all_cond[j, :, :CROPS, :]
+    for i in range(8):
+        for j in range(4):
+            part = all_small[j, :CROPS, SHARD * i : SHARD * (i + 1)]
+            own_cond[i, CROPS * j : CROPS * (j + 1), :SHARD] = part
     for copy in to_peers:
         copy.start()
     conds_ref[place.peer] = own_cond[place.peer]
-    first.pass_along(1)
     for copy in to_peers:
         copy.wait_recv()
-    for i in range(8):
-        partial_ref[i] = dot(conds_ref[i][:, :SHARD].astype(BF16), ada_ref[...])
-    for copy in over_x:
-        copy.start()
-    first.pass_along(2)
-    first.pass_along(3)
-    for k in range(4):
+    every_cond = conds_ref[...].reshape(128, 256)[:, :SHARD].astype(BF16)
+    partial_ref[...] = dot(every_cond, ada_ref[...]).reshape(partial_ref.shape)
+    for k in ORDER:
+        over_x[k].start()
+    first.pass_across(0)
+    for k in (1, 2, 3):
+        first.pass_along(k)
+    for k in ORDER:
         over_x[k].wait_recv()
         partial_ref[2 * zs[k] + x] += from_x[k]
-    for copy in along:
-        copy.start()
-    for k in range(2):
-        first.pass_across(k)
+        if k:
+            along[k - 1].start()
+    first_end = lengths_ref[0, 0]
+    second_end = first_end + lengths_ref[0, 1]
+    tokens = lax.broadcasted_iota(jnp.int32, (TOK_DEV, 1), 0)
+    column_ref[...] = (tokens >= first_end).astype(jnp.int32) + (tokens >= second_end).astype(jnp.int32)
+    tokens = lax.broadcasted_iota(jnp.int32, (1, TOK_DEV), 1)
+    row_ref[...] = (tokens >= first_end).astype(jnp.int32) + (tokens >= second_end).astype(jnp.int32)
+    spread = jnp.broadcast_to(slot_ref[...].astype(F32), (128, TOK_DEV))
+    slot_column_ref[...] = jnp.transpose(spread)[:, :1].astype(jnp.int32)
+    token_groups_ref[...] = jnp.zeros_like(token_groups_ref)
+    token_groups_ref[:, :GROUPS] = per_crop(groups_ref[...].astype(F32), column_ref[...]).astype(BF16)
+    first.pass_across(1)
     for copy in along:
         copy.wait_recv()
-    total = partial_ref[place.peer] + from_z[0] + from_z[1] + from_z[2] + ada_bias_ref[...]
-    column_ref[...] = jnp.zeros_like(column_ref)
+    total = partial_ref[place.peer] + from_z[0] + from_z[1] + from_z[2] + vectors_ref[:, 2 * D :]
+    rows_ref[...] = jnp.zeros_like(rows_ref)
     for j in range(4):
-        column_ref[j, :CROPS, :] = total[CROPS * j : CROPS * (j + 1)]
+        rows_ref[j, :CROPS, :] = total[CROPS * j : CROPS * (j + 1)]
     for copy in finals:
         copy.start()
-    mods_ref[place.index] = column_ref[place.index]
-    for k in range(2, 4):
-        first.pass_across(k)
+    tables_ref[place.index] = rows_ref[place.index]
     ups.start()
-    for k in range(4):
-        first.pass_pair(k)
+    for copy in swaps:
+        copy.start()
+    first.pass_across(2)
     for copy in finals:
         copy.wait_recv()
-    own_bias.wait()
+    for j in (0, 2):
+        mods_ref[3 * j // 2] = tables_ref[j, :, :D]
+        mods_ref[3 * j // 2 + 1, :, : D // 2] = tables_ref[j, :, D:]
+        mods_ref[3 * j // 2 + 1, :, D // 2 :] = tables_ref[j + 1, :, : D // 2]
+        mods_ref[3 * j // 2 + 2] = tables_ref[j + 1, :, D // 2 :]
+    first.pass_pair(0)
+    first.pass_across(3)
+    for copy in swaps:
+        copy.wait_recv()
+    own_stage.wait()
+    for j in range(4):
+        here = slice(OUT_SHARD * j, OUT_SHARD * (j + 1))
+        down_out[:, here] = stage_ref[j]
+        up_bias_ref[j] = all_small[j, CROPS : CROPS + 1, :]
+        row = all_small[j, CROPS + 1 : CROPS + 2, :]
+        query_ref[:, here] = row[:, :OUT_SHARD]
+        value_ref[:, here] = row[:, OUT_SHARD : 2 * OUT_SHARD]
+        out_bias_ref[:, here] = row[:, 2 * OUT_SHARD : 3 * OUT_SHARD]
+        down_bias_ref[:, here] = row[:, 3 * OUT_SHARD :]
+    qkv_bias_ref[...] = jnp.zeros_like(qkv_bias_ref)
+    qkv_bias_ref[0, :, :QKV_SHARD] = query_ref[:, :QKV_SHARD]
+    qkv_bias_ref[1, :, :OUT_SHARD] = query_ref[:, QKV_SHARD:]
+    qkv_bias_ref[2, :, 2 * OUT_SHARD : QKV_SHARD] = value_ref[:, :OUT_SHARD]
+    qkv_bias_ref[3, :, :QKV_SHARD] = value_ref[:, OUT_SHARD:]
+    for k in (1, 2, 3):
+        first.pass_pair(k)
     first.finish()
     ups.finish()
     for copy in small.made:
         copy.wait_send()
 
 
-def gather_all(mixed, up, cond, ada, ada_bias, bias):
+def gather_all(qkv, out, up, down, cond, ada, vectors, slot, groups, lengths):
     vmem = pltpu.VMEM
     wide = ada.shape[1]
     return pl.pallas_call(
         gather_kernel,
-        out_shape=[shape_of(2, 2, 4, 2, SHARD, D), shape_of(4, SHARD, D)]
-        + [shape_of(4, 8, wide, dtype=F32), shape_of(4, 32, 128), shape_of(8, 16, 256, dtype=F32)],
-        in_specs=[ANYWHERE] * 2 + [IN_VMEM] * 4,
-        out_specs=[ANYWHERE] * 2 + [IN_VMEM] * 3,
+        out_shape=[
+            shape_of(2, 2, 4, 2, SHARD, D),
+            shape_of(4, SHARD, D),
+            shape_of(SHARD, D),
+            shape_of(6, 8, D, dtype=F32),
+            shape_of(8, 16, 256, dtype=F32),
+            shape_of(4, 1, PAD_SHARD, dtype=F32),
+            shape_of(4, 1, D, dtype=F32),
+            shape_of(1, D, dtype=F32),
+            shape_of(1, D, dtype=F32),
+            shape_of(TOK_DEV, 1, dtype=jnp.int32),
+            shape_of(1, TOK_DEV, dtype=jnp.int32),
+            shape_of(TOK_DEV, 1, dtype=jnp.int32),
+            shape_of(TOK_DEV, 128),
+        ],
+        in_specs=[IN_VMEM] * 2 + [ANYWHERE] * 2 + [IN_VMEM] * 5 + [IN_SMEM],
+        out_specs=[ANYWHERE] * 2 + [IN_VMEM] * 11,
         scratch_shapes=[DMA((GATHER_COPIES,))] * 2
         + [DMA((1,)), DMA((3,)), DMA((3,)), DMA((1,)), DMA((23,)), DMA((23,)), DMA((1,))]
         + [
-            vmem((4, 8, 8, 256), F32),
+            vmem((SHARD, D), BF16),
+            vmem((4, SHARD, OUT_SHARD), BF16),
+            vmem((8, D), F32),
+            vmem((4, 8, D), F32),
             vmem((8, 16, 256), F32),
             vmem((8, 16, wide), F32),
             vmem((4, 16, wide), F32),
             vmem((3, 16, wide), F32),
             vmem((4, 8, wide), F32),
+            vmem((4, 8, wide), F32),
+            vmem((1, D), F32),
+            vmem((1, D), F32),
         ],
-        compiler_params=pltpu.CompilerParams(
-            collective_id=1, has_side_effects=True, vmem_limit_bytes=VMEM_BYTES
-        ),
-    )(mixed, up, cond, ada, ada_bias, bias)
+        compiler_params=talking(1),
+    )(qkv, out, up, down, cond, ada, vectors, slot, groups, lengths)
 
 
 def close_ada(conds_ref, every, ada_ref, sums_ref):
-    total = jnp.zeros(ada_ref.shape, F32)
     rows = jnp.zeros((16, ada_ref.shape[1]), F32)
-    for i in range(0, 8, 2):
-        rows = rows + every[i] + every[i + 1]
-        cond = jnp.concatenate([conds_ref[i][:, :SHARD], conds_ref[i + 1][:, :SHARD]], axis=0)
-        rest = jnp.concatenate([every[i], every[i + 1]], axis=0)
-        for _ in range(3):
-            part = rest.astype(BF16)
-            total = total + dot(cond.astype(BF16), part, TN)
-            rest = rest - part.astype(F32)
+    for i in range(8):
+        rows = rows + every[i].astype(F32)
+    cond = conds_ref[...].reshape(128, 256)[:, :SHARD].astype(BF16)
+    total = dot(cond, every[...].reshape(128, ada_ref.shape[1]), TN)
     ada_ref[...] = total
     sums_ref[...] = jnp.zeros_like(sums_ref)
     sums_ref[0:1, :] = jnp.sum(rows[:12], axis=0, keepdims=True)
@@ -1323,43 +1459,31 @@
     block_in, condition, lengths, head_mask, group_mask, buffer_slot, ada_weight, ada_bias, qkv_weight,
     query_bias, value_bias, out_weight, out_bias, up_weight, up_bias, down_weight, down_bias, cotangent,
 ):
-    x, cot = block_in[0], cotangent[0]
-    finish = jnp.cumsum(lengths[0])
-    position = jnp.arange(TOK_DEV, dtype=jnp.int32)
-    segment = jnp.sum((position[:, None] >= finish[None, :]).astype(jnp.int32), axis=1)
-    column, row = segment[:, None], segment[None, :]
-    slot = buffer_slot[0].astype(jnp.int32)
-    slot_column, slot_row = slot[:, None], slot[None, :]
-    mask = head_mask[0].T.astype(F32)
-    chosen = (segment[:, None] == jnp.arange(CROPS)[None, :])[:, :, None]
-    groups = jnp.sum(jnp.where(chosen, group_mask[0].astype(F32)[None], 0.0), axis=1)
-    groups = jnp.pad(groups, ((0, 0), (0, 128 - GROUPS))).astype(BF16)
-    cond = jax.nn.silu(condition[0].astype(F32)).astype(BF16).astype(F32)
-    cond = cond.reshape(CROPS, 8, SHARD).transpose(1, 0, 2)
-    cond = jnp.pad(cond, ((0, 0), (0, 8 - CROPS), (0, 256 - SHARD)))
-    vectors = jnp.concatenate([query_bias, value_bias, out_bias, up_bias, down_bias])
-    packed = jnp.pad(vectors.reshape(18, 128), ((0, 14), (0, 0)))
-    down_rows = lax.all_to_all(down_weight, "fsdp", split_axis=0, concat_axis=1, tiled=True)
-    mixed_block = jnp.concatenate([qkv_weight, out_weight], axis=1)
-    mixed_weight, up_column, mods, biases, conds = gather_all(
-        mixed_block, up_weight, cond, ada_weight, ada_bias.astype(F32)[None], packed
+    x, cot, slot_row, mask = block_in[0], cotangent[0], buffer_slot.astype(jnp.int32), head_mask[0]
+    vectors = (up_bias, query_bias, value_bias, out_bias, down_bias, ada_bias)
+    total = sum(vector.shape[0] for vector in vectors)
+    starts = (0, 1152, 1440, 1728, 2016, 2304)
+    padded = [
+        jnp.pad(vector.astype(F32), (start, total - start - vector.shape[0]))
+        for start, vector in zip(starts, vectors)
+    ]
+    vectors = sum(padded)[None]
+    (
+        mixed_weight, up_column, down_rows, mods, conds, qkv_bias, bias_up, bias_out, bias_down,
+        column, row, slot_column, groups,
+    ) = gather_all(
+        qkv_weight, out_weight, up_weight, down_weight, condition[0], ada_weight, vectors, slot_row,
+        group_mask[0], lengths,
     )
     mixed_weight = mixed_weight.reshape(4, D, D)
-    mods = mods.transpose(1, 0, 2).reshape(8, 6, D).transpose(1, 0, 2)
-    biases = biases[:, :18].reshape(4, 2304).astype(F32)
     edges = (0, 288, 576, 864, 2016, 2304)
-    bias_query, bias_value, bias_out, bias_up, bias_down = [
-        biases[:, low:high].reshape(1, -1) for low, high in zip(edges[:-1], edges[1:])
-    ]
-    qkv_bias = jnp.concatenate([bias_query, jnp.zeros_like(bias_query), bias_value], axis=1)
-    qkv_bias = jnp.pad(qkv_bias.reshape(4, 1, QKV_SHARD), ((0, 0), (0, 0), (0, PAD_SHARD - QKV_SHARD)))
     first, heads, mixed, lse, attn, after, arrived, picked, full_out, up, down_column = attend(
         x, mixed_weight, mods, qkv_bias, bias_out, column, row, slot_row, groups, mask, up_column,
         down_rows,
     )
     up = up.reshape(4, D, D)
     pull, grad_rows, block_out, gate_two, grad_down_bias, parts_down, down = feed(
-        up, arrived, picked, bias_up.reshape(4, 1, D), bias_down, cot, after, mods, column,
+        up, arrived, picked, bias_up, bias_down, cot, after, mods, column,
         slot_column, slot_row, down_column,
     )
     down = down.reshape(4, D, D)
@@ -1381,10 +1505,11 @@
     wide = mod_grads.shape[2]
     bias_grads = jnp.pad(bias_grads, ((0, 0), (0, 5 * wide - 2304))).reshape(4, 5, wide)
     rest = jnp.concatenate([mod_grads, bias_grads], axis=1)
-    grad_in, share_up, share_mixed, grad_ada, totals = unproject(
-        mixed_weight, triple, grad_split, first, mixed, x, mid, mods, column, plane_up, rest, conds
-    )
-    share_down = lax.all_to_all(share_down, "fsdp", split_axis=1, concat_axis=0, tiled=True)
+    grad_in, share_up, share_qkv, share_out, grad_ada, totals, share_down = unproject(
+        mixed_weight, triple, grad_split, first, mixed, x, mid, mods, column, plane_up, rest, conds,
+        share_down,
+    )
+    share_down = share_down.reshape(4 * SHARD, OUT_SHARD)
     bias_totals = totals[1:3].reshape(-1)
     grad_query, grad_value, grad_out, grad_ups, grad_downs = [
         bias_totals[low:high] for low, high in zip(edges[:-1], edges[1:])
@@ -1394,10 +1519,10 @@
         grad_in[None],
         grad_ada,
         totals[0],
-        share_mixed[:, :QKV_SHARD],
+        share_qkv,
         grad_query,
         grad_value,
-        share_mixed[:, QKV_SHARD:],
+        share_out,
         grad_out,
         share_up,
         grad_ups,

time: 527 us -> 474 us (0.90)
  the two profiles are of different devices: /device:TPU:8 before, /device:TPU:9 now
where the time goes in v5:
time: 474 us; the launch traced here: 465 us
  Pallas kernels  438 us (92%)
  local copies, waits for them, and re-layouts  23.5 us (5%)
    pallas_call x1, Pallas kernels, unproject(): pl.pallas_call(unproject_kernel, grid=(8,), out_shape=[shape_of(TOK_DEV,...  103 us
    pallas_call x1, Pallas kernels, gather_all(): pl.pallas_call(gather_kernel, out_shape=[shape_of(2, 2, 4, 2, SHARD, D),...  87.8 us
    pallas_call x1, Pallas kernels, feed(): pl.pallas_call(feed_kernel, grid=(8,), out_shape=[shape_of(4, PLACES, D),...  69.9 us
    pallas_call x1, Pallas kernels, attend(): pl.pallas_call(attend_kernel, out_shape=[shape_of(TOK_DEV, D), shape_of(3...  61.6 us
    pallas_call x1, Pallas kernels, unfeed(): pl.pallas_call(unfeed_kernel, grid=(4,), out_shape=[shape_of(4, 1, D, dty...  59.6 us
    pallas_call x1, Pallas kernels, unattend(): pl.pallas_call(unattend_kernel, out_shape=[shape_of(4, TOK_DEV, PAD_SHARD...  56.6 us
    unnamed x35, local copies, waits for them, and re-layouts  17.1 us

profile of v5, /device:TPU:9, one launch (start us, length us, event | category | flops | bytes accessed | tf_op | source)
XLA Modules:
  0.0 465.5 jit_solution(7036126057512892018)
XLA Ops:
  0.7 1.9 copy.33.down_ref
  2.6 1.5 convert_add_fusion
  4.1 1.3 copy.46
  5.3 87.8 %shard_map.273 = (bf16[2,2,4,2,144,1152]{5,4,3,2,1,0:T(8,128)(2,1)}, bf16[4,144,1152]{2,1,0:T(8,128)(2,1)}, bf16[144,1152]{1,0:T(8,128)(2,1)}, f32[6,8,1152]{2,1...) custom-call(bf16[144,864]{1,0:T(8,128)(2,1)} %qkv_ref.1, ...), custom_call_target="tpu_custom_call" | custom-call | tf_op jit(solution)/shard_map/pallas_call | solution.py:1407
  93.2 0.6 copy.45
  93.7 61.6 %shard_map.274 = (bf16[768,1152]{1,0:T(8,128)(2,1)}, bf16[48,768,128]{2,1,0:T(8,128)(2,1)}, bf16[768,1152]{1,0:T(8,128)(2,1)}, f32[16,1,768]{2,1,0:T(1,128)}, bf...) custom-call(bf16[768,1152]{1,0:T(8,128)(2,1)} %bitcast.34, ...), custom_call_target="tpu_custom_call" | custom-call | tf_op jit(solution)/shard_map/pallas_call | solution.py:556
  155.4 69.9 %shard_map.275 = (bf16[4,512,1152]{2,1,0:T(8,128)(2,1)}, bf16[512,1152]{1,0:T(8,128)(2,1)}, bf16[768,1152]{1,0:T(8,128)(2,1)}, f32[8,1152]{1,0:T(8,128)}, f32[1,...) custom-call(bf16[4,1152,1152]{2,1,0:T(8,128)(2,1)} %bitcast.31, ...), custom_call_target="tpu_custom_call" | custom-call | tf_op jit(solution)/shard_map/pallas_call | solution.py:755
  225.3 59.6 %shard_map.276 = (f32[4,1,1152]{2,1,0:T(1,128)}, f32[768,1152]{1,0:T(8,128)}, bf16[768,1152]{1,0:T(8,128)(2,1)}, f32[3,8,1152]{2,1,0:T(8,128)}, f32[1,1152]{1,0:...) custom-call(bf16[4,1152,1152]{2,1,0:T(8,128)(2,1)} %bitcast.33, bf16[4,1152,1152]{2,1,0:T(8,128)(2,1)} %bitcast.32, ...), custom_call_target="tpu_custom_call" | custom-call | tf_op jit(solution)/shard_map/pallas_call | solution.py:888
  284.8 0.8 bitcast_dynamic-update-slice_fusion.2
  285.6 0.8 bitcast_dynamic-update-slice_fusion.1
  286.4 0.8 bitcast_dynamic-update-slice_fusion
  287.2 0.1 reshape.69
  287.4 56.6 %shard_map.277 = (bf16[4,768,896]{2,1,0:T(8,128)(2,1)}, f32[4,1,896]{2,1,0:T(1,128)}, f32[144,1152]{1,0:T(8,128)}, bf16[4,144,1152]{2,1,0:T(8,128)(2,1)}, bf16[4,768,288]{2,1,0:T(8,128)(2,1)}) custom-call(bf16[768,1152]{1,0:T(8,128)(2,1)} %get-tuple-element.86.grad_ref, bf16[1152,1152]{1,0:T(8,128)(2,1)} %get-tuple-element.87.weight_in, ...), custom_call_target="tpu_custom_call" | custom-call | tf_op jit(solution)/shard_map/pallas_call | solution.py:1017
  344.1 0.8 slice_reduce_fusion
  345.1 0.1 concatenate.10
  345.3 0.1 reshape.73
  345.4 0.7 pad_maximum_fusion.rest_ref
  346.2 102.9 %shard_map.278 = (f32[768,1152]{1,0:T(8,128)}, f32[144,1152]{1,0:T(8,128)}, f32[144,864]{1,0:T(8,128)}, f32[144,288]{1,0:T(8,128)}, f32[144,1728]{1,0:T(8,128)},...) custom-call(bf16[4,1152,1152]{2,1,0:T(8,128)(2,1)} %bitcast.30, bf16[4,768,896]{2,1,0:T(8,128)(2,1)} %get-tuple-element.92.triple_ref, ...), custom_call_target="tpu_custom_call" | custom-call | tf_op jit(solution)/shard_map/pallas_call | solution.py:1197
  449.1 2.5 copy.35
  451.6 1.4 slice.55
  453.0 0.8 reshape.74
  453.8 0.7 fusion.1
  454.5 0.7 slice.67
  455.1 1.4 slice_reduce_fusion.1
  456.6 2.8 copy.57
  459.4 1.8 copy.58
  461.2 0.2 copy-done.1
  461.4 1.0 copy.59
  462.3 0.4 copy-done.3
  462.7 0.8 copy.60
  463.5 0.7 copy.61
  464.2 0.8 copy.62
  (30 shorter events, 0.4 us)
Async XLA Ops:
  0.6 92.5 %copy-start.9 = (s32[1,3,16]{2,0,1:T(1,128)S(1)}, s32[1,3,16]{2,0,1:T(1,128)}, u32[]{:S(2)}) copy-start(s32[1,3,16]{2,0,1:T(1,128)} %param.21) | copy-start | bytes 580
  225.3 61.9 %copy-start.5 = (f32[8,1152]{1,0:T(8,128)S(1)}, f32[8,1152]{1,0:T(8,128)}, u32[]{:S(2)}) copy-start(f32[8,1152]{1,0:T(8,128)} %get-tuple-element.99) | copy-start | bytes 110596
  287.4 57.5 %copy-start.6 = (f32[4,1,1152]{2,1,0:T(1,128)S(1)}, f32[4,1,1152]{2,1,0:T(1,128)}, u32[]{:S(2)}) copy-start(f32[4,1,1152]{2,1,0:T(1,128)} %get-tuple-element.102) | copy-start | bytes 55300
  287.4 57.5 %copy-start.8 = (f32[1,1152]{1,0:T(1,128)S(1)}, f32[1,1152]{1,0:T(1,128)}, u32[]{:S(2)}) copy-start(f32[1,1152]{1,0:T(1,128)} %get-tuple-element.101) | copy-start | bytes 13828
  287.4 57.7 %copy-start.7 = (f32[1,1152]{1,0:T(1,128)S(1)}, f32[1,1152]{1,0:T(1,128)}, u32[]{:S(2)}) copy-start(f32[1,1152]{1,0:T(1,128)} %get-tuple-element.103) | copy-start | bytes 13828
  449.1 10.3 %copy-start = (f32[768,1152]{1,0:T(8,128)S(1)}, f32[768,1152]{1,0:T(8,128)}, u32[]{:S(2)}) copy-start(f32[768,1152]{1,0:T(8,128)} %get-tuple-element.106) | copy-start | bytes 10616836
  459.4 2.0 copy-start.1
  461.4 1.4 copy-start.3
  461.4 2.2 copy-start.4
  461.4 2.8 copy-start.2

commit v6 on v5

--- a/solution.py
+++ b/solution.py
@@ -288,49 +288,64 @@
 SCATTER_COPIES = 24
 
 
+class Corner:
+    def __init__(self, place, parts, across, copies):
+        x, y, zs = place.x, place.y, place.zs
+        a, b = pl.ds(0, UPPER), pl.ds(UPPER, SHARD - UPPER)
+        over_x, over_y = place.device(x=1 - x), place.device(y=1 - y)
+        self.over_y, self.over_x = [], []
+        for k in range(4):
+            block = parts.at[1 - y, zs[k], 1 - x]
+            self.over_y.append(copies.make(block.at[a], across.at[k, a], over_y))
+            self.over_x.append(copies.make(block.at[b], across.at[k, b], over_x))
+
+    def start(self, k):
+        self.over_y[k].start()
+        self.over_x[k].start()
+
+
 class Scatter:
-    def __init__(self, place, parts, bufs, column, send_sems, recv_sems):
+    def __init__(self, place, parts, bufs, column, send_sems, recv_sems, early=None):
         x, y, zs = place.x, place.y, place.zs
         self.place, self.parts, self.column = place, parts, column
-        self.by_x, self.by_y, self.from_x, self.from_y = [bufs.at[k] for k in range(4)]
+        self.across, self.from_x, self.from_y = [bufs.at[k] for k in range(3)]
+        self.early = early
         self.copies = Copies(send_sems, recv_sems)
         make = self.copies.make
         self.upper, self.lower = (0, UPPER), (UPPER, SHARD - UPPER)
         a, b = pl.ds(*self.upper), pl.ds(*self.lower)
         over_x, over_y = place.device(x=1 - x), place.device(y=1 - y)
         four = range(4)
-        self.across_y = [
-            make(parts.at[1 - y, zs[k], 1 - x, a], self.by_y.at[k, a], over_y) for k in four
-        ]
-        self.across_x = [
-            make(parts.at[1 - y, zs[k], 1 - x, b], self.by_x.at[k, b], over_x) for k in four
-        ]
+        if early is None:
+            self.corner = Corner(place, parts, self.across, self.copies)
         self.x_lower = [make(parts.at[y, zs[k], 1 - x, b], self.from_x.at[k, b], over_x) for k in four]
         self.y_upper = [make(parts.at[1 - y, zs[k], x, a], self.from_y.at[k, a], over_y) for k in four]
-        self.x_upper = [make(self.by_y.at[k, a], self.from_x.at[k, a], over_x) for k in four]
-        self.y_lower = [make(self.by_x.at[k, b], self.from_y.at[k, b], over_y) for k in four]
+        self.x_upper = [make(self.across.at[k, a], self.from_x.at[k, a], over_x) for k in four]
+        self.y_lower = [make(self.across.at[k, b], self.from_y.at[k, b], over_y) for k in four]
 
     def start(self, k):
-        self.across_y[k].start()
-        self.across_x[k].start()
+        self.corner.start(k)
 
     def follow(self, k):
         self.x_lower[k].start()
         self.y_upper[k].start()
 
-    def add(self, target, k, index, rows):
+    def add(self, k, index, rows):
+        given = self.across if self.early is None else self.early
         for at in range(0, rows[1], 16):
             here = pl.ds(rows[0] + at, 16)
-            total = self.parts[(*index, here)].astype(F32) + target[k, here].astype(F32)
-            target[k, here] = total.astype(BF16)
+            total = self.parts[(*index, here)].astype(F32) + given[k, here].astype(F32)
+            self.across[k, here] = total.astype(BF16)
 
     def pass_across(self, k):
         x, y, z = self.place.x, self.place.y, self.place.zs[k]
-        self.across_y[k].wait_recv()
-        self.add(self.by_y, k, (y, z, 1 - x), self.upper)
+        if self.early is None:
+            self.corner.over_y[k].wait_recv()
+        self.add(k, (y, z, 1 - x), self.upper)
         self.x_upper[k].start()
-        self.across_x[k].wait_recv()
-        self.add(self.by_x, k, (1 - y, z, x), self.lower)
+        if self.early is None:
+            self.corner.over_x[k].wait_recv()
+        self.add(k, (1 - y, z, x), self.lower)
         self.y_lower[k].start()
 
     def collect(self, k):
@@ -598,15 +613,18 @@
 def feed_kernel(
     up_ref, arrived_ref, picked_ref, up_bias_ref, down_bias_ref, cot_ref, after_ref,
     mods_ref, column_ref, slot_column_ref, slot_row_ref, down_ref,
-    pull_ref, grad_rows_ref, block_out_ref, gate_ref, bias_ref, parts_ref, down_out,
-    active_ref, total_ref, branch_ref, buffers_ref, halves_ref, tiles_ref,
-    send_sems, recv_sems, local_sems, pair_send, pair_recv, tile_sems,
+    pull_ref, grad_rows_ref, block_out_ref, gate_ref, bias_ref, parts_ref, down_out, across_out,
+    active_ref, total_ref, branch_ref, buffers_ref, halves_ref, tiles_ref, across_ref,
+    send_sems, recv_sems, local_sems, pair_send, pair_recv, tile_sems, corner_send, corner_recv,
 ):
     step = pl.program_id(0)
     place = Place()
     downs = Spread(
         place, down_ref, lambda y, c, z, x: down_out.at[z, x, y, c], send_sems, recv_sems, local_sems
     )
+
+    corners = Copies(corner_send, corner_recv)
+    corner = Corner(place, parts_ref, across_ref, corners)
 
     def rows_of(x, y, c):
         return pl.ds(pl.multiple_of((4 * x + 2 * y + c) * SHARD, 16), SHARD)
@@ -711,6 +729,8 @@
         free(2)
         free(3)
         for k in range(4):
+            corner.start(k)
+        for k in range(4):
             downs.pass_pair(k)
         downs.finish()
         for m in (0, 1):
@@ -744,6 +764,11 @@
             block_out_ref[here, :] = (after_ref[here, :] + gate * branch).astype(BF16)
             gates = gates + crop_sums(segment, cot_ref[here, :].astype(F32) * branch)
         gate_ref[...] = gates
+        for copy in corners.made:
+            copy.wait()
+        leave = pltpu.make_async_copy(across_ref, across_out, local_sems.at[0])
+        leave.start()
+        leave.wait()
 
 
 def whole(*shape):
@@ -763,6 +788,7 @@
             shape_of(1, D, dtype=F32),
             shape_of(2, 4, 2, SHARD, D),
             shape_of(4, 2, 2, 2, SHARD, D),
+            shape_of(4, SHARD, D),
         ],
         in_specs=[
             early(D, D), whole(PLACES, D), whole(PLACES, 128), early(1, D), whole(1, D),
@@ -771,7 +797,7 @@
         ],
         out_specs=[
             early(PLACES, D), whole(PLACES, D), whole(TOK_DEV, D), whole(8, D), whole(1, D),
-            whole(2, 4, 2, SHARD, D), ANYWHERE,
+            whole(2, 4, 2, SHARD, D), ANYWHERE, ANYWHERE,
         ],
         scratch_shapes=[
             pltpu.VMEM((4, PLACES, D), BF16),
@@ -780,12 +806,15 @@
             pltpu.VMEM((2, D, D), BF16),
             pltpu.VMEM((2, 4, 2, SHARD, D), BF16),
             pltpu.VMEM((2, 2, 2, 2, SHARD, D), BF16),
+            pltpu.VMEM((4, SHARD, D), BF16),
             DMA((SPREAD_COPIES,)),
             DMA((SPREAD_COPIES,)),
             DMA((4,)),
             DMA((4, 2, 2)),
             DMA((4, 2, 2)),
             DMA((2, 2, 2)),
+            DMA((8,)),
+            DMA((8,)),
         ],
         compiler_params=talking(3),
     )(up, arrived, picked, up_bias, down_bias, cot, after, mods, column, slot_column, slot_row, down)
@@ -793,21 +822,22 @@
 
 def unfeed_kernel(
     down_ref, up_ref, pull_ref, grad_rows_ref, arrived_ref, after_ref, cot_ref, attn_ref, mods_ref,
-    column_ref, slot_column_ref, given_ref,
+    column_ref, slot_column_ref, given_ref, early_ref,
     up_bias_ref, mid_ref, grad_attn_ref, sums_ref, out_bias_ref, parts_out, plane_ref,
     hidden_ref, total_ref, back_ref, buffers_ref, parts_ref, bufs_ref,
     send_sems, recv_sems, pair_send, pair_recv, out_sem,
 ):
     step = pl.program_id(0)
     place = Place()
-    scatter = Scatter(place, given_ref, bufs_ref, plane_ref, send_sems, recv_sems)
+    scatter = Scatter(place, given_ref, bufs_ref, plane_ref, send_sems, recv_sems, early_ref)
     pair = Pair(place, buffers_ref, parts_ref, pair_send, pair_recv)
 
     @pl.when(step == 0)
     def _():
         place.meet()
         for k in ORDER:
-            scatter.start(k)
+            scatter.follow(k)
+            scatter.pass_across(k)
         total_ref[...] = jnp.zeros_like(total_ref)
 
     bias = jnp.zeros((1, D), F32)
@@ -836,18 +866,6 @@
     @pl.when(step >= 1)
     def _():
         pair.take(step - 1)
-
-    @pl.when(step == 0)
-    def _():
-        for k in ORDER:
-            scatter.follow(k)
-
-    for here_step, ks in ((1, (1, 2)), (2, (3, 0))):
-
-        @pl.when(step == here_step)
-        def _():
-            for k in ks:
-                scatter.pass_across(k)
 
     @pl.when(step == 3)
     def _():
@@ -883,7 +901,7 @@
         leave.wait()
 
 
-def unfeed(down, up, pull, grad_rows, arrived, after, cot, attn, mods, column, slot_column, given):
+def unfeed(down, up, pull, grad_rows, arrived, after, cot, attn, mods, column, slot_column, given, early):
     block = lambda *tail: pl.BlockSpec((1, *tail), lambda i: (i, 0, 0))
     return pl.pallas_call(
         unfeed_kernel,
@@ -900,7 +918,7 @@
         in_specs=[
             block(D, D), block(D, D), block(PLACES, D), whole(PLACES, D), whole(PLACES, D),
             whole(TOK_DEV, D), whole(TOK_DEV, D), whole(TOK_DEV, D), whole(6, 8, D), whole(TOK_DEV, 1),
-            whole(TOK_DEV, 1), whole(2, 4, 2, SHARD, D),
+            whole(TOK_DEV, 1), whole(2, 4, 2, SHARD, D), whole(4, SHARD, D),
         ],
         out_specs=[
             block(1, D), whole(TOK_DEV, D), whole(TOK_DEV, D), whole(3, 8, D), whole(1, D), ANYWHERE, whole(4, SHARD, D),
@@ -911,7 +929,7 @@
             pltpu.VMEM((PLACES, D), BF16),
             pltpu.VMEM((2, D, D), BF16),
             pltpu.VMEM((2, D, D), BF16),
-            pltpu.VMEM((4, 4, SHARD, D), BF16),
+            pltpu.VMEM((3, 4, SHARD, D), BF16),
             DMA((SCATTER_COPIES,)),
             DMA((SCATTER_COPIES,)),
             DMA((2,)),
@@ -919,7 +937,7 @@
             DMA((1,)),
         ],
         compiler_params=talking(4),
-    )(down, up, pull, grad_rows, arrived, after, cot, attn, mods, column, slot_column, given)
+    )(down, up, pull, grad_rows, arrived, after, cot, attn, mods, column, slot_column, given, early)
 
 
 def unattend_kernel(
@@ -1036,7 +1054,7 @@
             pltpu.VMEM((3 * HEADS, TOK_DEV, 128), BF16),
             pltpu.VMEM((TOK_DEV, 128), F32),
             pltpu.VMEM((TOK_DEV, 128), F32),
-            pltpu.VMEM((4, 4, SHARD, D), BF16),
+            pltpu.VMEM((3, 4, SHARD, D), BF16),
             pltpu.VMEM((3, SHARD, D), BF16),
             DMA((SCATTER_COPIES,)),
             DMA((SCATTER_COPIES,)),
@@ -1222,7 +1240,7 @@
             vmem((TOK_DEV, D), F32),
             vmem((2, D, D), BF16),
             vmem((2, D, D), BF16),
-            vmem((4, 4, SHARD, D), BF16),
+            vmem((3, 4, SHARD, D), BF16),
             vmem((4, SHARD, D), BF16),
             vmem((3, SHARD, D), BF16),
             vmem((3, SHARD, D), BF16),
@@ -1254,7 +1272,8 @@
     mixed_out, up_out, down_out, mods_ref, conds_ref, qkv_bias_ref, up_bias_ref, out_bias_ref,
     down_bias_ref, column_ref, row_ref, slot_column_ref, token_groups_ref,
     send_sems, recv_sems, local_sem, up_send, up_recv, up_local, small_send, small_recv, local_small,
-    mixed_ref, stage_ref, own_small, all_small, own_cond, partial_ref, from_x, from_z, rows_ref, tables_ref,
+    mixed_ref, stage_ref, own_small, all_small, crop_rows, own_crops, all_crops, ada_parts, ada_all,
+    product_ref, columns_ref, total_ref, rows_ref, tables_ref,
     query_ref, value_ref,
 ):
     place = Place()
@@ -1275,24 +1294,21 @@
     small = Copies(small_send, small_recv)
     to_mates = [small.make(own_small, all_small.at[place.index], mate) for mate in place.mates]
     others = [(k, far) for k in range(4) for far in (0, 1) if k or far]
-    to_peers = []
-    for k, far in others:
-        there = 1 - x if far else x
-        to_peers.append(
-            small.make(
-                own_cond.at[2 * zs[k] + there],
-                conds_ref.at[place.peer],
-                place.device(z=zs[k], x=there),
+
+    def to_peers(source, target):
+        copies = []
+        for k, far in others:
+            there = 1 - x if far else x
+            copies.append(
+                small.make(
+                    source(2 * zs[k] + there), target.at[place.peer], place.device(z=zs[k], x=there)
+                )
             )
-        )
-    over_x = [
-        small.make(partial_ref.at[2 * zs[k] + 1 - x], from_x.at[k], place.device(x=1 - x))
-        for k in range(4)
-    ]
-    along = [
-        small.make(partial_ref.at[2 * zs[k] + x], from_z.at[k - 1], place.device(z=zs[k]))
-        for k in (1, 2, 3)
-    ]
+        return copies
+
+    crops = to_peers(lambda peer: own_crops, all_crops)
+    ada = to_peers(lambda peer: ada_parts.at[peer], ada_all)
+    products = to_peers(lambda peer: product_ref.at[peer], columns_ref)
     finals = [
         small.make(rows_ref.at[other], tables_ref.at[place.index], mate)
         for other, mate in zip(place.mate_index, place.mates)
@@ -1319,30 +1335,23 @@
         copy.start()
     own_stage.start()
     all_small[place.index] = own_small[...]
-    own_cond[...] = jnp.zeros_like(own_cond)
+    thin = ada_ref.shape[1] // 8
+    ada_parts[...] = jnp.zeros_like(ada_parts)
+    for i in range(8):
+        ada_parts[i, :, :thin] = ada_ref[:, thin * i : thin * (i + 1)]
+    for copy in ada:
+        copy.start()
+    ada_all[place.peer] = ada_parts[place.peer]
+    crop_rows[...] = jnp.zeros_like(crop_rows)
     for copy in to_mates:
         copy.wait_recv()
-    for i in range(8):
-        for j in range(4):
-            part = all_small[j, :CROPS, SHARD * i : SHARD * (i + 1)]
-            own_cond[i, CROPS * j : CROPS * (j + 1), :SHARD] = part
-    for copy in to_peers:
+    for j in range(4):
+        crop_rows[CROPS * j : CROPS * (j + 1), :] = all_small[j, :CROPS, :]
+    own_crops[...] = crop_rows[...].astype(BF16)
+    for copy in crops:
         copy.start()
-    conds_ref[place.peer] = own_cond[place.peer]
-    for copy in to_peers:
-        copy.wait_recv()
-    every_cond = conds_ref[...].reshape(128, 256)[:, :SHARD].astype(BF16)
-    partial_ref[...] = dot(every_cond, ada_ref[...]).reshape(partial_ref.shape)
-    for k in ORDER:
-        over_x[k].start()
+    all_crops[place.peer] = own_crops[...]
     first.pass_across(0)
-    for k in (1, 2, 3):
-        first.pass_along(k)
-    for k in ORDER:
-        over_x[k].wait_recv()
-        partial_ref[2 * zs[k] + x] += from_x[k]
-        if k:
-            along[k - 1].start()
     first_end = lengths_ref[0, 0]
     second_end = first_end + lengths_ref[0, 1]
     tokens = lax.broadcasted_iota(jnp.int32, (TOK_DEV, 1), 0)
@@ -1353,20 +1362,41 @@
     slot_column_ref[...] = jnp.transpose(spread)[:, :1].astype(jnp.int32)
     token_groups_ref[...] = jnp.zeros_like(token_groups_ref)
     token_groups_ref[:, :GROUPS] = per_crop(groups_ref[...].astype(F32), column_ref[...]).astype(BF16)
+    for k in (1, 2, 3):
+        first.pass_along(k)
     first.pass_across(1)
-    for copy in along:
+    for copy in crops + ada:
         copy.wait_recv()
-    total = partial_ref[place.peer] + from_z[0] + from_z[1] + from_z[2] + vectors_ref[:, 2 * D :]
+    every_crop = all_crops[...].reshape(128, D)
+    product = dot(every_crop, ada_all[...].reshape(D, ada_all.shape[2]))
+    product_ref[...] = product.reshape(product_ref.shape)
+    for copy in products:
+        copy.start()
+    ups.start()
+    columns_ref[place.peer] = product_ref[place.peer]
+    conds_ref[...] = jnp.zeros_like(conds_ref)
+    mine = jnp.zeros((128, SHARD), F32)
+    for i in range(8):
+        part = every_crop[:, SHARD * i : SHARD * (i + 1)].astype(F32)
+        mine = mine + jnp.where(place.peer == i, part, 0.0)
+    conds_ref[:, :, :SHARD] = mine.reshape(8, 16, SHARD)
+    first.pass_across(2)
+    for copy in products:
+        copy.wait_recv()
+    for i in range(8):
+        total_ref[:, thin * i : thin * (i + 1)] = columns_ref[i, :, :thin]
+    total = total_ref[...] + vectors_ref[:, 2 * D :]
     rows_ref[...] = jnp.zeros_like(rows_ref)
     for j in range(4):
         rows_ref[j, :CROPS, :] = total[CROPS * j : CROPS * (j + 1)]
     for copy in finals:
         copy.start()
     tables_ref[place.index] = rows_ref[place.index]
-    ups.start()
     for copy in swaps:
         copy.start()
-    first.pass_across(2)
+    first.pass_across(3)
+    first.pass_pair(0)
+    first.pass_pair(1)
     for copy in finals:
         copy.wait_recv()
     for j in (0, 2):
@@ -1374,8 +1404,6 @@
         mods_ref[3 * j // 2 + 1, :, : D // 2] = tables_ref[j, :, D:]
         mods_ref[3 * j // 2 + 1, :, D // 2 :] = tables_ref[j + 1, :, : D // 2]
         mods_ref[3 * j // 2 + 2] = tables_ref[j + 1, :, D // 2 :]
-    first.pass_pair(0)
-    first.pass_across(3)
     for copy in swaps:
         copy.wait_recv()
     own_stage.wait()
@@ -1393,7 +1421,7 @@
     qkv_bias_ref[1, :, :OUT_SHARD] = query_ref[:, QKV_SHARD:]
     qkv_bias_ref[2, :, 2 * OUT_SHARD : QKV_SHARD] = value_ref[:, :OUT_SHARD]
     qkv_bias_ref[3, :, :QKV_SHARD] = value_ref[:, OUT_SHARD:]
-    for k in (1, 2, 3):
+    for k in (2, 3):
         first.pass_pair(k)
     first.finish()
     ups.finish()
@@ -1424,16 +1452,20 @@
         in_specs=[IN_VMEM] * 2 + [ANYWHERE] * 2 + [IN_VMEM] * 5 + [IN_SMEM],
         out_specs=[ANYWHERE] * 2 + [IN_VMEM] * 11,
         scratch_shapes=[DMA((GATHER_COPIES,))] * 2
-        + [DMA((1,)), DMA((3,)), DMA((3,)), DMA((1,)), DMA((23,)), DMA((23,)), DMA((1,))]
+        + [DMA((1,)), DMA((3,)), DMA((3,)), DMA((1,)), DMA((30,)), DMA((30,)), DMA((1,))]
         + [
             vmem((SHARD, D), BF16),
             vmem((4, SHARD, OUT_SHARD), BF16),
             vmem((8, D), F32),
             vmem((4, 8, D), F32),
+            vmem((16, D), F32),
+            vmem((16, D), BF16),
+            vmem((8, 16, D), BF16),
+            vmem((8, SHARD, 256), BF16),
+            vmem((8, SHARD, 256), BF16),
             vmem((8, 16, 256), F32),
-            vmem((8, 16, wide), F32),
-            vmem((4, 16, wide), F32),
-            vmem((3, 16, wide), F32),
+            vmem((8, 16, 256), F32),
+            vmem((16, wide), F32),
             vmem((4, 8, wide), F32),
             vmem((4, 8, wide), F32),
             vmem((1, D), F32),
@@ -1482,13 +1514,13 @@
         down_rows,
     )
     up = up.reshape(4, D, D)
-    pull, grad_rows, block_out, gate_two, grad_down_bias, parts_down, down = feed(
+    pull, grad_rows, block_out, gate_two, grad_down_bias, parts_down, down, early_down = feed(
         up, arrived, picked, bias_up, bias_down, cot, after, mods, column,
         slot_column, slot_row, down_column,
     )
     down = down.reshape(4, D, D)
     grad_up_bias, mid, grad_attn, sums, grad_out_bias, parts_up, plane_down = unfeed(
-        down, up, pull, grad_rows, arrived, after, cot, attn, mods, column, slot_column, parts_down
+        down, up, pull, grad_rows, arrived, after, cot, attn, mods, column, slot_column, parts_down, early_down
     )
     triple, triple_sums, share_down, plane_up, grad_split = unattend(
         grad_attn, full_out, heads, lse, column, row, parts_up.reshape(2, 4, 2, SHARD, D), plane_down,

time: 474 us -> 463 us (0.977)
  Pallas kernels: 438 us -> 429 us
    pallas_call x1, Pallas kernels: 59.6 us -> 49.5 us  [unfeed(): pl.pallas_call(unfeed_kernel, grid=(4,), out_shape=[shape_of(4, 1, D, dty...]
    unnamed x35 -> x37, local copies, waits for them, and re-layouts: 17.1 us -> 16.7 us
where the time goes in v6:
time: 463 us; the launch traced here: 454 us
  Pallas kernels  429 us (93%)
  local copies, waits for them, and re-layouts  21.9 us (5%)
    pallas_call x1, Pallas kernels, unproject(): pl.pallas_call(unproject_kernel, grid=(8,), out_shape=[shape_of(TOK_DEV,...  103 us
    pallas_call x1, Pallas kernels, gather_all(): pl.pallas_call(gather_kernel, out_shape=[shape_of(2, 2, 4, 2, SHARD, D),...  86.7 us
    pallas_call x1, Pallas kernels, feed(): pl.pallas_call(feed_kernel, grid=(8,), out_shape=[shape_of(4, PLACES, D),...  72.6 us
    pallas_call x1, Pallas kernels, attend(): pl.pallas_call(attend_kernel, out_shape=[shape_of(TOK_DEV, D), shape_of(3...  60.7 us
    pallas_call x1, Pallas kernels, unattend(): pl.pallas_call(unattend_kernel, out_shape=[shape_of(4, TOK_DEV, PAD_SHARD...  57 us
    pallas_call x1, Pallas kernels, unfeed(): pl.pallas_call(unfeed_kernel, grid=(4,), out_shape=[shape_of(4, 1, D, dty...  49.5 us
    unnamed x37, local copies, waits for them, and re-layouts  16.7 us

profile of v6, /device:TPU:9, one launch (start us, length us, event | category | flops | bytes accessed | tf_op | source)
XLA Modules:
  0.0 454.5 jit_solution(1026239289072680653)
XLA Ops:
  0.7 1.9 copy.33.down_ref
  2.6 1.5 convert_add_fusion
  4.1 1.3 copy.46
  5.3 86.7 %shard_map.273 = (bf16[2,2,4,2,144,1152]{5,4,3,2,1,0:T(8,128)(2,1)}, bf16[4,144,1152]{2,1,0:T(8,128)(2,1)}, bf16[144,1152]{1,0:T(8,128)(2,1)}, f32[6,8,1152]{2,1...) custom-call(bf16[144,864]{1,0:T(8,128)(2,1)} %qkv_ref.1, ...), custom_call_target="tpu_custom_call" | custom-call | tf_op jit(solution)/shard_map/pallas_call | solution.py:1435
  92.1 0.6 copy.45
  92.6 60.7 %shard_map.274 = (bf16[768,1152]{1,0:T(8,128)(2,1)}, bf16[48,768,128]{2,1,0:T(8,128)(2,1)}, bf16[768,1152]{1,0:T(8,128)(2,1)}, f32[16,1,768]{2,1,0:T(1,128)}, bf...) custom-call(bf16[768,1152]{1,0:T(8,128)(2,1)} %bitcast.36, ...), custom_call_target="tpu_custom_call" | custom-call | tf_op jit(solution)/shard_map/pallas_call | solution.py:571
  153.3 72.6 %shard_map.275 = (bf16[4,512,1152]{2,1,0:T(8,128)(2,1)}, bf16[512,1152]{1,0:T(8,128)(2,1)}, bf16[768,1152]{1,0:T(8,128)(2,1)}, f32[8,1152]{1,0:T(8,128)}, f32[1,...) custom-call(bf16[4,1152,1152]{2,1,0:T(8,128)(2,1)} %bitcast.29, ...), custom_call_target="tpu_custom_call" | custom-call | tf_op jit(solution)/shard_map/pallas_call | solution.py:780
  225.9 49.5 %shard_map.276 = (f32[4,1,1152]{2,1,0:T(1,128)}, f32[768,1152]{1,0:T(8,128)}, bf16[768,1152]{1,0:T(8,128)(2,1)}, f32[3,8,1152]{2,1,0:T(8,128)}, f32[1,1152]{1,0:...) custom-call(bf16[4,1152,1152]{2,1,0:T(8,128)(2,1)} %bitcast.33, bf16[4,1152,1152]{2,1,0:T(8,128)(2,1)} %bitcast.30, ...), custom_call_target="tpu_custom_call" | custom-call | tf_op jit(solution)/shard_map/pallas_call | solution.py:906
  275.5 0.8 bitcast_dynamic-update-slice_fusion.2
  276.2 0.8 bitcast_dynamic-update-slice_fusion.1
  277.0 0.8 bitcast_dynamic-update-slice_fusion
  277.8 0.1 reshape.69
  278.0 57.0 %shard_map.277 = (bf16[4,768,896]{2,1,0:T(8,128)(2,1)}, f32[4,1,896]{2,1,0:T(1,128)}, f32[144,1152]{1,0:T(8,128)}, bf16[4,144,1152]{2,1,0:T(8,128)(2,1)}, bf16[4,768,288]{2,1,0:T(8,128)(2,1)}) custom-call(bf16[768,1152]{1,0:T(8,128)(2,1)} %get-tuple-element.88.grad_ref, bf16[1152,1152]{1,0:T(8,128)(2,1)} %get-tuple-element.89.weight_in, ...), custom_call_target="tpu_custom_call" | custom-call | tf_op jit(solution)/shard_map/pallas_call | solution.py:1035
  335.0 0.8 slice_reduce_fusion
  336.1 0.1 concatenate.10
  336.2 0.1 reshape.73
  336.4 0.7 pad_maximum_fusion.rest_ref
  337.1 102.6 %shard_map.278 = (f32[768,1152]{1,0:T(8,128)}, f32[144,1152]{1,0:T(8,128)}, f32[144,864]{1,0:T(8,128)}, f32[144,288]{1,0:T(8,128)}, f32[144,1728]{1,0:T(8,128)},...) custom-call(bf16[4,1152,1152]{2,1,0:T(8,128)(2,1)} %bitcast.32, bf16[4,768,896]{2,1,0:T(8,128)(2,1)} %get-tuple-element.94.triple_ref, ...), custom_call_target="tpu_custom_call" | custom-call | tf_op jit(solution)/shard_map/pallas_call | solution.py:1215
  439.7 2.3 copy.35
  442.1 0.8 slice.55
  443.0 0.7 fusion.1
  443.7 0.7 slice.67
  444.3 1.4 slice_reduce_fusion.1
  445.8 1.2 copy.57
  447.0 1.4 copy-done
  448.4 1.8 copy.58
  450.2 0.2 copy-done.2
  450.4 1.0 copy.59
  451.3 0.4 copy-done.4
  451.7 0.8 copy.60
  452.5 0.7 copy.61
  453.2 0.8 copy.62
  (32 shorter events, 0.5 us)
Async XLA Ops:
  0.6 91.4 %copy-start.10 = (s32[1,3,16]{2,0,1:T(1,128)S(1)}, s32[1,3,16]{2,0,1:T(1,128)}, u32[]{:S(2)}) copy-start(s32[1,3,16]{2,0,1:T(1,128)} %param.21) | copy-start | bytes 580
  225.9 51.8 %copy-start.6 = (f32[8,1152]{1,0:T(8,128)S(1)}, f32[8,1152]{1,0:T(8,128)}, u32[]{:S(2)}) copy-start(f32[8,1152]{1,0:T(8,128)} %get-tuple-element.101) | copy-start | bytes 110596
  278.0 57.9 %copy-start.7 = (f32[4,1,1152]{2,1,0:T(1,128)S(1)}, f32[4,1,1152]{2,1,0:T(1,128)}, u32[]{:S(2)}) copy-start(f32[4,1,1152]{2,1,0:T(1,128)} %get-tuple-element.104) | copy-start | bytes 55300
  278.0 57.9 %copy-start.9 = (f32[1,1152]{1,0:T(1,128)S(1)}, f32[1,1152]{1,0:T(1,128)}, u32[]{:S(2)}) copy-start(f32[1,1152]{1,0:T(1,128)} %get-tuple-element.103) | copy-start | bytes 13828
  278.0 58.0 %copy-start.8 = (f32[1,1152]{1,0:T(1,128)S(1)}, f32[1,1152]{1,0:T(1,128)}, u32[]{:S(2)}) copy-start(f32[1,1152]{1,0:T(1,128)} %get-tuple-element.105) | copy-start | bytes 13828
  337.1 108.7 %copy-start.1 = (bf16[768,1152]{1,0:T(8,128)(2,1)S(1)}, bf16[768,1152]{1,0:T(8,128)(2,1)}, u32[]{:S(2)}) copy-start(bf16[768,1152]{1,0:T(8,128)(2,1)} %get-tuple-element.81) | copy-start | bytes 5308420
  445.8 2.6 copy-start
  448.4 2.0 copy-start.2
  450.4 1.4 copy-start.4
  450.4 2.2 copy-start.5
  450.4 2.8 copy-start.3

commit v7 on v6

--- a/solution.py
+++ b/solution.py
@@ -1076,6 +1076,10 @@
 ):
     step = pl.program_id(0)
     place = Place()
+
+    def block_at(step):
+        return lax.rem(step + 2 * (1 - place.y), 4)
+
     pair = Pair(place, buffers_ref, parts_ref, pair_send, pair_recv)
     blocks = parts_ref.reshape(2, 4, 2, SHARD, D)
     scatter = Scatter(place, blocks, bufs_ref, plane_ref, send_sems, recv_sems)
@@ -1111,45 +1115,53 @@
         def grad(i, carry):
             here = pl.ds(pl.multiple_of(i * 384, 384), 384)
             buffer = lax.rem(step, 2)
-            part = dot(first_ref[:, here], triple_ref[0], TN).astype(BF16)
+            part = dot(first_ref[:, here], triple_ref[block_at(step)], TN).astype(BF16)
             buffers_ref[buffer, here, :PAD_SHARD] = part
-            part = dot(mixed_ref[:, here], split_ref[0], TN).astype(BF16)
+            part = dot(mixed_ref[:, here], split_ref[block_at(step)], TN).astype(BF16)
             buffers_ref[buffer, here, QKV_SHARD:] = part
             return carry
 
         @pl.when(step >= 2)
         def _():
-            pair.free(step - 2)
+            pair.free(block_at(step - 2))
 
         lax.fori_loop(0, 3, grad, 0)
-        pair.send(step)
+        pair.send(block_at(step))
 
     @pl.when((step >= 1) & (step < 5))
     def _():
-        pair.take(step - 1)
+        pair.take(block_at(step - 1))
+
+    @pl.when(step == 2)
+    def _():
+        for k in (2, 3):
+            scatter.start(k)
+            scatter.y_upper[k].start()
 
     @pl.when(step == 4)
     def _():
-        pair.free(2)
-        pair.free(3)
-        scatter.start(2)
-        scatter.follow(2)
-        scatter.start(3)
-
-    for at, now, then in ((5, 2, 3), (6, 3, 1), (7, 1, 0)):
+        pair.free(block_at(2))
+        pair.free(block_at(3))
+        scatter.x_lower[2].start()
+        scatter.pass_across(2)
+        scatter.x_lower[3].start()
+
+    for at, now, then, last in ((4, None, None, 1), (5, 3, 1, 0), (6, 1, 0, None)):
 
         @pl.when(step == at)
         def _():
-            scatter.pass_across(now)
-            scatter.follow(then)
-            if at < 7:
-                scatter.start(1 if at == 5 else 0)
+            if now is not None:
+                scatter.pass_across(now)
+                scatter.x_lower[then].start()
+            if last is not None:
+                scatter.start(last)
+                scatter.y_upper[last].start()
 
     @pl.when(step >= 4)
     def _():
         for i in range(3):
             here = pl.ds(i * BLOCK, BLOCK)
-            part = dot(triple_ref[0, here, :], weight_ref[0, :, :PAD_SHARD], NT)
+            part = dot(triple_ref[step - 4, here, :], weight_ref[0, :, :PAD_SHARD], NT)
             total_ref[here, :] = jnp.where(step == 4, part, total_ref[here, :] + part)
 
     @pl.when(step == 7)
@@ -1225,7 +1237,7 @@
             shape_of(4, SHARD, OUT_SHARD, dtype=F32),
         ],
         in_specs=[
-            late(D, D), block(TOK_DEV, PAD_SHARD), early(TOK_DEV, OUT_SHARD), whole(TOK_DEV, D),
+            late(D, D), whole(4, TOK_DEV, PAD_SHARD), whole(4, TOK_DEV, OUT_SHARD), whole(TOK_DEV, D),
             whole(TOK_DEV, D), whole(TOK_DEV, D), whole(TOK_DEV, D), whole(6, 8, D), whole(TOK_DEV, 1),
             whole(4, SHARD, D), whole(4, 8, wide), whole(8, 16, 256), whole(SHARD, D),
         ],

time: 463 us -> 459 us (level)
  no operation moved by 1% of the time
where the time goes in v7:
time: 459 us; the launch traced here: 450 us
  Pallas kernels  425 us (93%)
  local copies, waits for them, and re-layouts  21.9 us (5%)
    pallas_call x1, Pallas kernels, unproject(): pl.pallas_call(unproject_kernel, grid=(8,), out_shape=[shape_of(TOK_DEV,...  98.6 us
    pallas_call x1, Pallas kernels, gather_all(): pl.pallas_call(gather_kernel, out_shape=[shape_of(2, 2, 4, 2, SHARD, D),...  86.7 us
    pallas_call x1, Pallas kernels, feed(): pl.pallas_call(feed_kernel, grid=(8,), out_shape=[shape_of(4, PLACES, D),...  72.6 us
    pallas_call x1, Pallas kernels, attend(): pl.pallas_call(attend_kernel, out_shape=[shape_of(TOK_DEV, D), shape_of(3...  60.7 us
    pallas_call x1, Pallas kernels, unattend(): pl.pallas_call(unattend_kernel, out_shape=[shape_of(4, TOK_DEV, PAD_SHARD...  57 us
    pallas_call x1, Pallas kernels, unfeed(): pl.pallas_call(unfeed_kernel, grid=(4,), out_shape=[shape_of(4, 1, D, dty...  49.5 us
    unnamed x37, local copies, waits for them, and re-layouts  16.7 us

profile of v7, /device:TPU:9, one launch (start us, length us, event | category | flops | bytes accessed | tf_op | source)
XLA Modules:
  0.0 450.5 jit_solution(6752771482596507644)
XLA Ops:
  0.7 1.9 copy.33.down_ref
  2.6 1.5 convert_add_fusion
  4.1 1.3 copy.46
  5.3 86.7 %shard_map.273 = (bf16[2,2,4,2,144,1152]{5,4,3,2,1,0:T(8,128)(2,1)}, bf16[4,144,1152]{2,1,0:T(8,128)(2,1)}, bf16[144,1152]{1,0:T(8,128)(2,1)}, f32[6,8,1152]{2,1...) custom-call(bf16[144,864]{1,0:T(8,128)(2,1)} %qkv_ref.1, ...), custom_call_target="tpu_custom_call" | custom-call | tf_op jit(solution)/shard_map/pallas_call | solution.py:1447
  92.1 0.6 copy.45
  92.6 60.7 %shard_map.274 = (bf16[768,1152]{1,0:T(8,128)(2,1)}, bf16[48,768,128]{2,1,0:T(8,128)(2,1)}, bf16[768,1152]{1,0:T(8,128)(2,1)}, f32[16,1,768]{2,1,0:T(1,128)}, bf...) custom-call(bf16[768,1152]{1,0:T(8,128)(2,1)} %bitcast.36, ...), custom_call_target="tpu_custom_call" | custom-call | tf_op jit(solution)/shard_map/pallas_call | solution.py:571
  153.3 72.6 %shard_map.275 = (bf16[4,512,1152]{2,1,0:T(8,128)(2,1)}, bf16[512,1152]{1,0:T(8,128)(2,1)}, bf16[768,1152]{1,0:T(8,128)(2,1)}, f32[8,1152]{1,0:T(8,128)}, f32[1,...) custom-call(bf16[4,1152,1152]{2,1,0:T(8,128)(2,1)} %bitcast.29, ...), custom_call_target="tpu_custom_call" | custom-call | tf_op jit(solution)/shard_map/pallas_call | solution.py:780
  225.9 49.5 %shard_map.276 = (f32[4,1,1152]{2,1,0:T(1,128)}, f32[768,1152]{1,0:T(8,128)}, bf16[768,1152]{1,0:T(8,128)(2,1)}, f32[3,8,1152]{2,1,0:T(8,128)}, f32[1,1152]{1,0:...) custom-call(bf16[4,1152,1152]{2,1,0:T(8,128)(2,1)} %bitcast.33, bf16[4,1152,1152]{2,1,0:T(8,128)(2,1)} %bitcast.30, ...), custom_call_target="tpu_custom_call" | custom-call | tf_op jit(solution)/shard_map/pallas_call | solution.py:906
  275.5 0.8 bitcast_dynamic-update-slice_fusion.2
  276.2 0.8 bitcast_dynamic-update-slice_fusion.1
  277.0 0.8 bitcast_dynamic-update-slice_fusion
  277.8 0.1 reshape.69
  278.0 57.0 %shard_map.277 = (bf16[4,768,896]{2,1,0:T(8,128)(2,1)}, f32[4,1,896]{2,1,0:T(1,128)}, f32[144,1152]{1,0:T(8,128)}, bf16[4,144,1152]{2,1,0:T(8,128)(2,1)}, bf16[4,768,288]{2,1,0:T(8,128)(2,1)}) custom-call(bf16[768,1152]{1,0:T(8,128)(2,1)} %get-tuple-element.88.grad_ref, bf16[1152,1152]{1,0:T(8,128)(2,1)} %get-tuple-element.89.weight_in, ...), custom_call_target="tpu_custom_call" | custom-call | tf_op jit(solution)/shard_map/pallas_call | solution.py:1035
  335.0 0.8 slice_reduce_fusion
  336.1 0.1 concatenate.10
  336.2 0.1 reshape.73
  336.4 0.7 pad_maximum_fusion.rest_ref
  337.1 98.6 %shard_map.278 = (f32[768,1152]{1,0:T(8,128)}, f32[144,1152]{1,0:T(8,128)}, f32[144,864]{1,0:T(8,128)}, f32[144,288]{1,0:T(8,128)}, f32[144,1728]{1,0:T(8,128)},...) custom-call(bf16[4,1152,1152]{2,1,0:T(8,128)(2,1)} %bitcast.32, bf16[4,768,896]{2,1,0:T(8,128)(2,1)} %get-tuple-element.94.triple_ref, ...), custom_call_target="tpu_custom_call" | custom-call | tf_op jit(solution)/shard_map/pallas_call | solution.py:1227
  435.7 2.3 copy.35
  438.1 0.8 slice.55
  439.0 0.7 fusion.1
  439.6 0.7 slice.67
  440.3 1.4 slice_reduce_fusion.1
  441.7 1.2 copy.57
  442.9 1.4 copy-done
  444.4 1.8 copy.58
  446.2 0.2 copy-done.2
  446.3 1.0 copy.59
  447.3 0.4 copy-done.4
  447.7 0.8 copy.60
  448.5 0.7 copy.61
  449.2 0.8 copy.62
  (32 shorter events, 0.5 us)
Async XLA Ops:
  0.6 91.4 %copy-start.10 = (s32[1,3,16]{2,0,1:T(1,128)S(1)}, s32[1,3,16]{2,0,1:T(1,128)}, u32[]{:S(2)}) copy-start(s32[1,3,16]{2,0,1:T(1,128)} %param.21) | copy-start | bytes 580
  225.9 51.8 %copy-start.6 = (f32[8,1152]{1,0:T(8,128)S(1)}, f32[8,1152]{1,0:T(8,128)}, u32[]{:S(2)}) copy-start(f32[8,1152]{1,0:T(8,128)} %get-tuple-element.101) | copy-start | bytes 110596
  278.0 57.9 %copy-start.7 = (f32[4,1,1152]{2,1,0:T(1,128)S(1)}, f32[4,1,1152]{2,1,0:T(1,128)}, u32[]{:S(2)}) copy-start(f32[4,1,1152]{2,1,0:T(1,128)} %get-tuple-element.104) | copy-start | bytes 55300
  278.0 57.9 %copy-start.9 = (f32[1,1152]{1,0:T(1,128)S(1)}, f32[1,1152]{1,0:T(1,128)}, u32[]{:S(2)}) copy-start(f32[1,1152]{1,0:T(1,128)} %get-tuple-element.103) | copy-start | bytes 13828
  278.0 58.0 %copy-start.8 = (f32[1,1152]{1,0:T(1,128)S(1)}, f32[1,1152]{1,0:T(1,128)}, u32[]{:S(2)}) copy-start(f32[1,1152]{1,0:T(1,128)} %get-tuple-element.105) | copy-start | bytes 13828
  337.1 104.6 %copy-start.1 = (bf16[768,1152]{1,0:T(8,128)(2,1)S(1)}, bf16[768,1152]{1,0:T(8,128)(2,1)}, u32[]{:S(2)}) copy-start(bf16[768,1152]{1,0:T(8,128)(2,1)} %get-tuple-element.81) | copy-start | bytes 5308420
  441.7 2.6 copy-start
  444.4 2.0 copy-start.2
  446.3 1.4 copy-start.4
  446.3 2.2 copy-start.5
  446.3 2.8 copy-start.3
